TPU v7x, 512 devices: a whole 4x4x16 slice. The times are simulated.
512 devices in a mesh: dp: 512 (over z, x, y, core).
Axes of the slice: x: 4, y: 4, z: 16, core: 2. Of those that a mesh axis runs over, the one named last changes fastest.
Arguments:
- queries: bfloat16 [16384, 32, 128], P('dp'), may hold values from -10 to 10
- positives: int32 [16384], P('dp'), may hold values from 0 to 3
- pages: bfloat16 [512, 1024, 128], P('dp'), may hold values from -1.5 to 1.5
Outputs:
- loss: float32 [16384], P('dp')
- query_grad: float32 [16384, 32, 128], P('dp')
- page_grad: float32 [512, 1024, 128], P('dp')
All inputs are finite; a program needn't handle non-finite values.
Results may differ from a plain program's by a relative error of at most 0.0059.
Values may be sent and summed in bfloat16 or wider, within the bound.
No kernel may reach another device: no remote copies, remote signals or barrier semaphores. Data moves between devices by JAX's collectives and lax.ppermute only.
A program may use at most 64 MiB of HBM per device.

v0:
```python
import jax
import jax.numpy as jnp
from jax import lax
from jax.sharding import PartitionSpec as P

W = 4


tau_scale = 0.1


def passed_along(value, axis, steps):
    count = lax.axis_size(axis)
    pairs = [(source, (source + steps) % count) for source in range(count)]
    return lax.ppermute(value, axis, pairs)


def token_scores(query_rows, page):
    logits = (
        lax.dot_general(
            query_rows, page, (((1,), (1,)), ((), ())), preferred_element_type=jnp.float32
        )
        / tau_scale
    )
    largest = jnp.max(logits, axis=1, keepdims=True)
    powers = jnp.exp(logits - largest)
    total = jnp.sum(powers, axis=1, keepdims=True)
    return (powers, total, largest)


def device_terms(query_block, positive, window):
    count, tokens, width = query_block.shape
    query_rows = query_block.reshape(count * tokens, width)
    score_list = []
    kept = []
    for page in window:
        powers, total, largest = token_scores(query_rows, page)
        kept.append((powers, total))
        smooth_max = tau_scale * (largest[:, 0] + jnp.log(total[:, 0]))
        score_list.append(jnp.sum(smooth_max.reshape(count, tokens), axis=1))
    scores = jnp.stack(score_list, axis=1)
    is_positive = (jnp.arange(len(window), dtype=jnp.int32)[None, :] == positive[:, None]).astype(
        jnp.float32
    )
    positive_score = jnp.sum(is_positive * scores, axis=1, keepdims=True)
    margins = scores - positive_score
    others = 1.0 - is_positive
    loss = jnp.sum(others * jax.nn.softplus(margins), axis=1)
    sigmoid_terms = others * jax.nn.sigmoid(margins)
    slopes = sigmoid_terms - is_positive * jnp.sum(sigmoid_terms, axis=1, keepdims=True)
    query_grad = jnp.zeros((count * tokens, width), jnp.float32)
    page_terms = []
    for offset, page in enumerate(window):
        powers, total = kept[offset]
        row_slope = jnp.repeat(slopes[:, offset], tokens)[:, None]
        weight = (powers * (row_slope / total)).astype(jnp.bfloat16)
        query_grad = query_grad + jnp.dot(weight, page, preferred_element_type=jnp.float32)
        page_terms.append(
            lax.dot_general(
                weight, query_rows, (((0,), (0,)), ((), ())), preferred_element_type=jnp.float32
            )
        )
    return (loss, query_grad.reshape(count, tokens, width), page_terms)


def on_device(queries, positives, pages):
    own_page = pages[0]
    window = [own_page]
    for offset in range(1, W):
        window.append(passed_along(window[-1], "dp", 1))
    loss, query_grad, page_terms = device_terms(queries, positives, window)
    page_total = page_terms[0]
    for offset in range(1, W):
        page_total = page_total + passed_along(page_terms[offset], "dp", -offset)
    return (loss, query_grad, page_total[None])


def solution(mesh):
    in_specs = (P("dp", None, None), P("dp"), P("dp", None, None))
    out_specs = (P("dp"), P("dp", None, None), P("dp", None, None))
    return jax.shard_map(
        on_device, mesh=mesh, in_specs=in_specs, out_specs=out_specs, check_vma=False
    )
```

profile of v0, /device:TPU:1, one launch (start us, length us, event | category | flops | bytes accessed | tf_op | source)
XLA Modules:
  0.0 88.1 jit_solution(5925353314179672765)
XLA Ops:
  0.6 4.7 %collective-permute-start = (bf16[1024,128]{1,0:T(8,128)(2,1)}, bf16[1024,128]{1,0:T(8,128)(2,1)S(1)}, u32[]{:S(2)}, u32[]{:S(2)}) collective-permute-start(bf16[1024,128]{1,0:T(8,128)(2,1)} %bitcast.45), channel_id=1, source_target_pairs={{0,1},{1,2},{2,3},{3,4},{4,5},{5,6},{6,7},{7,8},{8,9},{9,10},{10,1... | collective-permute-start | bytes 786440 | tf_op jit(solution)/shard_map/ppermute | solution.py:15
  5.4 1.7 %multiply_reduce_fusion.3 = (f32[1024]{0:T(1024)S(1)}, f32[1024,1024]{0,1:T(8,128)S(1)}) fusion(bf16[1024,128]{1,0:T(8,128)(2,1)S(1)} %bitcast.37, bf16[1,1024,128]{2,1,0:T(8,128)(2,1)} %param.5), kind=kOutput, calls=%fused_computation.11 | convolution fusion | flops 270531584 | bytes 4722688 | tf_op jit(solution)/shard_map/dot_general | solution.py:20
  7.1 1.9 %copy-done.1 = f32[1024,1024]{0,1:T(8,128)} copy-done((f32[1024,1024]{0,1:T(8,128)}, f32[1024,1024]{0,1:T(8,128)S(1)}, u32[]{:S(2)}) %copy-start.1) | copy-done | bytes 4194328
  10.0 0.8 collective-permute-done
  10.8 2.5 %collective-permute-start.1 = (bf16[1024,128]{1,0:T(8,128)(2,1)S(1)}, bf16[1024,128]{1,0:T(8,128)(2,1)S(1)}, u32[]{:S(2)}, u32[]{:S(2)}) collective-permute-start(bf16[1024,128]{1,0:T(8,128)(2,1)S(1)} %collective-permute-done), channel_id=1, source_target_pairs={{0,1},{1,2},{2,3},{3,4},{4,5},{5,6},{6,7},{7,8},{8,9},{9,10},{10,1... | collective-permute-start | bytes 786440 | tf_op jit(solution)/shard_map/ppermute | solution.py:15
  14.0 2.0 %copy-done.3 = f32[1024,1024]{0,1:T(8,128)} copy-done((f32[1024,1024]{0,1:T(8,128)}, f32[1024,1024]{0,1:T(8,128)S(1)}, u32[]{:S(2)}) %copy-start.3) | copy-done | bytes 4194328
  16.9 8.1 %collective-permute-done.1 = bf16[1024,128]{1,0:T(8,128)(2,1)S(1)} collective-permute-done((bf16[1024,128]{1,0:T(8,128)(2,1)S(1)}, bf16[1024,128]{1,0:T(8,128)(2,1)S(1)}, u32[]{:S(2)}, u32[]{:S(2)}) %collective-permute-start.1) | collective-permute-done | bytes 262176 | tf_op jit(solution)/shard_map/ppermute | solution.py:15
  25.0 1.9 %collective-permute-start.2 = (bf16[1024,128]{1,0:T(8,128)(2,1)S(1)}, bf16[1024,128]{1,0:T(8,128)(2,1)S(1)}, u32[]{:S(2)}, u32[]{:S(2)}) collective-permute-start(bf16[1024,128]{1,0:T(8,128)(2,1)S(1)} %collective-permute-done.1), channel_id=1, source_target_pairs={{0,1},{1,2},{2,3},{3,4},{4,5},{5,6},{6,7},{7,8},{8,9},{9,10},{10,1... | collective-permute-start | bytes 786440 | tf_op jit(solution)/shard_map/ppermute | solution.py:15
  27.6 1.9 %copy-done.5 = f32[1024,1024]{0,1:T(8,128)} copy-done((f32[1024,1024]{0,1:T(8,128)}, f32[1024,1024]{0,1:T(8,128)S(1)}, u32[]{:S(2)}) %copy-start.5) | copy-done | bytes 4194328
  30.5 7.6 %collective-permute-done.2 = bf16[1024,128]{1,0:T(8,128)(2,1)S(1)} collective-permute-done((bf16[1024,128]{1,0:T(8,128)(2,1)S(1)}, bf16[1024,128]{1,0:T(8,128)(2,1)S(1)}, u32[]{:S(2)}, u32[]{:S(2)}) %collective-permute-start.2) | collective-permute-done | bytes 262176 | tf_op jit(solution)/shard_map/ppermute | solution.py:15
  38.8 2.0 %copy-done.7 = f32[1024,1024]{0,1:T(8,128)} copy-done((f32[1024,1024]{0,1:T(8,128)}, f32[1024,1024]{0,1:T(8,128)S(1)}, u32[]{:S(2)}) %copy-start.7) | copy-done | bytes 4194328
  42.5 3.1 %fusion.7 = f32[1024,128]{1,0:T(8,128)S(1)} fusion(f32[1024,1024]{0,1:T(8,128)} %copy-done.1, f32[1024]{0:T(1024)S(1)} %div.52, f32[1024]{0:T(1024)S(1)} %get-tuple-element.16, bf16[1,1024,128]{2,1,0:T(8,128)(2,1)S(1)} %copy-done.9), kind=kOutput, calls=%fused_computation.23 | convolution fusion | flops 272629760 | bytes 4988928 | tf_op jit(solution)/shard_map/dot_general | solution.py:57
  46.1 3.2 %fusion.10 = f32[1024,128]{1,0:T(8,128)S(1)} fusion(bf16[1024,128]{1,0:T(8,128)(2,1)S(1)} %bitcast.44, f32[1024,1024]{0,1:T(8,128)} %copy-done.7, f32[1024]{0:T(1024)S(1)} %div.55, f32[1024]{0:T(1024)S(1)} %get-tuple-element.10), kind=kOutput, calls=%fused_computation.26 | convolution fusion | flops 272629760 | bytes 4988928 | tf_op jit(solution)/shard_map/dot_general | solution.py:59
  49.3 4.3 %collective-permute-start.5 = (f32[1024,128]{1,0:T(8,128)S(1)}, f32[1024,128]{1,0:T(8,128)S(1)}, u32[]{:S(2)}, u32[]{:S(2)}) collective-permute-start(f32[1024,128]{1,0:T(8,128)S(1)} %fusion.10), channel_id=1, source_target_pairs={{0,509},{1,510},{2,511},{3,0},{4,1},{5,2},{6,3},{7,4},{8,5},{9,6},... | collective-permute-start | bytes 1572872 | tf_op jit(solution)/shard_map/ppermute | solution.py:15
  53.6 0.9 %fusion.9 = f32[1024,128]{1,0:T(8,128)S(1)} fusion(bf16[1024,128]{1,0:T(8,128)(2,1)S(1)} %bitcast.43, f32[1024,1024]{0,1:T(8,128)S(1)} %copy-done.6, f32[1024]{0:T(1024)S(1)} %div.54, f32[1024]{0:T(1024)S(1)} %get-tuple-element.12), kind=kOutput, calls=%fused_computation.25 | convolution fusion | flops 272629760 | bytes 4988928 | tf_op jit(solution)/shard_map/dot_general | solution.py:59
  54.6 9.1 %collective-permute-start.4 = (f32[1024,128]{1,0:T(8,128)S(1)}, f32[1024,128]{1,0:T(8,128)S(1)}, u32[]{:S(2)}, u32[]{:S(2)}) collective-permute-start(f32[1024,128]{1,0:T(8,128)S(1)} %fusion.9), channel_id=1, source_target_pairs={{0,510},{1,511},{2,0},{3,1},{4,2},{5,3},{6,4},{7,5},{8,6},{9,7},{1... | collective-permute-start | bytes 1572872 | tf_op jit(solution)/shard_map/ppermute | solution.py:15
  63.7 0.9 %fusion.8 = f32[1024,128]{1,0:T(8,128)S(1)} fusion(bf16[1024,128]{1,0:T(8,128)(2,1)S(1)} %bitcast.42, f32[1024,1024]{0,1:T(8,128)S(1)} %copy-done.4, f32[1024]{0:T(1024)S(1)} %div.53, f32[1024]{0:T(1024)S(1)} %get-tuple-element.14), kind=kOutput, calls=%fused_computation.24 | convolution fusion | flops 272629760 | bytes 4988928 | tf_op jit(solution)/shard_map/dot_general | solution.py:59
  64.6 3.1 %collective-permute-start.3 = (f32[1024,128]{1,0:T(8,128)S(1)}, f32[1024,128]{1,0:T(8,128)S(1)}, u32[]{:S(2)}, u32[]{:S(2)}) collective-permute-start(f32[1024,128]{1,0:T(8,128)S(1)} %fusion.8), channel_id=1, source_target_pairs={{0,511},{1,0},{2,1},{3,2},{4,3},{5,4},{6,5},{7,6},{8,7},{9,8},{10,... | collective-permute-start | bytes 1572872 | tf_op jit(solution)/shard_map/ppermute | solution.py:15
  67.8 1.0 %convolution_add_fusion.3 = f32[1024,128]{1,0:T(8,128)S(1)} fusion(f32[1024,128]{1,0:T(8,128)S(1)} %fusion.7, bf16[1024,128]{1,0:T(8,128)(2,1)S(1)} %collective-permute-done, f32[1024,1024]{0,1:T(8,128)S(1)} %copy-done.4, f32[1024]{0:T(1024)S(1)} %div.53, f32[1024]{0:T(1024)S(1)} %get-tuple-element.14), kind=kOutput, calls=%fused_computation.22 | convolution fusion | flops 272760832 | bytes 5513216 | tf_op jit(solution)/shard_map/dot_general | solution.py:57
  68.8 1.0 %convolution_add_fusion.2 = f32[1024,128]{1,0:T(8,128)S(1)} fusion(f32[1024,128]{1,0:T(8,128)S(1)} %convolution_add_fusion.3, bf16[1024,128]{1,0:T(8,128)(2,1)S(1)} %collective-permute-done.1, f32[1024,1024]{0,1:T(8,128)S(1)} %copy-done.6, f32[1024]{0:T(1024)S(1)} %div.54, f32[1024]{0:T(1024)S(1)} %get-tuple-element.12), kind=kOutput, calls=%fused_computation.21 | convolution fusion | flops 272760832 | bytes 5513216 | tf_op jit(solution)/shard_map/dot_general | solution.py:57
  69.8 1.8 %convolution_add_fusion.1 = f32[1024,128]{1,0:T(8,128)} fusion(f32[1024,128]{1,0:T(8,128)S(1)} %convolution_add_fusion.2, bf16[1024,128]{1,0:T(8,128)(2,1)S(1)} %collective-permute-done.2, f32[1024,1024]{0,1:T(8,128)S(1)} %copy-done.8, f32[1024]{0:T(1024)S(1)} %div.55, f32[1024]{0:T(1024)S(1)} %get-tuple-element.10), kind=kOutput, calls=%fused_computation.20 | convolution fusion | flops 272760832 | bytes 5513216 | tf_op jit(solution)/shard_map/dot_general | solution.py:57
  71.6 11.2 %collective-permute-done.4 = f32[1024,128]{1,0:T(8,128)S(1)} collective-permute-done((f32[1024,128]{1,0:T(8,128)S(1)}, f32[1024,128]{1,0:T(8,128)S(1)}, u32[]{:S(2)}, u32[]{:S(2)}) %collective-permute-start.4) | collective-permute-done | bytes 524320 | tf_op jit(solution)/shard_map/ppermute | solution.py:15
  82.8 3.5 %collective-permute-done.3 = f32[1024,128]{1,0:T(8,128)S(1)} collective-permute-done((f32[1024,128]{1,0:T(8,128)S(1)}, f32[1024,128]{1,0:T(8,128)S(1)}, u32[]{:S(2)}, u32[]{:S(2)}) %collective-permute-start.3) | collective-permute-done | bytes 524320 | tf_op jit(solution)/shard_map/ppermute | solution.py:15
  86.3 1.8 %fusion.6 = f32[1,1024,128]{2,1,0:T(8,128)} fusion(f32[1024,128]{1,0:T(8,128)S(1)} %collective-permute-done.5, f32[1024,128]{1,0:T(8,128)S(1)} %collective-permute-done.4, f32[1024,128]{1,0:T(8,128)S(1)} %collective-permute-done.3, bf16[1024,128]{1,0:T(8,128)(2,1)S(1)} %bitcast.41, f32[1024,1024]{0,1:T(8,128)S(1)} %copy-done.2, f32[1024]{0:T(1024)S(1)} %div.52, ...), kind=kOutput, calls=%fused_computation.19 | convolution fusion | flops 273022976 | bytes 6561792 | tf_op jit(solution)/shard_map/dot_general | solution.py:59
  (54 shorter events, 7.1 us)
Async XLA Ops:
  0.6 4.8 %copy-start = (bf16[32,32,128]{2,1,0:T(8,128)(2,1)S(1)}, bf16[32,32,128]{2,1,0:T(8,128)(2,1)}, u32[]{:S(2)}) copy-start(bf16[32,32,128]{2,1,0:T(8,128)(2,1)} %param.3) | copy-start | bytes 786436
  0.6 10.2 %collective-permute-start = (bf16[1024,128]{1,0:T(8,128)(2,1)}, bf16[1024,128]{1,0:T(8,128)(2,1)S(1)}, u32[]{:S(2)}, u32[]{:S(2)}) collective-permute-start(bf16[1024,128]{1,0:T(8,128)(2,1)} %bitcast.45), channel_id=1, source_target_pairs={{0,1},{1,2},{2,3},{3,4},{4,5},{5,6},{6,7},{7,8},{8,9},{9,10},{10,1... | collective-permute-start | bytes 786440 | tf_op jit(solution)/shard_map/ppermute | solution.py:15
  7.1 1.9 %copy-start.1 = (f32[1024,1024]{0,1:T(8,128)}, f32[1024,1024]{0,1:T(8,128)S(1)}, u32[]{:S(2)}) copy-start(f32[1024,1024]{0,1:T(8,128)S(1)} %get-tuple-element.17) | copy-start | bytes 12582916
  10.8 14.2 %collective-permute-start.1 = (bf16[1024,128]{1,0:T(8,128)(2,1)S(1)}, bf16[1024,128]{1,0:T(8,128)(2,1)S(1)}, u32[]{:S(2)}, u32[]{:S(2)}) collective-permute-start(bf16[1024,128]{1,0:T(8,128)(2,1)S(1)} %collective-permute-done), channel_id=1, source_target_pairs={{0,1},{1,2},{2,3},{3,4},{4,5},{5,6},{6,7},{7,8},{8,9},{9,10},{10,1... | collective-permute-start | bytes 786440 | tf_op jit(solution)/shard_map/ppermute | solution.py:15
  14.0 2.0 %copy-start.3 = (f32[1024,1024]{0,1:T(8,128)}, f32[1024,1024]{0,1:T(8,128)S(1)}, u32[]{:S(2)}) copy-start(f32[1024,1024]{0,1:T(8,128)S(1)} %get-tuple-element.15) | copy-start | bytes 12582916
  25.0 13.1 %collective-permute-start.2 = (bf16[1024,128]{1,0:T(8,128)(2,1)S(1)}, bf16[1024,128]{1,0:T(8,128)(2,1)S(1)}, u32[]{:S(2)}, u32[]{:S(2)}) collective-permute-start(bf16[1024,128]{1,0:T(8,128)(2,1)S(1)} %collective-permute-done.1), channel_id=1, source_target_pairs={{0,1},{1,2},{2,3},{3,4},{4,5},{5,6},{6,7},{7,8},{8,9},{9,10},{10,1... | collective-permute-start | bytes 786440 | tf_op jit(solution)/shard_map/ppermute | solution.py:15
  27.6 2.0 %copy-start.5 = (f32[1024,1024]{0,1:T(8,128)}, f32[1024,1024]{0,1:T(8,128)S(1)}, u32[]{:S(2)}) copy-start(f32[1024,1024]{0,1:T(8,128)S(1)} %get-tuple-element.13) | copy-start | bytes 12582916
  30.5 11.2 %copy-start.10 = (s32[32]{0:T(128)S(1)}, s32[32]{0:T(128)}, u32[]{:S(2)}) copy-start(s32[32]{0:T(128)} %param.4) | copy-start | bytes 388
  30.5 12.0 %copy-start.9 = (bf16[1,1024,128]{2,1,0:T(8,128)(2,1)S(1)}, bf16[1,1024,128]{2,1,0:T(8,128)(2,1)}, u32[]{:S(2)}) copy-start(bf16[1,1024,128]{2,1,0:T(8,128)(2,1)} %param.5) | copy-start | bytes 786436
  38.8 2.0 %copy-start.7 = (f32[1024,1024]{0,1:T(8,128)}, f32[1024,1024]{0,1:T(8,128)S(1)}, u32[]{:S(2)}) copy-start(f32[1024,1024]{0,1:T(8,128)S(1)} %get-tuple-element.11) | copy-start | bytes 12582916
  46.1 7.6 %copy-start.6 = (f32[1024,1024]{0,1:T(8,128)S(1)}, f32[1024,1024]{0,1:T(8,128)}, u32[]{:S(2)}) copy-start(f32[1024,1024]{0,1:T(8,128)} %copy-done.5) | copy-start | bytes 12582916
  46.1 17.6 %copy-start.4 = (f32[1024,1024]{0,1:T(8,128)S(1)}, f32[1024,1024]{0,1:T(8,128)}, u32[]{:S(2)}) copy-start(f32[1024,1024]{0,1:T(8,128)} %copy-done.3) | copy-start | bytes 12582916
  49.3 22.3 %collective-permute-start.5 = (f32[1024,128]{1,0:T(8,128)S(1)}, f32[1024,128]{1,0:T(8,128)S(1)}, u32[]{:S(2)}, u32[]{:S(2)}) collective-permute-start(f32[1024,128]{1,0:T(8,128)S(1)} %fusion.10), channel_id=1, source_target_pairs={{0,509},{1,510},{2,511},{3,0},{4,1},{5,2},{6,3},{7,4},{8,5},{9,6},... | collective-permute-start | bytes 1572872 | tf_op jit(solution)/shard_map/ppermute | solution.py:15
  54.6 28.3 %collective-permute-start.4 = (f32[1024,128]{1,0:T(8,128)S(1)}, f32[1024,128]{1,0:T(8,128)S(1)}, u32[]{:S(2)}, u32[]{:S(2)}) collective-permute-start(f32[1024,128]{1,0:T(8,128)S(1)} %fusion.9), channel_id=1, source_target_pairs={{0,510},{1,511},{2,0},{3,1},{4,2},{5,3},{6,4},{7,5},{8,6},{9,7},{1... | collective-permute-start | bytes 1572872 | tf_op jit(solution)/shard_map/ppermute | solution.py:15
  64.6 5.2 %copy-start.8 = (f32[1024,1024]{0,1:T(8,128)S(1)}, f32[1024,1024]{0,1:T(8,128)}, u32[]{:S(2)}) copy-start(f32[1024,1024]{0,1:T(8,128)} %copy-done.7) | copy-start | bytes 12582916
  64.6 21.7 %collective-permute-start.3 = (f32[1024,128]{1,0:T(8,128)S(1)}, f32[1024,128]{1,0:T(8,128)S(1)}, u32[]{:S(2)}, u32[]{:S(2)}) collective-permute-start(f32[1024,128]{1,0:T(8,128)S(1)} %fusion.8), channel_id=1, source_target_pairs={{0,511},{1,0},{2,1},{3,2},{4,3},{5,4},{6,5},{7,6},{8,7},{9,8},{10,... | collective-permute-start | bytes 1572872 | tf_op jit(solution)/shard_map/ppermute | solution.py:15
  68.8 17.6 %copy-start.2 = (f32[1024,1024]{0,1:T(8,128)S(1)}, f32[1024,1024]{0,1:T(8,128)}, u32[]{:S(2)}) copy-start(f32[1024,1024]{0,1:T(8,128)} %copy-done.1) | copy-start | bytes 12582916
where the time goes:
time: 88.4 us; the launch traced here: 88.1 us
  waiting for transfers between devices  31.2 us (35%)
  starting transfers between devices  25.6 us (29%)
  matrix products  17.7 us (20%)
  local copies, waits for them, and re-layouts  8.73 us (10%)
  other arithmetic  4.04 us (5%)
  between operations  0.9 us (1%)
    ppermute x6, waiting for transfers between devices, passed_along(): return lax.ppermute(value, axis, pairs)  31.2 us
    ppermute x6, starting transfers between devices, passed_along(): return lax.ppermute(value, axis, pairs)  25.6 us
    unnamed x22, local copies, waits for them, and re-layouts  7.85 us
    dot_general x4, matrix products, device_terms(): jnp.dot(weight, page, preferred_element_type=jnp.float32)  6.95 us
    dot_general x4, matrix products, device_terms(): lax.dot_general(weight, query_rows, (((0,), (0,)), ((), ())), preferred_e...  6.87 us
    dot_general x4, matrix products, token_scores(): lax.dot_general(query_rows, page, (((1,), (1,)), ((), ())), preferred_ele...  3.85 us
    reduce_sum x4, other arithmetic, token_scores(): total = jnp.sum(powers, axis=1, keepdims=True)  2.92 us
  transfers between devices with their start and end apart: 6, of which 5 were waited for; matrix products, arithmetic and copies ran while one was open for 13% of the time, Pallas kernels for 0%

commit v1 on v0

v1 whole, which is shorter than its diff:
```python
import functools
import math

import jax
import jax.numpy as jnp
from jax import lax
from jax.experimental import pallas as pl
from jax.experimental.pallas import tpu as pltpu
from jax.sharding import PartitionSpec as P


tau_scale = 0.1
EXPONENT = math.log2(math.e) / tau_scale
CHUNK = 256
PAD = 16
MIB = 1024 * 1024

VMEM = pl.BlockSpec(memory_space=pltpu.VMEM)


def passed_along(value, axis, steps):
    count = lax.axis_size(axis)
    pairs = [(source, (source + steps) % count) for source in range(count)]
    return lax.ppermute(value, axis, pairs)


def on_core(body, outs, args, flops, name, limit=24):
    return pl.pallas_call(
        body,
        out_shape=[pltpu.VMEM(shape, dtype) for shape, dtype in outs],
        in_specs=[VMEM] * len(args),
        out_specs=[VMEM] * len(outs),
        compiler_params=pltpu.CompilerParams(vmem_limit_bytes=limit * MIB),
        cost_estimate=pl.CostEstimate(flops=flops, bytes_accessed=2 * MIB, transcendentals=0),
        name=name,
    )(*args)


def rows_dot(a, b):
    return lax.dot_general(a, b, (((1,), (1,)), ((), ())), preferred_element_type=jnp.float32)


def token_powers(page, query, powers_ref, total_ref, smooth_ref, row):
    rows = query.shape[0]
    for start in range(0, rows, CHUNK):
        cut = slice(start, start + CHUNK)
        products = rows_dot(page[...], query[cut, :])
        largest = jnp.max(products, axis=0, keepdims=True)
        powers = jnp.exp2((products - largest) * EXPONENT)
        total = jnp.sum(powers, axis=0, keepdims=True)
        powers_ref[:, cut] = powers.astype(jnp.bfloat16)
        total_ref[row : row + 1, cut] = total
        smooth_ref[row : row + 1, cut] = largest + tau_scale * jnp.log(total)


def mix_pages(page_t, powers_ref, mixed_ref):
    rows = powers_ref.shape[1]
    for start in range(0, rows, CHUNK):
        cut = slice(start, start + CHUNK)
        mixed_ref[:, cut] = jnp.dot(page_t, powers_ref[:, cut], preferred_element_type=jnp.float32)


def turned(value):
    return value.astype(jnp.float32).T.astype(jnp.bfloat16)


def unit_body(page, query, powers_ref, mixed_ref, total_ref, smooth_ref, query_t_ref):
    token_powers(page, query, powers_ref, total_ref, smooth_ref, 0)
    mix_pages(turned(page[...]), powers_ref, mixed_ref)
    query_t_ref[...] = turned(query[...])


def query_sums(value, tokens):
    lane = lax.broadcasted_iota(jnp.int32, value.shape, 1)
    width = value.shape[1]
    step = tokens // 2
    while step:
        ahead = pltpu.roll(value, width - step, 1)
        behind = pltpu.roll(value, step, 1)
        value = value + jnp.where((lane & step) != 0, behind, ahead)
        step //= 2
    return value


def pair_body(tokens, page, query, next_query, smooth_a, smooth_b, positive,
              powers_a_ref, powers_b_ref, total_ref, own_ref, next_ref, smooth_ref):
    token_powers(page, query, powers_a_ref, total_ref, smooth_ref, 0)
    token_powers(page, next_query, powers_b_ref, total_ref, smooth_ref, 1)
    rows = jnp.concatenate([smooth_a[...], smooth_ref[0:1, :], smooth_b[...], smooth_ref[1:2, :]], axis=0)
    sums = query_sums(rows, tokens)
    own_ref[0:2, :] = sums[0:2, :]
    own_ref[2:3, :] = positive[...]
    own_ref[3:4, :] = positive[...]
    next_ref[...] = sums[2:4, :]


def mix_body(page, powers_a, powers_b, mixed_a_ref, mixed_b_ref):
    page_t = turned(page[...])
    mix_pages(page_t, powers_a, mixed_a_ref)
    mix_pages(page_t, powers_b, mixed_b_ref)


def slopes_of(scores, positive):
    flags = [(positive == float(offset)).astype(jnp.float32) for offset in range(4)]
    positive_score = sum(flag * score for flag, score in zip(flags, scores))
    margins = [score - positive_score for score in scores]
    loss = sum((1.0 - flag) * jax.nn.softplus(margin) for flag, margin in zip(flags, margins))
    terms = [(1.0 - flag) * jax.nn.sigmoid(margin) for flag, margin in zip(flags, margins)]
    total = sum(terms)
    return loss, [term - flag * total for flag, term in zip(flags, terms)]


def to_short(value):
    largest = jnp.maximum(jnp.max(jnp.abs(value), axis=0, keepdims=True), 1e-38)
    power = jnp.minimum(jnp.floor(math.log2(32000.0) - jnp.log2(largest)), 126.0)
    short = jnp.round(value * jnp.exp2(power)).astype(jnp.int32).astype(jnp.int16)
    tail = jnp.broadcast_to(power, (PAD, value.shape[1])).astype(jnp.int32).astype(jnp.int16)
    return short, tail


def from_short(ref, rows):
    power = ref[rows : rows + PAD, :].astype(jnp.int32).astype(jnp.float32)[0:1, :]
    return ref[0:rows, :].astype(jnp.int32).astype(jnp.float32) * jnp.exp2(-power)


def scaled(query_t, weight):
    return (query_t.astype(jnp.float32) * weight).astype(jnp.bfloat16)


def send_body(from_next, from_last, own, onward, total_own_a, total_own_b, total_far, query_t, next_query_t,
              powers_a, powers_b, mixed_own_b, mixed_far_b,
              page_out_ref, query_out_ref, loss_ref, weight_ref):
    loss, slopes = slopes_of([own[0:1, :], from_last[0:1, :], own[1:2, :], from_last[1:2, :]], own[2:3, :])
    _, next_slopes = slopes_of([from_next[0:1, :], onward[0:1, :], from_next[1:2, :], onward[1:2, :]], from_next[2:3, :])
    loss_ref[...] = loss
    weight_own_a = slopes[0] / total_own_a[...]
    weight_far_a = slopes[2] / total_far[0:1, :]
    weight_own_b = next_slopes[1] / total_own_b[...]
    weight_far_b = next_slopes[3] / total_far[1:2, :]
    weight_ref[0:1, :] = weight_own_a
    weight_ref[1:2, :] = weight_own_b
    weight_ref[2:3, :] = weight_far_a
    weight_ref[3:4, :] = weight_far_b
    page_term = rows_dot(powers_a[...], scaled(query_t[...], weight_far_a))
    page_term = page_term + rows_dot(powers_b[...], scaled(next_query_t[...], weight_far_b))
    count = page_term.shape[0]
    short, tail = to_short(page_term)
    page_out_ref[0:count, :] = short
    page_out_ref[count : count + PAD, :] = tail
    query_term = mixed_own_b[...] * weight_own_b + mixed_far_b[...] * weight_far_b
    width = query_term.shape[0]
    short, tail = to_short(query_term)
    query_out_ref[0:width, :] = short
    query_out_ref[width : width + PAD, :] = tail


def keep_body(weight, query_t, next_query_t, powers_a, powers_b, mixed_own_a, mixed_far_a,
              page_ref, query_ref):
    page_term = rows_dot(powers_a[...], scaled(query_t[...], weight[0:1, :]))
    page_ref[...] = page_term + rows_dot(powers_b[...], scaled(next_query_t[...], weight[1:2, :]))
    query_ref[...] = mixed_own_a[...] * weight[0:1, :] + mixed_far_a[...] * weight[2:3, :]


def last_body(page_own, query_own, page_in, query_in, page_ref, query_ref):
    query_ref[...] = (query_own[...] + from_short(query_in, query_own.shape[0])).T
    page_ref[...] = page_own[...] + from_short(page_in, page_own.shape[0])


def on_device(queries, positives, pages):
    count, tokens, width = queries.shape
    page = pages[0]
    patches = page.shape[0]
    query = queries.reshape(count * tokens, width)
    rows = count * tokens
    f32, bf16, i16 = jnp.float32, jnp.bfloat16, jnp.int16
    unit = 2 * rows * patches * width

    far_page = passed_along(page, "dp", 2)
    next_query = passed_along(query, "dp", -1)
    positive = jnp.repeat(positives.astype(f32), tokens)[None, :]

    unit_outs = [((patches, rows), bf16), ((width, rows), f32), ((1, rows), f32), ((1, rows), f32), ((width, rows), bf16)]
    powers_a, mixed_a, total_a, smooth_a, query_t = on_core(unit_body, unit_outs, (page, query), 2 * unit, "own_unit")
    powers_b, mixed_b, total_b, smooth_b, next_query_t = on_core(
        unit_body, unit_outs, (page, next_query), 2 * unit, "next_unit")
    powers_c, powers_d, total_far, own, onward, _ = on_core(
        functools.partial(pair_body, tokens),
        [((patches, rows), bf16), ((patches, rows), bf16), ((2, rows), f32), ((4, rows), f32), ((2, rows), f32), ((2, rows), f32)],
        (far_page, query, next_query, smooth_a, smooth_b, positive), 2 * unit, "far_units")
    from_next = passed_along(own, "dp", -1)
    from_last = passed_along(onward, "dp", 1)
    mixed_c, mixed_d = on_core(
        mix_body, [((width, rows), f32)] * 2, (far_page, powers_c, powers_d), 2 * unit, "far_mix")
    page_out, query_out, loss, weight = on_core(
        send_body,
        [((patches + PAD, width), i16), ((width + PAD, rows), i16), ((1, rows), f32), ((4, rows), f32)],
        (from_next, from_last, own, onward, total_a, total_b, total_far, query_t, next_query_t,
         powers_c, powers_d, mixed_b, mixed_d), 2 * unit, "send_terms")
    page_in = passed_along(page_out, "dp", -2)
    query_in = passed_along(query_out, "dp", 1)
    page_own, query_own = on_core(
        keep_body, [((patches, width), f32), ((width, rows), f32)],
        (weight, query_t, next_query_t, powers_a, powers_b, mixed_a, mixed_c), 2 * unit, "own_terms")
    query_grad, page_grad = pl.pallas_call(
        lambda a, b, c, d, page_ref, query_ref: last_body(a, b, c, d, page_ref, query_ref),
        out_shape=[jax.ShapeDtypeStruct((patches, width), f32), jax.ShapeDtypeStruct((rows, width), f32)],
        in_specs=[VMEM] * 4,
        out_specs=[VMEM] * 2,
        compiler_params=pltpu.CompilerParams(vmem_limit_bytes=24 * MIB),
        name="last_sum",
    )(page_own, query_own, page_in, query_in)[::-1]
    return (loss.reshape(count, tokens)[:, 0], query_grad.reshape(count, tokens, width), page_grad[None])


def solution(mesh):
    in_specs = (P("dp", None, None), P("dp"), P("dp", None, None))
    out_specs = (P("dp"), P("dp", None, None), P("dp", None, None))
    return jax.shard_map(
        on_device, mesh=mesh, in_specs=in_specs, out_specs=out_specs, check_vma=False
    )
```

time: 88.4 us -> 71.7 us (0.81)
  waiting for transfers between devices: 31.2 us -> 4.45 us
  matrix products: 17.7 us -> 0 us
  Pallas kernels: 0 us -> 16 us
  starting transfers between devices: 25.6 us -> 40.7 us
  other arithmetic: 4.04 us -> 1.32 us
    ppermute x6, waiting for transfers between devices: 31.2 us -> 4.45 us  [passed_along(): return lax.ppermute(value, axis, pairs)]
    dot_general x12 -> x0, matrix products: 17.7 us -> none  [the longest x4 6.95 us: device_terms(): jnp.dot(weight, page, preferred_element_type=jnp.float32)]
    pallas_call x0 -> x7, Pallas kernels: none -> 16 us  [the longest x6 13.8 us: on_core(): pl.pallas_call(body, out_shape=[pltpu.VMEM(shape, dtype) for shape, dtype...]
    ppermute x6, starting transfers between devices: 25.6 us -> 40.7 us  [passed_along(): return lax.ppermute(value, axis, pairs)]
    reduce_sum x10 -> x0, other arithmetic: 3.97 us -> none  [the longest x4 2.92 us: token_scores(): total = jnp.sum(powers, axis=1, keepdims=True)]
    unnamed x22 -> x15, local copies, waits for them, and re-layouts: 7.85 us -> 7.25 us
  transfers between devices with their start and end apart: 6 -> 6, of which waited for: 5 -> 2; matrix products, arithmetic and copies ran while one was open for 13% -> 4% of each run, Pallas kernels for 0% -> 10%
where the time goes in v1:
time: 71.7 us; the launch traced here: 71.2 us
  starting transfers between devices  40.7 us (57%)
  Pallas kernels  16 us (22%)
  local copies, waits for them, and re-layouts  7.99 us (11%)
  waiting for transfers between devices  4.45 us (6%)
  other arithmetic  1.32 us (2%)
  between operations  0.76 us (1%)
    ppermute x6, starting transfers between devices, passed_along(): return lax.ppermute(value, axis, pairs)  40.7 us
    pallas_call x6, Pallas kernels, on_core(): pl.pallas_call(body, out_shape=[pltpu.VMEM(shape, dtype) for shape, dtype...  13.8 us
    unnamed x15, local copies, waits for them, and re-layouts  7.25 us
    ppermute x6, waiting for transfers between devices, passed_along(): return lax.ppermute(value, axis, pairs)  4.45 us
    pallas_call x1, Pallas kernels, on_device(): pl.pallas_call(lambda a, b, c, d, page_ref, query_ref: last_body(a, b, c,...  2.17 us
  transfers between devices with their start and end apart: 6, of which 2 were waited for; matrix products, arithmetic and copies ran while one was open for 4% of the time, Pallas kernels for 10%

profile of v1, /device:TPU:1, one launch (start us, length us, event | category | flops | bytes accessed | tf_op | source)
XLA Modules:
  0.0 71.2 jit_solution(17167018340631292180)
XLA Ops:
  0.6 8.8 %collective-permute-start.1 = (bf16[1024,128]{1,0:T(8,128)(2,1)}, bf16[1024,128]{1,0:T(8,128)(2,1)}, u32[]{:S(2)}, u32[]{:S(2)}) collective-permute-start(bf16[1024,128]{1,0:T(8,128)(2,1)} %bitcast.9), channel_id=1, source_target_pairs={{0,511},{1,0},{2,1},{3,2},{4,3},{5,4},{6,5},{7,6},{8,7},{9,8},{10,... | collective-permute-start | bytes 786440 | tf_op jit(solution)/shard_map/ppermute | solution.py:24
  9.4 1.9 %collective-permute-start = (bf16[1024,128]{1,0:T(8,128)(2,1)}, bf16[1024,128]{1,0:T(8,128)(2,1)S(1)}, u32[]{:S(2)}, u32[]{:S(2)}) collective-permute-start(bf16[1024,128]{1,0:T(8,128)(2,1)} %bitcast.6), channel_id=1, source_target_pairs={{0,2},{1,3},{2,4},{3,5},{4,6},{5,7},{6,8},{7,9},{8,10},{9,11},{10,... | collective-permute-start | bytes 786440 | tf_op jit(solution)/shard_map/ppermute | solution.py:24
  11.4 0.7 convert_element_type.3
  12.2 1.0 %copy-done.4 = bf16[1,1024,128]{2,1,0:T(8,128)(2,1)S(1)} copy-done((bf16[1,1024,128]{2,1,0:T(8,128)(2,1)S(1)}, bf16[1,1024,128]{2,1,0:T(8,128)(2,1)}, u32[]{:S(2)}) %copy-start.4) | copy-done | bytes 262168
  13.1 0.9 %copy-done.5 = bf16[32,32,128]{2,1,0:T(8,128)(2,1)S(1)} copy-done((bf16[32,32,128]{2,1,0:T(8,128)(2,1)S(1)}, bf16[32,32,128]{2,1,0:T(8,128)(2,1)}, u32[]{:S(2)}) %copy-start.5) | copy-done | bytes 262168
  14.1 1.9 %own_unit.1 = (bf16[1024,1024]{1,0:T(8,128)(2,1)S(1)}, f32[128,1024]{1,0:T(8,128)S(1)}, f32[1,1024]{1,0:T(1,128)S(1)}, f32[1,1024]{1,0:T(1,128)S(1)}, bf16[128,1024]{1,0:T(8,128)(2,1)S(1)}) custom-call(bf16[1024,128]{1,0:T(8,128)(2,1)S(1)} %bitcast.7, bf16[1024,128]{1,0:T(8,128)(2,1)S(1)} %bitcast.10), custom_call_target="tpu_custom_call" | custom-call | flops 536870912 | bytes 2097152 | tf_op jit(solution)/shard_map/own_unit/pallas_call | solution.py:28
  16.0 2.9 %next_unit.1 = (bf16[1024,1024]{1,0:T(8,128)(2,1)S(1)}, f32[128,1024]{1,0:T(8,128)S(1)}, f32[1,1024]{1,0:T(1,128)S(1)}, f32[1,1024]{1,0:T(1,128)S(1)}, bf16[128,1024]{1,0:T(8,128)(2,1)S(1)}) custom-call(bf16[1024,128]{1,0:T(8,128)(2,1)S(1)} %bitcast.8, bf16[1024,128]{1,0:T(8,128)(2,1)} %collective-permute-done.1.query.next_query), custom_call_target="tpu_custom_call" | custom-call | flops 536870912 | bytes 2097152 | tf_op jit(solution)/shard_map/next_unit/pallas_call | solution.py:28
  18.9 1.3 %copy-done = bf16[1024,1024]{1,0:T(8,128)(2,1)} copy-done((bf16[1024,1024]{1,0:T(8,128)(2,1)}, bf16[1024,1024]{1,0:T(8,128)(2,1)S(1)}, u32[]{:S(2)}) %copy-start) | copy-done | bytes 2097176
  20.3 3.5 %collective-permute-done.page = bf16[1024,128]{1,0:T(8,128)(2,1)S(1)} collective-permute-done((bf16[1024,128]{1,0:T(8,128)(2,1)}, bf16[1024,128]{1,0:T(8,128)(2,1)S(1)}, u32[]{:S(2)}, u32[]{:S(2)}) %collective-permute-start) | collective-permute-done | bytes 262176 | tf_op jit(solution)/shard_map/ppermute | solution.py:24
  23.8 4.7 %far_units.1 = (bf16[1024,1024]{1,0:T(8,128)(2,1)S(1)}, bf16[1024,1024]{1,0:T(8,128)(2,1)S(1)}, f32[2,1024]{1,0:T(2,128)S(1)}, f32[4,1024]{1,0:T(4,128)S(1)}, f32[2,1024]{1,0:T(2,128)S(1)}, /*index=5*/f32[2,1024]{1,0:T(2,128)}) custom-call(bf16[1024,128]{1,0:T(8,128)(2,1)S(1)} %collective-permute-done.page, bf16[1024,128]{1,0:T(8,128)(2,1)S(1)} %bitcast.11, ...), custom_call_target="tpu_custom_call" | custom-call | flops 536870912 | bytes 2097152 | tf_op jit(solution)/shard_map/far_units/pallas_call | solution.py:28
  28.5 9.6 %collective-permute-start.2 = (f32[4,1024]{1,0:T(4,128)S(1)}, f32[4,1024]{1,0:T(4,128)S(1)}, u32[]{:S(2)}, u32[]{:S(2)}) collective-permute-start(f32[4,1024]{1,0:T(4,128)S(1)} %get-tuple-element.30.own), channel_id=1, source_target_pairs={{0,511},{1,0},{2,1},{3,2},{4,3},{5,4},{6,5},{7,6},{8,7},{9,8},{10,... | collective-permute-start | bytes 49160 | tf_op jit(solution)/shard_map/ppermute | solution.py:24
  38.1 1.9 %collective-permute-start.3 = (f32[2,1024]{1,0:T(2,128)S(1)}, f32[2,1024]{1,0:T(2,128)S(1)}, u32[]{:S(2)}, u32[]{:S(2)}) collective-permute-start(f32[2,1024]{1,0:T(2,128)S(1)} %get-tuple-element.31.onward), channel_id=1, source_target_pairs={{0,1},{1,2},{2,3},{3,4},{4,5},{5,6},{6,7},{7,8},{8,9},{9,10},{10,1... | collective-permute-start | bytes 24584 | tf_op jit(solution)/shard_map/ppermute | solution.py:24
  40.1 0.8 %far_mix.1 = (f32[128,1024]{1,0:T(8,128)S(1)}, f32[128,1024]{1,0:T(8,128)S(1)}) custom-call(bf16[1024,128]{1,0:T(8,128)(2,1)S(1)} %collective-permute-done.page, bf16[1024,1024]{1,0:T(8,128)(2,1)S(1)} %get-tuple-element.37.powers_a, bf16[1024,1024]{1,0:T(8,128)(2,1)S(1)} %get-tuple-element.38.powers_b), custom_call_target="tpu_custom_call" | custom-call | flops 536870912 | bytes 2097152 | tf_op jit(solution)/shard_map/far_mix/pallas_call | solution.py:28
  40.8 0.8 %copy-done.2 = f32[128,1024]{1,0:T(8,128)} copy-done((f32[128,1024]{1,0:T(8,128)}, f32[128,1024]{1,0:T(8,128)S(1)}, u32[]{:S(2)}) %copy-start.2) | copy-done | bytes 524312
  41.6 0.9 %collective-permute-done.3.from_last = f32[2,1024]{1,0:T(2,128)S(1)} collective-permute-done((f32[2,1024]{1,0:T(2,128)S(1)}, f32[2,1024]{1,0:T(2,128)S(1)}, u32[]{:S(2)}, u32[]{:S(2)}) %collective-permute-start.3) | collective-permute-done | bytes 8224 | tf_op jit(solution)/shard_map/ppermute | solution.py:24
  42.6 2.2 %send_terms.1 = (s16[1040,128]{1,0:T(8,128)(2,1)}, s16[144,1024]{1,0:T(8,128)(2,1)}, f32[1,1024]{1,0:T(1,128)S(1)}, f32[4,1024]{1,0:T(4,128)S(1)}) custom-call(f32[4,1024]{1,0:T(4,128)S(1)} %collective-permute-done.2.from_next, f32[2,1024]{1,0:T(2,128)S(1)} %collective-permute-done.3.from_last, f32[4,1024]{1,0:T(4,128)S(1)} %get-tuple-element.30.own, ...), custom_call_target="tpu_custom_call" | custom-call | flops 536870912 | bytes 2097152 | tf_op jit(solution)/shard_map/send_terms/pallas_call | solution.py:28
  44.8 2.5 %collective-permute-start.5 = (s16[144,1024]{1,0:T(8,128)(2,1)}, s16[144,1024]{1,0:T(8,128)(2,1)S(1)}, u32[]{:S(2)}, u32[]{:S(2)}) collective-permute-start(s16[144,1024]{1,0:T(8,128)(2,1)} %get-tuple-element.50), channel_id=1, source_target_pairs={{0,1},{1,2},{2,3},{3,4},{4,5},{5,6},{6,7},{7,8},{8,9},{9,10},{10,1... | collective-permute-start | bytes 884744 | tf_op jit(solution)/shard_map/ppermute | solution.py:24
  47.2 16.0 %collective-permute-start.4 = (s16[1040,128]{1,0:T(8,128)(2,1)}, s16[1040,128]{1,0:T(8,128)(2,1)}, u32[]{:S(2)}, u32[]{:S(2)}) collective-permute-start(s16[1040,128]{1,0:T(8,128)(2,1)} %get-tuple-element.49), channel_id=1, source_target_pairs={{0,510},{1,511},{2,0},{3,1},{4,2},{5,3},{6,4},{7,5},{8,6},{9,7},{1... | collective-permute-start | bytes 798728 | tf_op jit(solution)/shard_map/ppermute | solution.py:24
  63.7 0.7 reduce.3
  64.5 0.6 copy.7
  65.0 1.6 %copy-done.1 = bf16[1024,1024]{1,0:T(8,128)(2,1)S(1)} copy-done((bf16[1024,1024]{1,0:T(8,128)(2,1)S(1)}, bf16[1024,1024]{1,0:T(8,128)(2,1)}, u32[]{:S(2)}) %copy-start.1) | copy-done | bytes 2097176
  66.6 1.0 %copy-done.3 = f32[128,1024]{1,0:T(8,128)S(1)} copy-done((f32[128,1024]{1,0:T(8,128)S(1)}, f32[128,1024]{1,0:T(8,128)}, u32[]{:S(2)}) %copy-start.3) | copy-done | bytes 524312
  67.7 1.4 %own_terms.1 = (f32[1024,128]{1,0:T(8,128)S(1)}, f32[128,1024]{1,0:T(8,128)S(1)}) custom-call(f32[4,1024]{1,0:T(4,128)S(1)} %get-tuple-element.42.weight, bf16[128,1024]{1,0:T(8,128)(2,1)S(1)} %get-tuple-element.35.query_t, bf16[128,1024]{1,0:T(8,128)(2,1)S(1)} %get-tuple-element.36.next_query_t, bf16[1024,1024]{1,0:T(8,128)(2,1)S(1)} %get-tuple-element.43.powers_a, ...), custom_call_target="tpu_custom_call" | custom-call | flops 536870912 | bytes 2097152 | tf_op jit(solution)/shard_map/own_terms/pallas_call | solution.py:28
  69.1 2.2 %last_sum.1 = (f32[1024,128]{1,0:T(8,128)}, f32[1024,128]{1,0:T(8,128)}) custom-call(f32[1024,128]{1,0:T(8,128)S(1)} %get-tuple-element.47.a, f32[128,1024]{1,0:T(8,128)S(1)} %get-tuple-element.48.b, s16[1040,128]{1,0:T(8,128)(2,1)} %collective-permute-done.4.c, s16[144,1024]{1,0:T(8,128)(2,1)S(1)} %collective-permute-done.5.d), custom_call_target="tpu_custom_call" | custom-call | tf_op jit(solution)/shard_map/last_sum/pallas_call | solution.py:204
  (16 shorter events, 0.8 us)
Async XLA Ops:
  0.6 15.4 %collective-permute-start.1 = (bf16[1024,128]{1,0:T(8,128)(2,1)}, bf16[1024,128]{1,0:T(8,128)(2,1)}, u32[]{:S(2)}, u32[]{:S(2)}) collective-permute-start(bf16[1024,128]{1,0:T(8,128)(2,1)} %bitcast.9), channel_id=1, source_target_pairs={{0,511},{1,0},{2,1},{3,2},{4,3},{5,4},{6,5},{7,6},{8,7},{9,8},{10,... | collective-permute-start | bytes 786440 | tf_op jit(solution)/shard_map/ppermute | solution.py:24
  9.4 14.4 %collective-permute-start = (bf16[1024,128]{1,0:T(8,128)(2,1)}, bf16[1024,128]{1,0:T(8,128)(2,1)S(1)}, u32[]{:S(2)}, u32[]{:S(2)}) collective-permute-start(bf16[1024,128]{1,0:T(8,128)(2,1)} %bitcast.6), channel_id=1, source_target_pairs={{0,2},{1,3},{2,4},{3,5},{4,6},{5,7},{6,8},{7,9},{8,10},{9,11},{10,... | collective-permute-start | bytes 786440 | tf_op jit(solution)/shard_map/ppermute | solution.py:24
  12.2 1.0 %copy-start.4 = (bf16[1,1024,128]{2,1,0:T(8,128)(2,1)S(1)}, bf16[1,1024,128]{2,1,0:T(8,128)(2,1)}, u32[]{:S(2)}) copy-start(bf16[1,1024,128]{2,1,0:T(8,128)(2,1)} %param.5) | copy-start | bytes 786436
  13.1 0.9 %copy-start.5 = (bf16[32,32,128]{2,1,0:T(8,128)(2,1)S(1)}, bf16[32,32,128]{2,1,0:T(8,128)(2,1)}, u32[]{:S(2)}) copy-start(bf16[32,32,128]{2,1,0:T(8,128)(2,1)} %param.3) | copy-start | bytes 786436
  14.1 9.7 %copy-start.6 = (bf16[32,32,128]{2,1,0:T(8,128)(2,1)S(1)}, bf16[32,32,128]{2,1,0:T(8,128)(2,1)}, u32[]{:S(2)}) copy-start(bf16[32,32,128]{2,1,0:T(8,128)(2,1)} %param.3) | copy-start | bytes 786436
  18.9 1.3 %copy-start = (bf16[1024,1024]{1,0:T(8,128)(2,1)}, bf16[1024,1024]{1,0:T(8,128)(2,1)S(1)}, u32[]{:S(2)}) copy-start(bf16[1024,1024]{1,0:T(8,128)(2,1)S(1)} %get-tuple-element.44.powers_b) | copy-start | bytes 6291460
  28.5 14.1 %collective-permute-start.2 = (f32[4,1024]{1,0:T(4,128)S(1)}, f32[4,1024]{1,0:T(4,128)S(1)}, u32[]{:S(2)}, u32[]{:S(2)}) collective-permute-start(f32[4,1024]{1,0:T(4,128)S(1)} %get-tuple-element.30.own), channel_id=1, source_target_pairs={{0,511},{1,0},{2,1},{3,2},{4,3},{5,4},{6,5},{7,6},{8,7},{9,8},{10,... | collective-permute-start | bytes 49160 | tf_op jit(solution)/shard_map/ppermute | solution.py:24
  38.1 4.4 %collective-permute-start.3 = (f32[2,1024]{1,0:T(2,128)S(1)}, f32[2,1024]{1,0:T(2,128)S(1)}, u32[]{:S(2)}, u32[]{:S(2)}) collective-permute-start(f32[2,1024]{1,0:T(2,128)S(1)} %get-tuple-element.31.onward), channel_id=1, source_target_pairs={{0,1},{1,2},{2,3},{3,4},{4,5},{5,6},{6,7},{7,8},{8,9},{9,10},{10,1... | collective-permute-start | bytes 24584 | tf_op jit(solution)/shard_map/ppermute | solution.py:24
  40.8 0.8 %copy-start.2 = (f32[128,1024]{1,0:T(8,128)}, f32[128,1024]{1,0:T(8,128)S(1)}, u32[]{:S(2)}) copy-start(f32[128,1024]{1,0:T(8,128)S(1)} %get-tuple-element.46.mixed_far_a) | copy-start | bytes 1572868
  44.8 24.3 %collective-permute-start.5 = (s16[144,1024]{1,0:T(8,128)(2,1)}, s16[144,1024]{1,0:T(8,128)(2,1)S(1)}, u32[]{:S(2)}, u32[]{:S(2)}) collective-permute-start(s16[144,1024]{1,0:T(8,128)(2,1)} %get-tuple-element.50), channel_id=1, source_target_pairs={{0,1},{1,2},{2,3},{3,4},{4,5},{5,6},{6,7},{7,8},{8,9},{9,10},{10,1... | collective-permute-start | bytes 884744 | tf_op jit(solution)/shard_map/ppermute | solution.py:24
  47.2 21.8 %collective-permute-start.4 = (s16[1040,128]{1,0:T(8,128)(2,1)}, s16[1040,128]{1,0:T(8,128)(2,1)}, u32[]{:S(2)}, u32[]{:S(2)}) collective-permute-start(s16[1040,128]{1,0:T(8,128)(2,1)} %get-tuple-element.49), channel_id=1, source_target_pairs={{0,510},{1,511},{2,0},{3,1},{4,2},{5,3},{6,4},{7,5},{8,6},{9,7},{1... | collective-permute-start | bytes 798728 | tf_op jit(solution)/shard_map/ppermute | solution.py:24
  65.0 1.6 %copy-start.1 = (bf16[1024,1024]{1,0:T(8,128)(2,1)S(1)}, bf16[1024,1024]{1,0:T(8,128)(2,1)}, u32[]{:S(2)}) copy-start(bf16[1024,1024]{1,0:T(8,128)(2,1)} %copy-done) | copy-start | bytes 6291460
  66.6 1.0 %copy-start.3 = (f32[128,1024]{1,0:T(8,128)S(1)}, f32[128,1024]{1,0:T(8,128)}, u32[]{:S(2)}) copy-start(f32[128,1024]{1,0:T(8,128)} %copy-done.2) | copy-start | bytes 1572868

commit v2 on v1

v2 whole, which is shorter than its diff:
```python
import functools
import math

import jax
import jax.numpy as jnp
from jax import lax
from jax.experimental import pallas as pl
from jax.experimental.pallas import tpu as pltpu
from jax.sharding import PartitionSpec as P


tau_scale = 0.1
EXPONENT = math.log2(math.e) / tau_scale
CHUNK = 256
PAD = 16
MIB = 1024 * 1024

VMEM = pl.BlockSpec(memory_space=pltpu.VMEM)
ANY = pl.BlockSpec(memory_space=pl.ANY)


def passed_along(value, axis, steps):
    count = lax.axis_size(axis)
    pairs = [(source, (source + steps) % count) for source in range(count)]
    return lax.ppermute(value, axis, pairs)


def swapped(value, axis, first):
    count = lax.axis_size(axis)
    pairs = [(source, (source + (1 if source % 2 == first else -1)) % count) for source in range(count)]
    return lax.ppermute(value, axis, pairs)


def on_core(body, outs, args, flops, name, limit=8, specs=None, scratch=()):
    return pl.pallas_call(
        body,
        out_shape=[pltpu.VMEM(shape, dtype) for shape, dtype in outs],
        in_specs=specs or [VMEM] * len(args),
        out_specs=[VMEM] * len(outs),
        scratch_shapes=list(scratch),
        compiler_params=pltpu.CompilerParams(vmem_limit_bytes=limit * MIB),
        cost_estimate=pl.CostEstimate(flops=flops, bytes_accessed=2 * MIB, transcendentals=0),
        name=name,
    )(*args)


def rows_dot(a, b):
    return lax.dot_general(a, b, (((1,), (1,)), ((), ())), preferred_element_type=jnp.float32)


def token_powers(page, query, powers_ref, total_ref, smooth_ref, row):
    rows = query.shape[0]
    for start in range(0, rows, CHUNK):
        cut = slice(start, start + CHUNK)
        products = rows_dot(page[...], query[cut, :])
        largest = jnp.max(products, axis=0, keepdims=True)
        powers = jnp.exp2((products - largest) * EXPONENT)
        total = jnp.sum(powers, axis=0, keepdims=True)
        powers_ref[:, cut] = powers.astype(jnp.bfloat16)
        total_ref[row : row + 1, cut] = total
        smooth_ref[row : row + 1, cut] = largest + tau_scale * jnp.log(total)


def mix_pages(page_t, powers_ref, mixed_ref):
    rows = powers_ref.shape[1]
    for start in range(0, rows, CHUNK):
        cut = slice(start, start + CHUNK)
        mixed_ref[:, cut] = jnp.dot(page_t, powers_ref[:, cut], preferred_element_type=jnp.float32)


def turned(value):
    return value.astype(jnp.float32).T.astype(jnp.bfloat16)


def of_token(shape, token_axis, tokens):
    token = lax.broadcasted_iota(jnp.int32, shape, token_axis)
    query = lax.broadcasted_iota(jnp.int32, shape, 1 - token_axis)
    return token, query


def own_body(tokens, page_hbm, query_hbm, positive_hbm, powers_ref, mixed_ref, total_ref, smooth_ref,
             query_t_ref, query_ref, positive_ref, page, positives, sems):
    page_copy = pltpu.make_async_copy(page_hbm, page, sems.at[0])
    query_copy = pltpu.make_async_copy(query_hbm, query_ref, sems.at[1])
    positive_copy = pltpu.make_async_copy(positive_hbm, positives, sems.at[2])
    page_copy.start()
    query_copy.start()
    positive_copy.start()
    positive_copy.wait()
    token, query = of_token((positives.shape[1], query_ref.shape[0]), 1, tokens)
    inside = (token >= query * tokens) & (token < query * tokens + tokens)
    positive_ref[...] = jnp.sum(jnp.where(inside, positives[...].astype(jnp.float32).T, 0.0), axis=0, keepdims=True)
    page_copy.wait()
    query_copy.wait()
    token_powers(page, query_ref, powers_ref, total_ref, smooth_ref, 0)
    mix_pages(turned(page[...]), powers_ref, mixed_ref)
    query_t_ref[...] = turned(query_ref[...])


def far_body(page, query, powers_ref, total_ref, smooth_ref):
    token_powers(page, query, powers_ref, total_ref, smooth_ref, 0)


def query_sums(value, tokens):
    lane = lax.broadcasted_iota(jnp.int32, value.shape, 1)
    width = value.shape[1]
    step = tokens // 2
    while step:
        ahead = pltpu.roll(value, width - step, 1)
        behind = pltpu.roll(value, step, 1)
        value = value + jnp.where((lane & step) != 0, behind, ahead)
        step //= 2
    return value


def pair_body(tokens, page, far_page, next_query, smooth_a, smooth_c, positive,
              powers_b_ref, powers_d_ref, total_ref, scores_ref, near_ref, far_ref, next_query_t_ref, smooth_ref):
    token_powers(page, next_query, powers_b_ref, total_ref, smooth_ref, 0)
    token_powers(far_page, next_query, powers_d_ref, total_ref, smooth_ref, 1)
    rows = jnp.concatenate([smooth_a[...], smooth_c[...], smooth_ref[...]], axis=0)
    sums = query_sums(rows, tokens)
    scores_ref[...] = sums
    own = jnp.concatenate([sums[0:2, :], positive[...], positive[...]], axis=0)
    onward = jnp.concatenate([sums[2:4, :], sums[2:4, :]], axis=0)
    even = lax.axis_index("dp") % 2 == 0
    near_ref[...] = jnp.where(even, onward, own)
    far_ref[0:4, :] = jnp.where(even, own, onward)
    far_ref[4:8, :] = sums
    next_query_t_ref[...] = turned(next_query[...])


def mix_body(page, far_page, powers_b, powers_c, powers_d, mixed_b_ref, mixed_c_ref, mixed_d_ref):
    mix_pages(turned(page[...]), powers_b, mixed_b_ref)
    far_page_t = turned(far_page[...])
    mix_pages(far_page_t, powers_c, mixed_c_ref)
    mix_pages(far_page_t, powers_d, mixed_d_ref)


def slopes_of(scores, positive):
    flags = [(positive == float(offset)).astype(jnp.float32) for offset in range(4)]
    positive_score = sum(flag * score for flag, score in zip(flags, scores))
    margins = [score - positive_score for score in scores]
    loss = sum((1.0 - flag) * jax.nn.softplus(margin) for flag, margin in zip(flags, margins))
    terms = [(1.0 - flag) * jax.nn.sigmoid(margin) for flag, margin in zip(flags, margins)]
    total = sum(terms)
    return loss, [term - flag * total for flag, term in zip(flags, terms)]


def to_short(value):
    largest = jnp.maximum(jnp.max(jnp.abs(value), axis=0, keepdims=True), 1e-38)
    power = jnp.minimum(jnp.floor(math.log2(32000.0) - jnp.log2(largest)), 126.0)
    short = jnp.round(value * jnp.exp2(power)).astype(jnp.int32).astype(jnp.int16)
    tail = jnp.broadcast_to(power, (PAD, value.shape[1])).astype(jnp.int32).astype(jnp.int16)
    return short, tail


def from_short(ref, rows):
    power = ref[rows : rows + PAD, :].astype(jnp.int32).astype(jnp.float32)[0:1, :]
    return ref[0:rows, :].astype(jnp.int32).astype(jnp.float32) * jnp.exp2(-power)


def scaled(query_t, weight):
    return (query_t.astype(jnp.float32) * weight).astype(jnp.bfloat16)


def send_page_body(tokens, far, near, scores, positive, total_a, total_c, total_next, query_t, next_query_t,
                   powers_a, powers_b, page_out_ref, loss_ref, weight_ref):
    even = lax.axis_index("dp") % 2 == 0
    from_last = jnp.where(even, far[0:4, :], near[...])
    from_next = jnp.where(even, near[...], far[0:4, :])
    loss, slopes = slopes_of([scores[0:1, :], from_last[0:1, :], scores[1:2, :], from_last[1:2, :]], positive[...])
    _, next_slopes = slopes_of([from_next[0:1, :], scores[2:3, :], from_next[1:2, :], scores[3:4, :]], from_next[2:3, :])
    loss_ref[...] = loss
    weight_far_a = slopes[2] / total_c[...]
    weight_far_b = next_slopes[3] / total_next[1:2, :]
    weight_ref[0:1, :] = slopes[0] / total_a[...]
    weight_ref[1:2, :] = next_slopes[1] / total_next[0:1, :]
    weight_ref[2:3, :] = weight_far_a
    weight_ref[3:4, :] = weight_far_b
    page_term = rows_dot(powers_a[...], scaled(query_t[...], weight_far_a))
    page_term = page_term + rows_dot(powers_b[...], scaled(next_query_t[...], weight_far_b))
    count = page_term.shape[0]
    short, tail = to_short(page_term)
    page_out_ref[0:count, :] = short
    page_out_ref[count : count + PAD, :] = tail
    page_out_ref[count + PAD : count + 2 * PAD, :] = tail


def send_query_body(tokens, weight, mixed_own_b, mixed_far_b, loss_all, query_out_ref, loss_ref):
    query_term = (mixed_own_b[...] * weight[1:2, :] + mixed_far_b[...] * weight[3:4, :]).T
    count = query_term.shape[0]
    short, tail = to_short(query_term)
    query_out_ref[0:count, :] = short
    query_out_ref[count : count + PAD, :] = tail
    token, query = of_token((loss_ref.shape[1], loss_all.shape[1]), 1, tokens)
    loss_ref[...] = jnp.sum(jnp.where(token == query * tokens, loss_all[...], 0.0), axis=1, keepdims=True).T


def keep_body(weight, query_t, next_query_t, powers_a, powers_b, mixed_own_a, mixed_far_a,
              page_ref, query_ref):
    page_term = rows_dot(powers_a[...], scaled(query_t[...], weight[0:1, :]))
    page_ref[...] = page_term + rows_dot(powers_b[...], scaled(next_query_t[...], weight[1:2, :]))
    query_ref[...] = (mixed_own_a[...] * weight[0:1, :] + mixed_far_a[...] * weight[2:3, :]).T


def sum_body(own, arrived, sum_ref):
    sum_ref[...] = own[...] + from_short(arrived, own.shape[0])


def finish(body, shape, args, name):
    return pl.pallas_call(
        body,
        out_shape=jax.ShapeDtypeStruct(shape, jnp.float32),
        in_specs=[VMEM] * len(args),
        out_specs=VMEM,
        compiler_params=pltpu.CompilerParams(vmem_limit_bytes=4 * MIB),
        cost_estimate=pl.CostEstimate(flops=1000, bytes_accessed=1000, transcendentals=0),
        name=name,
    )(*args)


def in_hbm(value):
    return pltpu.with_memory_space_constraint(value, pltpu.HBM)


def on_device(queries, positives, pages):
    count, tokens, width = queries.shape
    page = pages[0]
    patches = page.shape[0]
    query = queries.reshape(count * tokens, width)
    rows = count * tokens
    f32, bf16, i16 = jnp.float32, jnp.bfloat16, jnp.int16
    unit = 2 * rows * patches * width

    far_page = passed_along(page, "dp", 2)
    next_query = passed_along(query, "dp", -1)

    powers_a, mixed_a, total_a, smooth_a, query_t, own_query, positive, own_page = on_core(
        functools.partial(own_body, tokens),
        [((patches, rows), bf16), ((width, rows), f32), ((1, rows), f32), ((1, rows), f32), ((width, rows), bf16),
         ((rows, width), bf16), ((1, rows), f32), ((patches, width), bf16)],
        tuple(in_hbm(value) for value in (page, query, positives[None])), 2 * unit, "own_unit", specs=[ANY] * 3,
        scratch=[pltpu.VMEM((1, count), jnp.int32), pltpu.SemaphoreType.DMA((3,))])
    powers_c, total_c, smooth_c = on_core(
        far_body, [((patches, rows), bf16), ((1, rows), f32), ((1, rows), f32)], (far_page, own_query), unit, "far_unit")
    powers_b, powers_d, total_next, scores, near, far, next_query_t = on_core(
        functools.partial(pair_body, tokens),
        [((patches, rows), bf16), ((patches, rows), bf16), ((2, rows), f32), ((4, rows), f32), ((4, rows), f32), ((8, rows), f32),
         ((width, rows), bf16)],
        (own_page, far_page, next_query, smooth_a, smooth_c, positive), 2 * unit, "next_units",
        scratch=[pltpu.VMEM((2, rows), f32)])
    far = swapped(far, "dp", 1)
    near = swapped(near, "dp", 0)
    mixed_b, mixed_c, mixed_d = on_core(
        mix_body, [((width, rows), f32)] * 3, (own_page, far_page, powers_b, powers_c, powers_d), 3 * unit, "mixes")
    page_out, loss_all, weight = on_core(
        functools.partial(send_page_body, tokens),
        [((patches + 2 * PAD, width), i16), ((1, rows), f32), ((4, rows), f32)],
        (far, near, scores, positive, total_a, total_c, total_next, query_t, next_query_t,
         powers_c, powers_d), 2 * unit, "send_page")
    page_in = passed_along(page_out, "dp", -2)
    query_out, loss = on_core(
        functools.partial(send_query_body, tokens),
        [((rows + PAD, width), i16), ((1, count), f32)],
        (weight, mixed_b, mixed_d, loss_all), unit, "send_query")
    query_in = passed_along(query_out, "dp", 1)
    page_own, query_own = on_core(
        keep_body, [((patches, width), f32), ((rows, width), f32)],
        (weight, query_t, next_query_t, powers_a, powers_b, mixed_a, mixed_c), 2 * unit, "own_terms")
    query_grad = finish(sum_body, (rows, width), (query_own, query_in), "query_sum")
    page_own, query_grad = lax.optimization_barrier((page_own, query_grad))
    page_grad = finish(sum_body, (patches, width), (page_own, page_in), "page_sum")
    return (loss[0], query_grad.reshape(count, tokens, width), page_grad[None])


def solution(mesh):
    in_specs = (P("dp", None, None), P("dp"), P("dp", None, None))
    out_specs = (P("dp"), P("dp", None, None), P("dp", None, None))
    return jax.shard_map(
        on_device, mesh=mesh, in_specs=in_specs, out_specs=out_specs, check_vma=False
    )
```

time: 71.7 us -> 55.6 us (0.78)
  starting transfers between devices: 40.7 us -> 29.7 us
  local copies, waits for them, and re-layouts: 7.99 us -> 0.51 us
  waiting for transfers between devices: 4.45 us -> 10.6 us
  Pallas kernels: 16 us -> 13.8 us
  other arithmetic: 1.32 us -> 0 us
    ppermute x6 -> x4, starting transfers between devices: 40.7 us -> 19.9 us  [passed_along(): return lax.ppermute(value, axis, pairs)]
    ppermute x0 -> x2, starting transfers between devices: none -> 9.78 us  [swapped(): return lax.ppermute(value, axis, pairs)]
    unnamed x15 -> x1, local copies, waits for them, and re-layouts: 7.25 us -> 0.51 us
    ppermute x6 -> x4, waiting for transfers between devices: 4.45 us -> 10.6 us  [passed_along(): return lax.ppermute(value, axis, pairs)]
    pallas_call x6 -> x7, Pallas kernels: 13.8 us -> 12.1 us  [on_core(): pl.pallas_call(body, out_shape=[pltpu.VMEM(shape, dtype) for shape, dtype...]
    pallas_call x1 -> x2, Pallas kernels: 2.17 us -> 1.73 us  [finish(): pl.pallas_call(body, out_shape=jax.ShapeDtypeStruct(shape, jnp.float32),...]
  transfers between devices with their start and end apart: 6 -> 6, of which waited for: 2 -> 2; matrix products, arithmetic and copies ran while one was open for 4% -> 1% of each run, Pallas kernels for 10% -> 15%
where the time goes in v2:
time: 55.6 us; the launch traced here: 55.3 us
  starting transfers between devices  29.7 us (53%)
  Pallas kernels  13.8 us (25%)
  waiting for transfers between devices  10.6 us (19%)
  between operations  0.75 us (1%)
    ppermute x4, starting transfers between devices, passed_along(): return lax.ppermute(value, axis, pairs)  19.9 us
    pallas_call x7, Pallas kernels, on_core(): pl.pallas_call(body, out_shape=[pltpu.VMEM(shape, dtype) for shape, dtype...  12.1 us
    ppermute x4, waiting for transfers between devices, passed_along(): return lax.ppermute(value, axis, pairs)  10.6 us
    ppermute x2, starting transfers between devices, swapped(): return lax.ppermute(value, axis, pairs)  9.78 us
    pallas_call x2, Pallas kernels, finish(): pl.pallas_call(body, out_shape=jax.ShapeDtypeStruct(shape, jnp.float32),...  1.73 us
  transfers between devices with their start and end apart: 6, of which 2 were waited for; matrix products, arithmetic and copies ran while one was open for 1% of the time, Pallas kernels for 15%

profile of v2, /device:TPU:1, one launch (start us, length us, event | category | flops | bytes accessed | tf_op | source)
XLA Modules:
  0.0 55.3 jit_solution(7590175460994112074)
XLA Ops:
  0.6 4.0 %collective-permute-start = (bf16[1024,128]{1,0:T(8,128)(2,1)}, bf16[1024,128]{1,0:T(8,128)(2,1)S(1)}, u32[]{:S(2)}, u32[]{:S(2)}) collective-permute-start(bf16[1024,128]{1,0:T(8,128)(2,1)} %bitcast.9), channel_id=1, source_target_pairs={{0,2},{1,3},{2,4},{3,5},{4,6},{5,7},{6,8},{7,9},{8,10},{9,11},{10,... | collective-permute-start | bytes 786440 | tf_op jit(solution)/shard_map/ppermute | solution.py:25
  4.7 6.7 %collective-permute-start.1 = (bf16[1024,128]{1,0:T(8,128)(2,1)}, bf16[1024,128]{1,0:T(8,128)(2,1)S(1)}, u32[]{:S(2)}, u32[]{:S(2)}) collective-permute-start(bf16[1024,128]{1,0:T(8,128)(2,1)} %bitcast.11), channel_id=1, source_target_pairs={{0,511},{1,0},{2,1},{3,2},{4,3},{5,4},{6,5},{7,6},{8,7},{9,8},{10,... | collective-permute-start | bytes 786440 | tf_op jit(solution)/shard_map/ppermute | solution.py:25
  11.4 3.1 %own_unit.1 = (bf16[1024,1024]{1,0:T(8,128)(2,1)S(1)}, f32[128,1024]{1,0:T(8,128)S(1)}, f32[1,1024]{1,0:T(1,128)S(1)}, f32[1,1024]{1,0:T(1,128)S(1)}, bf16[128,1...) custom-call(bf16[1024,128]{1,0:T(8,128)(2,1)} %bitcast.10, ...), custom_call_target="tpu_custom_call" | custom-call | flops 536870912 | bytes 2097152 | tf_op jit(solution)/shard_map/own_unit/pallas_call | solution.py:35
  14.4 9.0 %collective-permute-done.page.far_page = bf16[1024,128]{1,0:T(8,128)(2,1)S(1)} collective-permute-done((bf16[1024,128]{1,0:T(8,128)(2,1)}, bf16[1024,128]{1,0:T(8,128)(2,1)S(1)}, u32[]{:S(2)}, u32[]{:S(2)}) %collective-permute-start) | collective-permute-done | bytes 262176 | tf_op jit(solution)/shard_map/ppermute | solution.py:25
  23.5 1.5 %far_unit.1 = (bf16[1024,1024]{1,0:T(8,128)(2,1)S(1)}, f32[1,1024]{1,0:T(1,128)S(1)}, f32[1,1024]{1,0:T(1,128)S(1)}) custom-call(bf16[1024,128]{1,0:T(8,128)(2,1)S(1)} %collective-permute-done.page.far_page, bf16[1024,128]{1,0:T(8,128)(2,1)S(1)} %get-tuple-element.35.query), custom_call_target="tpu_custom_call" | custom-call | flops 268435456 | bytes 2097152 | tf_op jit(solution)/shard_map/far_unit/pallas_call | solution.py:35
  25.0 0.0 collective-permute-done.1.next_query
  25.0 3.4 %next_units.1 = (bf16[1024,1024]{1,0:T(8,128)(2,1)S(1)}, bf16[1024,1024]{1,0:T(8,128)(2,1)S(1)}, f32[2,1024]{1,0:T(2,128)S(1)}, f32[4,1024]{1,0:T(4,128)S(1)}, f...) custom-call(bf16[1024,128]{1,0:T(8,128)(2,1)S(1)} %get-tuple-element.33.page, ...), custom_call_target="tpu_custom_call" | custom-call | flops 536870912 | bytes 2097152 | tf_op jit(solution)/shard_map/next_units/pallas_call | solution.py:35
  28.4 1.9 %collective-permute-start.2 = (f32[8,1024]{1,0:T(8,128)S(1)}, f32[8,1024]{1,0:T(8,128)S(1)}, u32[]{:S(2)}, u32[]{:S(2)}) collective-permute-start(f32[8,1024]{1,0:T(8,128)S(1)} %get-tuple-element.38), channel_id=1, source_target_pairs={{0,511},{1,2},{2,1},{3,4},{4,3},{5,6},{6,5},{7,8},{8,7},{9,10},{10... | collective-permute-start | bytes 98312 | tf_op jit(solution)/shard_map/ppermute | solution.py:31
  30.4 7.9 %collective-permute-start.3 = (f32[4,1024]{1,0:T(4,128)S(1)}, f32[4,1024]{1,0:T(4,128)S(1)}, u32[]{:S(2)}, u32[]{:S(2)}) collective-permute-start(f32[4,1024]{1,0:T(4,128)S(1)} %get-tuple-element.39), channel_id=1, source_target_pairs={{0,1},{1,0},{2,3},{3,2},{4,5},{5,4},{6,7},{7,6},{8,9},{9,8},{10,11... | collective-permute-start | bytes 49160 | tf_op jit(solution)/shard_map/ppermute | solution.py:31
  38.2 1.0 %mixes.1 = (f32[128,1024]{1,0:T(8,128)S(1)}, f32[128,1024]{1,0:T(8,128)S(1)}, f32[128,1024]{1,0:T(8,128)S(1)}) custom-call(bf16[1024,128]{1,0:T(8,128)(2,1)S(1)} %get-tuple-element.33.page, bf16[1024,128]{1,0:T(8,128)(2,1)S(1)} %collective-permute-done.page.far_page, bf16[1024,1024]{1,0:T(8,128)(2,1)S(1)} %get-tuple-element.49.powers_b, ...), custom_call_target="tpu_custom_call" | custom-call | flops 805306368 | bytes 2097152 | tf_op jit(solution)/shard_map/mixes/pallas_call | solution.py:35
  39.3 0.0 collective-permute-done.3.near
  39.3 0.0 collective-permute-done.2.far
  39.3 1.4 %send_page.1 = (s16[1056,128]{1,0:T(8,128)(2,1)S(1)}, f32[1,1024]{1,0:T(1,128)S(1)}, f32[4,1024]{1,0:T(4,128)S(1)}) custom-call(f32[8,1024]{1,0:T(8,128)S(1)} %collective-permute-done.2.far, f32[4,1024]{1,0:T(4,128)S(1)} %collective-permute-done.3.near, f32[4,1024]{1,0:T(4,128)S(1)} %get-tuple-element.40.scores, f32[1,1024]{1,0:T(1,128)S(1)} %get-tuple-element.37.positive, ...), custom_call_target="tpu_custom_call" | custom-call | flops 536870912 | bytes 2097152 | tf_op jit(solution)/shard_map/send_page/pallas_call | solution.py:35
  40.7 7.3 %collective-permute-start.5 = (s16[1056,128]{1,0:T(8,128)(2,1)S(1)}, s16[1056,128]{1,0:T(8,128)(2,1)S(1)}, u32[]{:S(2)}, u32[]{:S(2)}) collective-permute-start(s16[1056,128]{1,0:T(8,128)(2,1)S(1)} %get-tuple-element.62), channel_id=1, source_target_pairs={{0,510},{1,511},{2,0},{3,1},{4,2},{5,3},{6,4},{7,5},{8,6},{9,7},{1... | collective-permute-start | bytes 811016 | tf_op jit(solution)/shard_map/ppermute | solution.py:25
  48.0 0.3 send_query.1
  48.3 1.9 %collective-permute-start.4 = (s16[1040,128]{1,0:T(8,128)(2,1)S(1)}, s16[1040,128]{1,0:T(8,128)(2,1)S(1)}, u32[]{:S(2)}, u32[]{:S(2)}) collective-permute-start(s16[1040,128]{1,0:T(8,128)(2,1)S(1)} %get-tuple-element.59), channel_id=1, source_target_pairs={{0,1},{1,2},{2,3},{3,4},{4,5},{5,6},{6,7},{7,8},{8,9},{9,10},{10,1... | collective-permute-start | bytes 798728 | tf_op jit(solution)/shard_map/ppermute | solution.py:25
  50.3 0.5 copy.6
  50.8 1.3 %own_terms.1 = (f32[1024,128]{1,0:T(8,128)S(1)}, f32[1024,128]{1,0:T(8,128)S(1)}) custom-call(f32[4,1024]{1,0:T(4,128)S(1)} %get-tuple-element.48.weight, bf16[128,1024]{1,0:T(8,128)(2,1)S(1)} %get-tuple-element.44.query_t, bf16[128,1024]{1,0:T(8,128)(2,1)S(1)} %get-tuple-element.45.next_query_t, bf16[1024,1024]{1,0:T(8,128)(2,1)S(1)} %get-tuple-element.54.powers_a, ...), custom_call_target="tpu_custom_call" | custom-call | flops 536870912 | bytes 2097152 | tf_op jit(solution)/shard_map/own_terms/pallas_call | solution.py:35
  52.0 1.5 %collective-permute-done.4.arrived = s16[1040,128]{1,0:T(8,128)(2,1)S(1)} collective-permute-done((s16[1040,128]{1,0:T(8,128)(2,1)S(1)}, s16[1040,128]{1,0:T(8,128)(2,1)S(1)}, u32[]{:S(2)}, u32[]{:S(2)}) %collective-permute-start.4) | collective-permute-done | bytes 266272 | tf_op jit(solution)/shard_map/ppermute | solution.py:25
  53.6 0.9 %query_sum.1 = f32[1024,128]{1,0:T(8,128)} custom-call(f32[1024,128]{1,0:T(8,128)S(1)} %get-tuple-element.58.own, s16[1040,128]{1,0:T(8,128)(2,1)S(1)} %collective-permute-done.4.arrived), custom_call_target="tpu_custom_call" | custom-call | flops 1000 | bytes 1000 | tf_op jit(solution)/shard_map/query_sum/pallas_call | solution.py:211
  54.5 0.0 collective-permute-done.5.arrived
  54.5 0.9 %page_sum.1 = f32[1024,128]{1,0:T(8,128)} custom-call(f32[1024,128]{1,0:T(8,128)S(1)} %get-tuple-element.61.own, s16[1056,128]{1,0:T(8,128)(2,1)S(1)} %collective-permute-done.5.arrived), custom_call_target="tpu_custom_call" | custom-call | flops 1000 | bytes 1000 | tf_op jit(solution)/shard_map/page_sum/pallas_call | solution.py:211
Async XLA Ops:
  0.6 22.8 %collective-permute-start = (bf16[1024,128]{1,0:T(8,128)(2,1)}, bf16[1024,128]{1,0:T(8,128)(2,1)S(1)}, u32[]{:S(2)}, u32[]{:S(2)}) collective-permute-start(bf16[1024,128]{1,0:T(8,128)(2,1)} %bitcast.9), channel_id=1, source_target_pairs={{0,2},{1,3},{2,4},{3,5},{4,6},{5,7},{6,8},{7,9},{8,10},{9,11},{10,... | collective-permute-start | bytes 786440 | tf_op jit(solution)/shard_map/ppermute | solution.py:25
  4.7 20.3 %collective-permute-start.1 = (bf16[1024,128]{1,0:T(8,128)(2,1)}, bf16[1024,128]{1,0:T(8,128)(2,1)S(1)}, u32[]{:S(2)}, u32[]{:S(2)}) collective-permute-start(bf16[1024,128]{1,0:T(8,128)(2,1)} %bitcast.11), channel_id=1, source_target_pairs={{0,511},{1,0},{2,1},{3,2},{4,3},{5,4},{6,5},{7,6},{8,7},{9,8},{10,... | collective-permute-start | bytes 786440 | tf_op jit(solution)/shard_map/ppermute | solution.py:25
  28.4 10.8 %collective-permute-start.2 = (f32[8,1024]{1,0:T(8,128)S(1)}, f32[8,1024]{1,0:T(8,128)S(1)}, u32[]{:S(2)}, u32[]{:S(2)}) collective-permute-start(f32[8,1024]{1,0:T(8,128)S(1)} %get-tuple-element.38), channel_id=1, source_target_pairs={{0,511},{1,2},{2,1},{3,4},{4,3},{5,6},{6,5},{7,8},{8,7},{9,10},{10... | collective-permute-start | bytes 98312 | tf_op jit(solution)/shard_map/ppermute | solution.py:31
  30.4 8.9 %collective-permute-start.3 = (f32[4,1024]{1,0:T(4,128)S(1)}, f32[4,1024]{1,0:T(4,128)S(1)}, u32[]{:S(2)}, u32[]{:S(2)}) collective-permute-start(f32[4,1024]{1,0:T(4,128)S(1)} %get-tuple-element.39), channel_id=1, source_target_pairs={{0,1},{1,0},{2,3},{3,2},{4,5},{5,4},{6,7},{7,6},{8,9},{9,8},{10,11... | collective-permute-start | bytes 49160 | tf_op jit(solution)/shard_map/ppermute | solution.py:31
  40.7 13.7 %collective-permute-start.5 = (s16[1056,128]{1,0:T(8,128)(2,1)S(1)}, s16[1056,128]{1,0:T(8,128)(2,1)S(1)}, u32[]{:S(2)}, u32[]{:S(2)}) collective-permute-start(s16[1056,128]{1,0:T(8,128)(2,1)S(1)} %get-tuple-element.62), channel_id=1, source_target_pairs={{0,510},{1,511},{2,0},{3,1},{4,2},{5,3},{6,4},{7,5},{8,6},{9,7},{1... | collective-permute-start | bytes 811016 | tf_op jit(solution)/shard_map/ppermute | solution.py:25
  48.3 5.3 %collective-permute-start.4 = (s16[1040,128]{1,0:T(8,128)(2,1)S(1)}, s16[1040,128]{1,0:T(8,128)(2,1)S(1)}, u32[]{:S(2)}, u32[]{:S(2)}) collective-permute-start(s16[1040,128]{1,0:T(8,128)(2,1)S(1)} %get-tuple-element.59), channel_id=1, source_target_pairs={{0,1},{1,2},{2,3},{3,4},{4,5},{5,6},{6,7},{7,8},{8,9},{9,10},{10,1... | collective-permute-start | bytes 798728 | tf_op jit(solution)/shard_map/ppermute | solution.py:25

commit v3 on v2

--- a/solution.py
+++ b/solution.py
@@ -25,10 +25,14 @@
     return lax.ppermute(value, axis, pairs)
 
 
-def swapped(value, axis, first):
+def odd_passed_along(value, axis, steps):
     count = lax.axis_size(axis)
-    pairs = [(source, (source + (1 if source % 2 == first else -1)) % count) for source in range(count)]
+    pairs = [(source, (source + steps) % count if source % 2 else source) for source in range(count)]
     return lax.ppermute(value, axis, pairs)
+
+
+def swapped(value, axis):
+    return lax.ppermute(value, axis, [(source, source ^ 1) for source in range(lax.axis_size(axis))])
 
 
 def on_core(body, outs, args, flops, name, limit=8, specs=None, scratch=()):
@@ -113,24 +117,20 @@
     return value
 
 
-def pair_body(tokens, page, far_page, next_query, smooth_a, smooth_c, positive,
-              powers_b_ref, powers_d_ref, total_ref, scores_ref, near_ref, far_ref, next_query_t_ref, smooth_ref):
-    token_powers(page, next_query, powers_b_ref, total_ref, smooth_ref, 0)
-    token_powers(far_page, next_query, powers_d_ref, total_ref, smooth_ref, 1)
-    rows = jnp.concatenate([smooth_a[...], smooth_c[...], smooth_ref[...]], axis=0)
-    sums = query_sums(rows, tokens)
-    scores_ref[...] = sums
-    own = jnp.concatenate([sums[0:2, :], positive[...], positive[...]], axis=0)
-    onward = jnp.concatenate([sums[2:4, :], sums[2:4, :]], axis=0)
-    even = lax.axis_index("dp") % 2 == 0
-    near_ref[...] = jnp.where(even, onward, own)
-    far_ref[0:4, :] = jnp.where(even, own, onward)
-    far_ref[4:8, :] = sums
-    next_query_t_ref[...] = turned(next_query[...])
-
-
-def mix_body(page, far_page, powers_b, powers_c, powers_d, mixed_b_ref, mixed_c_ref, mixed_d_ref):
-    mix_pages(turned(page[...]), powers_b, mixed_b_ref)
+def mate_body(tokens, far_page, last_page, mate_query, smooth_a, smooth_c, positive,
+              powers_d_ref, powers_b_ref, total_ref, message_ref, smooth_ref):
+    token_powers(far_page, mate_query, powers_d_ref, total_ref, smooth_ref, 0)
+    token_powers(last_page, mate_query, powers_b_ref, total_ref, smooth_ref, 1)
+    sums = query_sums(jnp.concatenate([smooth_a[...], smooth_c[...], smooth_ref[...]], axis=0), tokens)
+    message_ref[0:4, :] = sums
+    message_ref[4:5, :] = positive[...]
+    message_ref[5:8, :] = sums[0:3, :]
+
+
+def mix_body(last_page, far_page, mate_query, powers_b, powers_c, powers_d,
+             mixed_b_ref, mixed_c_ref, mixed_d_ref, mate_query_t_ref):
+    mate_query_t_ref[...] = turned(mate_query[...])
+    mix_pages(turned(last_page[...]), powers_b, mixed_b_ref)
     far_page_t = turned(far_page[...])
     mix_pages(far_page_t, powers_c, mixed_c_ref)
     mix_pages(far_page_t, powers_d, mixed_d_ref)
@@ -163,48 +163,53 @@
     return (query_t.astype(jnp.float32) * weight).astype(jnp.bfloat16)
 
 
-def send_page_body(tokens, far, near, scores, positive, total_a, total_c, total_next, query_t, next_query_t,
-                   powers_a, powers_b, page_out_ref, loss_ref, weight_ref):
+def put_short(ref, value):
+    count = value.shape[0]
+    short, tail = to_short(value)
+    ref[0:count, :] = short
+    for start in range(count, ref.shape[0], PAD):
+        ref[start : start + PAD, :] = tail
+
+
+def send_last_body(message, arrived, total_a, total_c, total_mate, mate_query_t, powers_b,
+                   out_ref, loss_ref, weight_ref):
     even = lax.axis_index("dp") % 2 == 0
-    from_last = jnp.where(even, far[0:4, :], near[...])
-    from_next = jnp.where(even, near[...], far[0:4, :])
-    loss, slopes = slopes_of([scores[0:1, :], from_last[0:1, :], scores[1:2, :], from_last[1:2, :]], positive[...])
-    _, next_slopes = slopes_of([from_next[0:1, :], scores[2:3, :], from_next[1:2, :], scores[3:4, :]], from_next[2:3, :])
+    own = message[...]
+    mate = arrived[...]
+    loss, slopes = slopes_of(
+        [own[0:1], jnp.where(even, mate[2:3], mate[3:4]), own[1:2], jnp.where(even, mate[3:4], mate[2:3])], own[4:5])
+    _, mate_slopes = slopes_of(
+        [mate[0:1], jnp.where(even, own[3:4], own[2:3]), mate[1:2], jnp.where(even, own[2:3], own[3:4])], mate[4:5])
     loss_ref[...] = loss
-    weight_far_a = slopes[2] / total_c[...]
-    weight_far_b = next_slopes[3] / total_next[1:2, :]
+    weight_b = jnp.where(even, mate_slopes[1], mate_slopes[3]) / total_mate[1:2, :]
     weight_ref[0:1, :] = slopes[0] / total_a[...]
-    weight_ref[1:2, :] = next_slopes[1] / total_next[0:1, :]
-    weight_ref[2:3, :] = weight_far_a
-    weight_ref[3:4, :] = weight_far_b
-    page_term = rows_dot(powers_a[...], scaled(query_t[...], weight_far_a))
-    page_term = page_term + rows_dot(powers_b[...], scaled(next_query_t[...], weight_far_b))
-    count = page_term.shape[0]
-    short, tail = to_short(page_term)
-    page_out_ref[0:count, :] = short
-    page_out_ref[count : count + PAD, :] = tail
-    page_out_ref[count + PAD : count + 2 * PAD, :] = tail
-
-
-def send_query_body(tokens, weight, mixed_own_b, mixed_far_b, loss_all, query_out_ref, loss_ref):
-    query_term = (mixed_own_b[...] * weight[1:2, :] + mixed_far_b[...] * weight[3:4, :]).T
-    count = query_term.shape[0]
-    short, tail = to_short(query_term)
-    query_out_ref[0:count, :] = short
-    query_out_ref[count : count + PAD, :] = tail
+    weight_ref[1:2, :] = weight_b
+    weight_ref[2:3, :] = slopes[2] / total_c[...]
+    weight_ref[3:4, :] = jnp.where(even, mate_slopes[3], mate_slopes[1]) / total_mate[0:1, :]
+    put_short(out_ref, rows_dot(powers_b[...], scaled(mate_query_t[...], weight_b)))
+
+
+def send_far_body(weight, query_t, mate_query_t, powers_c, powers_d, out_ref):
+    page_term = rows_dot(powers_c[...], scaled(query_t[...], weight[2:3, :]))
+    put_short(out_ref, page_term + rows_dot(powers_d[...], scaled(mate_query_t[...], weight[3:4, :])))
+
+
+def send_query_body(tokens, weight, mixed_b, mixed_d, loss_all, out_ref, loss_ref):
+    put_short(out_ref, (mixed_b[...] * weight[1:2, :] + mixed_d[...] * weight[3:4, :]).T)
     token, query = of_token((loss_ref.shape[1], loss_all.shape[1]), 1, tokens)
     loss_ref[...] = jnp.sum(jnp.where(token == query * tokens, loss_all[...], 0.0), axis=1, keepdims=True).T
 
 
-def keep_body(weight, query_t, next_query_t, powers_a, powers_b, mixed_own_a, mixed_far_a,
-              page_ref, query_ref):
-    page_term = rows_dot(powers_a[...], scaled(query_t[...], weight[0:1, :]))
-    page_ref[...] = page_term + rows_dot(powers_b[...], scaled(next_query_t[...], weight[1:2, :]))
-    query_ref[...] = (mixed_own_a[...] * weight[0:1, :] + mixed_far_a[...] * weight[2:3, :]).T
-
-
-def sum_body(own, arrived, sum_ref):
-    sum_ref[...] = own[...] + from_short(arrived, own.shape[0])
+def keep_body(weight, query_t, powers_a, mixed_a, mixed_c, page_ref, query_ref):
+    page_ref[...] = rows_dot(powers_a[...], scaled(query_t[...], weight[0:1, :]))
+    query_ref[...] = (mixed_a[...] * weight[0:1, :] + mixed_c[...] * weight[2:3, :]).T
+
+
+def sum_body(own, *refs):
+    total = own[...]
+    for arrived in refs[:-1]:
+        total = total + from_short(arrived, own.shape[0])
+    refs[-1][...] = total
 
 
 def finish(body, shape, args, name):
@@ -233,43 +238,46 @@
     unit = 2 * rows * patches * width
 
     far_page = passed_along(page, "dp", 2)
-    next_query = passed_along(query, "dp", -1)
-
-    powers_a, mixed_a, total_a, smooth_a, query_t, own_query, positive, own_page = on_core(
+    last_page = odd_passed_along(page, "dp", 4)
+    mate_query = swapped(query, "dp")
+
+    powers_a, mixed_a, total_a, smooth_a, query_t, own_query, positive = on_core(
         functools.partial(own_body, tokens),
         [((patches, rows), bf16), ((width, rows), f32), ((1, rows), f32), ((1, rows), f32), ((width, rows), bf16),
-         ((rows, width), bf16), ((1, rows), f32), ((patches, width), bf16)],
+         ((rows, width), bf16), ((1, rows), f32)],
         tuple(in_hbm(value) for value in (page, query, positives[None])), 2 * unit, "own_unit", specs=[ANY] * 3,
-        scratch=[pltpu.VMEM((1, count), jnp.int32), pltpu.SemaphoreType.DMA((3,))])
+        scratch=[pltpu.VMEM((patches, width), bf16), pltpu.VMEM((1, count), jnp.int32), pltpu.SemaphoreType.DMA((3,))])
     powers_c, total_c, smooth_c = on_core(
         far_body, [((patches, rows), bf16), ((1, rows), f32), ((1, rows), f32)], (far_page, own_query), unit, "far_unit")
-    powers_b, powers_d, total_next, scores, near, far, next_query_t = on_core(
-        functools.partial(pair_body, tokens),
-        [((patches, rows), bf16), ((patches, rows), bf16), ((2, rows), f32), ((4, rows), f32), ((4, rows), f32), ((8, rows), f32),
-         ((width, rows), bf16)],
-        (own_page, far_page, next_query, smooth_a, smooth_c, positive), 2 * unit, "next_units",
+    powers_d, powers_b, total_mate, message = on_core(
+        functools.partial(mate_body, tokens),
+        [((patches, rows), bf16), ((patches, rows), bf16), ((2, rows), f32), ((8, rows), f32)],
+        (far_page, last_page, mate_query, smooth_a, smooth_c, positive), 2 * unit, "mate_units",
         scratch=[pltpu.VMEM((2, rows), f32)])
-    far = swapped(far, "dp", 1)
-    near = swapped(near, "dp", 0)
-    mixed_b, mixed_c, mixed_d = on_core(
-        mix_body, [((width, rows), f32)] * 3, (own_page, far_page, powers_b, powers_c, powers_d), 3 * unit, "mixes")
-    page_out, loss_all, weight = on_core(
-        functools.partial(send_page_body, tokens),
-        [((patches + 2 * PAD, width), i16), ((1, rows), f32), ((4, rows), f32)],
-        (far, near, scores, positive, total_a, total_c, total_next, query_t, next_query_t,
-         powers_c, powers_d), 2 * unit, "send_page")
-    page_in = passed_along(page_out, "dp", -2)
+    arrived = swapped(message, "dp")
+    mixed_b, mixed_c, mixed_d, mate_query_t = on_core(
+        mix_body, [((width, rows), f32)] * 3 + [((width, rows), bf16)],
+        (last_page, far_page, mate_query, powers_b, powers_c, powers_d), 3 * unit, "mixes")
+    last_out, loss_all, weight = on_core(
+        send_last_body,
+        [((patches + 4 * PAD, width), i16), ((1, rows), f32), ((4, rows), f32)],
+        (message, arrived, total_a, total_c, total_mate, mate_query_t, powers_b), unit, "send_last")
+    last_in = odd_passed_along(last_out, "dp", -4)
+    far_out, = on_core(
+        send_far_body, [((patches + 3 * PAD, width), i16)],
+        (weight, query_t, mate_query_t, powers_c, powers_d), 2 * unit, "send_far")
+    far_in = passed_along(far_out, "dp", -2)
     query_out, loss = on_core(
         functools.partial(send_query_body, tokens),
         [((rows + PAD, width), i16), ((1, count), f32)],
-        (weight, mixed_b, mixed_d, loss_all), unit, "send_query")
-    query_in = passed_along(query_out, "dp", 1)
+        (weight, mixed_b, mixed_d, loss_all), 1000, "send_query")
+    query_in = swapped(query_out, "dp")
     page_own, query_own = on_core(
         keep_body, [((patches, width), f32), ((rows, width), f32)],
-        (weight, query_t, next_query_t, powers_a, powers_b, mixed_a, mixed_c), 2 * unit, "own_terms")
+        (weight, query_t, powers_a, mixed_a, mixed_c), 1000, "own_terms")
     query_grad = finish(sum_body, (rows, width), (query_own, query_in), "query_sum")
     page_own, query_grad = lax.optimization_barrier((page_own, query_grad))
-    page_grad = finish(sum_body, (patches, width), (page_own, page_in), "page_sum")
+    page_grad = finish(sum_body, (patches, width), (page_own, far_in, last_in), "page_sum")
     return (loss[0], query_grad.reshape(count, tokens, width), page_grad[None])
 
 

time: 55.6 us -> 50.7 us (0.912)
  starting transfers between devices: 29.7 us -> 23.9 us
    ppermute x4 -> x2, starting transfers between devices: 19.9 us -> 5.99 us  [passed_along(): return lax.ppermute(value, axis, pairs)]
    ppermute x2 -> x5, starting transfers between devices: 9.78 us -> 17.9 us  [the longest x3 9.49 us: swapped(): lax.ppermute(value, axis, [(source, source ^ 1) for source in range(lax.a...]
    ppermute x2 -> x5, waiting for transfers between devices: 0.01 us -> 0.92 us  [the longest x2 0.65 us: odd_passed_along(): return lax.ppermute(value, axis, pairs)]
    ppermute x4 -> x2, waiting for transfers between devices: 10.6 us -> 10.1 us  [passed_along(): return lax.ppermute(value, axis, pairs)]
    pallas_call x7 -> x8, Pallas kernels: 12.1 us -> 12.4 us  [on_core(): pl.pallas_call(body, out_shape=[pltpu.VMEM(shape, dtype) for shape, dtype...]
  transfers between devices with their start and end apart: 6 -> 7, of which waited for: 2 -> 4; matrix products, arithmetic and copies ran while one was open for 1% -> 1% of each run, Pallas kernels for 15% -> 18%
where the time goes in v3:
time: 50.7 us; the launch traced here: 50.4 us
  starting transfers between devices  23.9 us (47%)
  Pallas kernels  14.2 us (28%)
  waiting for transfers between devices  11.1 us (22%)
  between operations  0.74 us (1%)
  local copies, waits for them, and re-layouts  0.51 us (1%)
    pallas_call x8, Pallas kernels, on_core(): pl.pallas_call(body, out_shape=[pltpu.VMEM(shape, dtype) for shape, dtype...  12.4 us
    ppermute x2, waiting for transfers between devices, passed_along(): return lax.ppermute(value, axis, pairs)  10.1 us
    ppermute x3, starting transfers between devices, swapped(): lax.ppermute(value, axis, [(source, source ^ 1) for source in range(lax.a...  9.49 us
    ppermute x2, starting transfers between devices, odd_passed_along(): return lax.ppermute(value, axis, pairs)  8.38 us
    ppermute x2, starting transfers between devices, passed_along(): return lax.ppermute(value, axis, pairs)  5.99 us
    pallas_call x2, Pallas kernels, finish(): pl.pallas_call(body, out_shape=jax.ShapeDtypeStruct(shape, jnp.float32),...  1.81 us
  transfers between devices with their start and end apart: 7, of which 4 were waited for; matrix products, arithmetic and copies ran while one was open for 1% of the time, Pallas kernels for 18%

profile of v3, /device:TPU:1, one launch (start us, length us, event | category | flops | bytes accessed | tf_op | source)
XLA Modules:
  0.0 50.4 jit_solution(9772971936496537484)
XLA Ops:
  0.6 4.0 %collective-permute-start = (bf16[1024,128]{1,0:T(8,128)(2,1)}, bf16[1024,128]{1,0:T(8,128)(2,1)S(1)}, u32[]{:S(2)}, u32[]{:S(2)}) collective-permute-start(bf16[1024,128]{1,0:T(8,128)(2,1)} %bitcast.9), channel_id=1, source_target_pairs={{0,2},{1,3},{2,4},{3,5},{4,6},{5,7},{6,8},{7,9},{8,10},{9,11},{10,... | collective-permute-start | bytes 786440 | tf_op jit(solution)/shard_map/ppermute | solution.py:25
  4.7 4.5 %collective-permute-start.1 = (bf16[1024,128]{1,0:T(8,128)(2,1)}, bf16[1024,128]{1,0:T(8,128)(2,1)S(1)}, u32[]{:S(2)}, u32[]{:S(2)}) collective-permute-start(bf16[1024,128]{1,0:T(8,128)(2,1)} %bitcast.10), channel_id=1, source_target_pairs={{0,0},{1,5},{2,2},{3,7},{4,4},{5,9},{6,6},{7,11},{8,8},{9,13},{10,... | collective-permute-start | bytes 786440 | tf_op jit(solution)/shard_map/ppermute | solution.py:31
  9.2 3.7 %collective-permute-start.2 = (bf16[1024,128]{1,0:T(8,128)(2,1)}, bf16[1024,128]{1,0:T(8,128)(2,1)S(1)}, u32[]{:S(2)}, u32[]{:S(2)}) collective-permute-start(bf16[1024,128]{1,0:T(8,128)(2,1)} %bitcast.12), channel_id=1, source_target_pairs={{0,1},{1,0},{2,3},{3,2},{4,5},{5,4},{6,7},{7,6},{8,9},{9,8},{10,11... | collective-permute-start | bytes 786440 | tf_op jit(solution)/shard_map/ppermute | solution.py:35
  12.9 3.0 %own_unit.1 = (bf16[1024,1024]{1,0:T(8,128)(2,1)S(1)}, f32[128,1024]{1,0:T(8,128)S(1)}, f32[1,1024]{1,0:T(1,128)S(1)}, f32[1,1024]{1,0:T(1,128)S(1)}, bf16[128,1...) custom-call(bf16[1024,128]{1,0:T(8,128)(2,1)} %bitcast.11, bf16[1024,128]{1,0:T(8,128)(2,1)} %bitcast.13, ...), custom_call_target="tpu_custom_call" | custom-call | flops 536870912 | bytes 2097152 | tf_op jit(solution)/shard_map/own_unit/pallas_call | solution.py:39
  16.0 8.6 %collective-permute-done.page.far_page = bf16[1024,128]{1,0:T(8,128)(2,1)S(1)} collective-permute-done((bf16[1024,128]{1,0:T(8,128)(2,1)}, bf16[1024,128]{1,0:T(8,128)(2,1)S(1)}, u32[]{:S(2)}, u32[]{:S(2)}) %collective-permute-start) | collective-permute-done | bytes 262176 | tf_op jit(solution)/shard_map/ppermute | solution.py:25
  24.6 1.5 %far_unit.1 = (bf16[1024,1024]{1,0:T(8,128)(2,1)S(1)}, f32[1,1024]{1,0:T(1,128)S(1)}, f32[1,1024]{1,0:T(1,128)S(1)}) custom-call(bf16[1024,128]{1,0:T(8,128)(2,1)S(1)} %collective-permute-done.page.far_page, bf16[1024,128]{1,0:T(8,128)(2,1)S(1)} %get-tuple-element.31.query), custom_call_target="tpu_custom_call" | custom-call | flops 268435456 | bytes 2097152 | tf_op jit(solution)/shard_map/far_unit/pallas_call | solution.py:39
  26.2 0.6 %collective-permute-done.1.last_page = bf16[1024,128]{1,0:T(8,128)(2,1)S(1)} collective-permute-done((bf16[1024,128]{1,0:T(8,128)(2,1)}, bf16[1024,128]{1,0:T(8,128)(2,1)S(1)}, u32[]{:S(2)}, u32[]{:S(2)}) %collective-permute-start.1) | collective-permute-done | bytes 262176 | tf_op jit(solution)/shard_map/ppermute | solution.py:31
  26.8 0.0 collective-permute-done.2.mate_query
  26.8 3.4 %mate_units.1 = (bf16[1024,1024]{1,0:T(8,128)(2,1)S(1)}, bf16[1024,1024]{1,0:T(8,128)(2,1)S(1)}, f32[2,1024]{1,0:T(2,128)S(1)}, f32[8,1024]{1,0:T(8,128)S(1)}) custom-call(bf16[1024,128]{1,0:T(8,128)(2,1)S(1)} %collective-permute-done.page.far_page, bf16[1024,128]{1,0:T(8,128)(2,1)S(1)} %collective-permute-done.1.last_page, ...), custom_call_target="tpu_custom_call" | custom-call | flops 536870912 | bytes 2097152 | tf_op jit(solution)/shard_map/mate_units/pallas_call | solution.py:39
  30.2 3.8 %collective-permute-start.3 = (f32[8,1024]{1,0:T(8,128)S(1)}, f32[8,1024]{1,0:T(8,128)S(1)}, u32[]{:S(2)}, u32[]{:S(2)}) collective-permute-start(f32[8,1024]{1,0:T(8,128)S(1)} %get-tuple-element.34.message), channel_id=1, source_target_pairs={{0,1},{1,0},{2,3},{3,2},{4,5},{5,4},{6,7},{7,6},{8,9},{9,8},{10,11... | collective-permute-start | bytes 98312 | tf_op jit(solution)/shard_map/ppermute | solution.py:35
  34.0 1.0 %mixes.1 = (f32[128,1024]{1,0:T(8,128)S(1)}, f32[128,1024]{1,0:T(8,128)S(1)}, f32[128,1024]{1,0:T(8,128)S(1)}, bf16[128,1024]{1,0:T(8,128)(2,1)S(1)}) custom-call(bf16[1024,128]{1,0:T(8,128)(2,1)S(1)} %collective-permute-done.1.last_page, bf16[1024,128]{1,0:T(8,128)(2,1)S(1)} %collective-permute-done.page.far_page, ...), custom_call_target="tpu_custom_call" | custom-call | flops 805306368 | bytes 2097152 | tf_op jit(solution)/shard_map/mixes/pallas_call | solution.py:39
  35.1 0.0 collective-permute-done.3.arrived
  35.1 1.0 %send_last.1 = (s16[1088,128]{1,0:T(8,128)(2,1)S(1)}, f32[1,1024]{1,0:T(1,128)S(1)}, f32[4,1024]{1,0:T(4,128)S(1)}) custom-call(f32[8,1024]{1,0:T(8,128)S(1)} %get-tuple-element.34.message, f32[8,1024]{1,0:T(8,128)S(1)} %collective-permute-done.3.arrived, f32[1,1024]{1,0:T(1,128)S(1)} %get-tuple-element.35.total_a, f32[1,1024]{1,0:T(1,128)S(1)} %get-tuple-element.36.total_c, ...), custom_call_target="tpu_custom_call" | custom-call | flops 268435456 | bytes 2097152 | tf_op jit(solution)/shard_map/send_last/pallas_call | solution.py:39
  36.1 3.9 %collective-permute-start.6 = (s16[1088,128]{1,0:T(8,128)(2,1)S(1)}, s16[1088,128]{1,0:T(8,128)(2,1)S(1)}, u32[]{:S(2)}, u32[]{:S(2)}) collective-permute-start(s16[1088,128]{1,0:T(8,128)(2,1)S(1)} %get-tuple-element.56), channel_id=1, source_target_pairs={{0,0},{1,509},{2,2},{3,511},{4,4},{5,1},{6,6},{7,3},{8,8},{9,5},{1... | collective-permute-start | bytes 835592 | tf_op jit(solution)/shard_map/ppermute | solution.py:31
  40.0 1.3 %send_far.1 = s16[1072,128]{1,0:T(8,128)(2,1)S(1)} custom-call(f32[4,1024]{1,0:T(4,128)S(1)} %get-tuple-element.42.weight, bf16[128,1024]{1,0:T(8,128)(2,1)S(1)} %get-tuple-element.47.query_t, bf16[128,1024]{1,0:T(8,128)(2,1)S(1)} %get-tuple-element.41.mate_query_t, bf16[1024,1024]{1,0:T(8,128)(2,1)S(1)} %get-tuple-element.39.powers_c, ...), custom_call_target="tpu_custom_call" | custom-call | flops 536870912 | bytes 2097152 | tf_op jit(solution)/shard_map/send_far/pallas_call | solution.py:39
  41.3 2.0 %collective-permute-start.5 = (s16[1072,128]{1,0:T(8,128)(2,1)S(1)}, s16[1072,128]{1,0:T(8,128)(2,1)S(1)}, u32[]{:S(2)}, u32[]{:S(2)}) collective-permute-start(s16[1072,128]{1,0:T(8,128)(2,1)S(1)} %send_far.1), channel_id=1, source_target_pairs={{0,510},{1,511},{2,0},{3,1},{4,2},{5,3},{6,4},{7,5},{8,6},{9,7},{1... | collective-permute-start | bytes 823304 | tf_op jit(solution)/shard_map/ppermute | solution.py:25
  43.3 0.3 send_query.1
  43.6 1.9 %collective-permute-start.4 = (s16[1040,128]{1,0:T(8,128)(2,1)S(1)}, s16[1040,128]{1,0:T(8,128)(2,1)S(1)}, u32[]{:S(2)}, u32[]{:S(2)}) collective-permute-start(s16[1040,128]{1,0:T(8,128)(2,1)S(1)} %get-tuple-element.53), channel_id=1, source_target_pairs={{0,1},{1,0},{2,3},{3,2},{4,5},{5,4},{6,7},{7,6},{8,9},{9,8},{10,11... | collective-permute-start | bytes 798728 | tf_op jit(solution)/shard_map/ppermute | solution.py:35
  45.5 0.7 %own_terms.1 = (f32[1024,128]{1,0:T(8,128)S(1)}, f32[1024,128]{1,0:T(8,128)S(1)}) custom-call(f32[4,1024]{1,0:T(4,128)S(1)} %get-tuple-element.42.weight, bf16[128,1024]{1,0:T(8,128)(2,1)S(1)} %get-tuple-element.47.query_t, bf16[1024,1024]{1,0:T(8,128)(2,1)S(1)} %get-tuple-element.48.powers_a, f32[128,1024]{1,0:T(8,128)S(1)} %get-tuple-element.49.mixed_a, ...), custom_call_target="tpu_custom_call" | custom-call | flops 1000 | bytes 2097152 | tf_op jit(solution)/shard_map/own_terms/pallas_call | solution.py:39
  46.3 0.5 %copy.6 = f32[32]{0:T(128)} copy(f32[32]{0:T(128)S(1)} %bitcast.6) | data formatting | bytes 256
  46.8 0.3 collective-permute-done.4.refs_0_
  47.0 0.9 %query_sum.1 = f32[1024,128]{1,0:T(8,128)} custom-call(f32[1024,128]{1,0:T(8,128)S(1)} %get-tuple-element.52.own, s16[1040,128]{1,0:T(8,128)(2,1)S(1)} %collective-permute-done.4.refs_0_), custom_call_target="tpu_custom_call" | custom-call | flops 1000 | bytes 1000 | tf_op jit(solution)/shard_map/query_sum/pallas_call | solution.py:216
  47.9 1.5 %collective-permute-done.5.refs_0_ = s16[1072,128]{1,0:T(8,128)(2,1)S(1)} collective-permute-done((s16[1072,128]{1,0:T(8,128)(2,1)S(1)}, s16[1072,128]{1,0:T(8,128)(2,1)S(1)}, u32[]{:S(2)}, u32[]{:S(2)}) %collective-permute-start.5) | collective-permute-done | bytes 274464 | tf_op jit(solution)/shard_map/ppermute | solution.py:25
  49.4 0.9 %page_sum.1 = f32[1024,128]{1,0:T(8,128)} custom-call(f32[1024,128]{1,0:T(8,128)S(1)} %get-tuple-element.55.own, s16[1072,128]{1,0:T(8,128)(2,1)S(1)} %collective-permute-done.5.refs_0_, s16[1088,128]{1,0:T(8,128)(2,1)S(1)} %collective-permute-done.6.refs_1_), custom_call_target="tpu_custom_call" | custom-call | flops 1000 | bytes 1000 | tf_op jit(solution)/shard_map/page_sum/pallas_call | solution.py:216
  (1 shorter events, 0.0 us)
Async XLA Ops:
  0.6 24.0 %collective-permute-start = (bf16[1024,128]{1,0:T(8,128)(2,1)}, bf16[1024,128]{1,0:T(8,128)(2,1)S(1)}, u32[]{:S(2)}, u32[]{:S(2)}) collective-permute-start(bf16[1024,128]{1,0:T(8,128)(2,1)} %bitcast.9), channel_id=1, source_target_pairs={{0,2},{1,3},{2,4},{3,5},{4,6},{5,7},{6,8},{7,9},{8,10},{9,11},{10,... | collective-permute-start | bytes 786440 | tf_op jit(solution)/shard_map/ppermute | solution.py:25
  4.7 22.1 %collective-permute-start.1 = (bf16[1024,128]{1,0:T(8,128)(2,1)}, bf16[1024,128]{1,0:T(8,128)(2,1)S(1)}, u32[]{:S(2)}, u32[]{:S(2)}) collective-permute-start(bf16[1024,128]{1,0:T(8,128)(2,1)} %bitcast.10), channel_id=1, source_target_pairs={{0,0},{1,5},{2,2},{3,7},{4,4},{5,9},{6,6},{7,11},{8,8},{9,13},{10,... | collective-permute-start | bytes 786440 | tf_op jit(solution)/shard_map/ppermute | solution.py:31
  9.2 17.6 %collective-permute-start.2 = (bf16[1024,128]{1,0:T(8,128)(2,1)}, bf16[1024,128]{1,0:T(8,128)(2,1)S(1)}, u32[]{:S(2)}, u32[]{:S(2)}) collective-permute-start(bf16[1024,128]{1,0:T(8,128)(2,1)} %bitcast.12), channel_id=1, source_target_pairs={{0,1},{1,0},{2,3},{3,2},{4,5},{5,4},{6,7},{7,6},{8,9},{9,8},{10,11... | collective-permute-start | bytes 786440 | tf_op jit(solution)/shard_map/ppermute | solution.py:35
  30.2 4.9 %collective-permute-start.3 = (f32[8,1024]{1,0:T(8,128)S(1)}, f32[8,1024]{1,0:T(8,128)S(1)}, u32[]{:S(2)}, u32[]{:S(2)}) collective-permute-start(f32[8,1024]{1,0:T(8,128)S(1)} %get-tuple-element.34.message), channel_id=1, source_target_pairs={{0,1},{1,0},{2,3},{3,2},{4,5},{5,4},{6,7},{7,6},{8,9},{9,8},{10,11... | collective-permute-start | bytes 98312 | tf_op jit(solution)/shard_map/ppermute | solution.py:35
  36.1 13.3 %collective-permute-start.6 = (s16[1088,128]{1,0:T(8,128)(2,1)S(1)}, s16[1088,128]{1,0:T(8,128)(2,1)S(1)}, u32[]{:S(2)}, u32[]{:S(2)}) collective-permute-start(s16[1088,128]{1,0:T(8,128)(2,1)S(1)} %get-tuple-element.56), channel_id=1, source_target_pairs={{0,0},{1,509},{2,2},{3,511},{4,4},{5,1},{6,6},{7,3},{8,8},{9,5},{1... | collective-permute-start | bytes 835592 | tf_op jit(solution)/shard_map/ppermute | solution.py:31
  41.3 8.1 %collective-permute-start.5 = (s16[1072,128]{1,0:T(8,128)(2,1)S(1)}, s16[1072,128]{1,0:T(8,128)(2,1)S(1)}, u32[]{:S(2)}, u32[]{:S(2)}) collective-permute-start(s16[1072,128]{1,0:T(8,128)(2,1)S(1)} %send_far.1), channel_id=1, source_target_pairs={{0,510},{1,511},{2,0},{3,1},{4,2},{5,3},{6,4},{7,5},{8,6},{9,7},{1... | collective-permute-start | bytes 823304 | tf_op jit(solution)/shard_map/ppermute | solution.py:25
  43.6 3.4 %collective-permute-start.4 = (s16[1040,128]{1,0:T(8,128)(2,1)S(1)}, s16[1040,128]{1,0:T(8,128)(2,1)S(1)}, u32[]{:S(2)}, u32[]{:S(2)}) collective-permute-start(s16[1040,128]{1,0:T(8,128)(2,1)S(1)} %get-tuple-element.53), channel_id=1, source_target_pairs={{0,1},{1,0},{2,3},{3,2},{4,5},{5,4},{6,7},{7,6},{8,9},{9,8},{10,11... | collective-permute-start | bytes 798728 | tf_op jit(solution)/shard_map/ppermute | solution.py:35

commit v4 on v3

v4 whole, which is shorter than its diff:
```python
import functools
import math

import jax
import jax.numpy as jnp
from jax import lax
from jax.experimental import pallas as pl
from jax.experimental.pallas import tpu as pltpu
from jax.sharding import PartitionSpec as P


tau_scale = 0.1
EXPONENT = math.log2(math.e) / tau_scale
CHUNK = 128
COLUMNS = 8
PAD = 16
MIB = 1024 * 1024

VMEM = pl.BlockSpec(memory_space=pltpu.VMEM)
ANY = pl.BlockSpec(memory_space=pl.ANY)


def passed_along(value, axis, steps):
    count = lax.axis_size(axis)
    pairs = [(source, (source + steps) % count) for source in range(count)]
    return lax.ppermute(value, axis, pairs)


def odd_passed_along(value, axis, steps):
    count = lax.axis_size(axis)
    pairs = [(source, (source + steps) % count if source % 2 else source) for source in range(count)]
    return lax.ppermute(value, axis, pairs)


def swapped(value, axis):
    return lax.ppermute(value, axis, [(source, source ^ 1) for source in range(lax.axis_size(axis))])


def on_core(body, outs, args, flops, name, limit=8, specs=None, scratch=()):
    return pl.pallas_call(
        body,
        out_shape=[pltpu.VMEM(shape, dtype) for shape, dtype in outs],
        in_specs=specs or [VMEM] * len(args),
        out_specs=[VMEM] * len(outs),
        scratch_shapes=list(scratch),
        compiler_params=pltpu.CompilerParams(vmem_limit_bytes=limit * MIB),
        cost_estimate=pl.CostEstimate(flops=flops, bytes_accessed=2 * MIB, transcendentals=0),
        name=name,
    )(*args)


def rows_dot(a, b):
    return lax.dot_general(a, b, (((1,), (1,)), ((), ())), preferred_element_type=jnp.float32)


def token_powers(page, query, powers_ref, stats_ref, unit):
    rows = query.shape[0]
    for start in range(0, rows, CHUNK):
        cut = slice(start, start + CHUNK)
        products = rows_dot(query[cut, :], page[...])
        largest = jnp.max(products, axis=1, keepdims=True)
        powers = jnp.exp2((products - largest) * EXPONENT)
        powers_ref[cut, :] = powers.astype(jnp.bfloat16)
        stats_ref[cut, 2 * unit : 2 * unit + 1] = largest
        stats_ref[cut, 2 * unit + 1 : 2 * unit + 2] = jnp.sum(powers, axis=1, keepdims=True)


def token_rows(stats_ref, units, total_ref):
    stats = stats_ref[...].T
    smooth = []
    for unit in range(units):
        total = stats[2 * unit + 1 : 2 * unit + 2, :]
        total_ref[unit : unit + 1, :] = total
        smooth.append(stats[2 * unit : 2 * unit + 1, :] + tau_scale * jnp.log(total))
    return smooth


def mix_pages(page, powers_ref, mixed_ref):
    mixed_ref[...] = jnp.dot(powers_ref[...], page[...], preferred_element_type=jnp.float32)


def page_terms(query_t, weight, powers_ref):
    return jnp.dot(scaled(query_t[...], weight), powers_ref[...], preferred_element_type=jnp.float32)


def weight_columns(weight):
    return jnp.concatenate([weight[...], weight[...]], axis=0).T


def turned(value):
    return value.astype(jnp.float32).T.astype(jnp.bfloat16)


def of_token(shape, token_axis, tokens):
    token = lax.broadcasted_iota(jnp.int32, shape, token_axis)
    query = lax.broadcasted_iota(jnp.int32, shape, 1 - token_axis)
    return token, query


def own_body(tokens, page_hbm, query_hbm, positive_hbm, powers_ref, mixed_ref, total_ref, smooth_ref,
             query_t_ref, query_ref, positive_ref, page, positives, sems, stats):
    page_copy = pltpu.make_async_copy(page_hbm, page, sems.at[0])
    query_copy = pltpu.make_async_copy(query_hbm, query_ref, sems.at[1])
    positive_copy = pltpu.make_async_copy(positive_hbm, positives, sems.at[2])
    page_copy.start()
    query_copy.start()
    positive_copy.start()
    positive_copy.wait()
    token, query = of_token((positives.shape[1], query_ref.shape[0]), 1, tokens)
    inside = (token >= query * tokens) & (token < query * tokens + tokens)
    positive_ref[...] = jnp.sum(jnp.where(inside, positives[...].astype(jnp.float32).T, 0.0), axis=0, keepdims=True)
    page_copy.wait()
    query_copy.wait()
    token_powers(page, query_ref, powers_ref, stats, 0)
    smooth_ref[...] = token_rows(stats, 1, total_ref)[0]
    mix_pages(page, powers_ref, mixed_ref)
    query_t_ref[...] = turned(query_ref[...])


def far_body(page, query, powers_ref, total_ref, smooth_ref, stats):
    token_powers(page, query, powers_ref, stats, 0)
    smooth_ref[...] = token_rows(stats, 1, total_ref)[0]


def query_sums(value, tokens):
    lane = lax.broadcasted_iota(jnp.int32, value.shape, 1)
    width = value.shape[1]
    step = tokens // 2
    while step:
        ahead = pltpu.roll(value, width - step, 1)
        behind = pltpu.roll(value, step, 1)
        value = value + jnp.where((lane & step) != 0, behind, ahead)
        step //= 2
    return value


def mate_body(page, query, smooth_c, powers_ref, total_ref, smooth_ref, stats):
    token_powers(page, query, powers_ref, stats, 0)
    smooth_ref[0:1, :] = smooth_c[...]
    smooth_ref[1:2, :] = token_rows(stats, 1, total_ref)[0]


def last_body(tokens, page, mate_query, smooth_a, smooth_far, positive,
              powers_ref, total_ref, message_ref, stats):
    token_powers(page, mate_query, powers_ref, stats, 0)
    smooth = token_rows(stats, 1, total_ref)
    sums = query_sums(jnp.concatenate([smooth_a[...], smooth_far[...]] + smooth, axis=0), tokens)
    message_ref[0:4, :] = sums
    message_ref[4:5, :] = positive[...]
    message_ref[5:8, :] = sums[0:3, :]


def mix_body(far_page, mate_query, powers_c, powers_d, mixed_c_ref, mixed_d_ref, mate_query_t_ref):
    mate_query_t_ref[...] = turned(mate_query[...])
    mix_pages(far_page, powers_c, mixed_c_ref)
    mix_pages(far_page, powers_d, mixed_d_ref)


def slopes_of(scores, positive):
    flags = [(positive == float(offset)).astype(jnp.float32) for offset in range(4)]
    positive_score = sum(flag * score for flag, score in zip(flags, scores))
    margins = [score - positive_score for score in scores]
    loss = sum((1.0 - flag) * jax.nn.softplus(margin) for flag, margin in zip(flags, margins))
    terms = [(1.0 - flag) * jax.nn.sigmoid(margin) for flag, margin in zip(flags, margins)]
    total = sum(terms)
    return loss, [term - flag * total for flag, term in zip(flags, terms)]


def to_short(value):
    largest = jnp.maximum(jnp.max(jnp.abs(value), axis=0, keepdims=True), 1e-38)
    power = jnp.minimum(jnp.floor(math.log2(32000.0) - jnp.log2(largest)), 126.0)
    short = jnp.round(value * jnp.exp2(power)).astype(jnp.int32).astype(jnp.int16)
    tail = jnp.broadcast_to(power, (PAD, value.shape[1])).astype(jnp.int32).astype(jnp.int16)
    return short, tail


def from_short(ref, rows):
    power = ref[rows : rows + PAD, :].astype(jnp.int32).astype(jnp.float32)[0:1, :]
    return ref[0:rows, :].astype(jnp.int32).astype(jnp.float32) * jnp.exp2(-power)


def scaled(query_t, weight):
    return (query_t.astype(jnp.float32) * weight).astype(jnp.bfloat16)


def put_short(ref, value):
    count = value.shape[0]
    short, tail = to_short(value)
    ref[0:count, :] = short
    for start in range(count, ref.shape[0], PAD):
        ref[start : start + PAD, :] = tail


def send_last_body(message, arrived, total_a, total_c, total_d, total_b, mate_query_t, powers_b,
                   out_ref, loss_ref, weight_ref):
    even = lax.axis_index("dp") % 2 == 0
    own = message[...]
    mate = arrived[...]
    loss, slopes = slopes_of(
        [own[0:1], jnp.where(even, mate[2:3], mate[3:4]), own[1:2], jnp.where(even, mate[3:4], mate[2:3])], own[4:5])
    _, mate_slopes = slopes_of(
        [mate[0:1], jnp.where(even, own[3:4], own[2:3]), mate[1:2], jnp.where(even, own[2:3], own[3:4])], mate[4:5])
    loss_ref[...] = loss
    weight_b = jnp.where(even, mate_slopes[1], mate_slopes[3]) / total_b[...]
    weight_ref[0:1, :] = slopes[0] / total_a[...]
    weight_ref[1:2, :] = weight_b
    weight_ref[2:3, :] = slopes[2] / total_c[...]
    weight_ref[3:4, :] = jnp.where(even, mate_slopes[3], mate_slopes[1]) / total_d[...]
    put_short(out_ref, page_terms(mate_query_t, weight_b, powers_b).T)


def send_far_body(weight, query_t, mate_query_t, powers_c, powers_d, out_ref):
    term = page_terms(query_t, weight[2:3, :], powers_c) + page_terms(mate_query_t, weight[3:4, :], powers_d)
    put_short(out_ref, term.T)


def send_query_body(tokens, weight, last_page, powers_b, mixed_d, loss_all, out_ref, loss_ref):
    mixed_b = jnp.dot(powers_b[...], last_page[...], preferred_element_type=jnp.float32)
    columns = weight_columns(weight)
    put_short(out_ref, mixed_b * columns[:, 1:2] + mixed_d[...] * columns[:, 3:4])
    token, query = of_token((loss_ref.shape[1], loss_all.shape[1]), 1, tokens)
    loss_ref[...] = jnp.sum(jnp.where(token == query * tokens, loss_all[...], 0.0), axis=1, keepdims=True).T


def keep_body(weight, query_t, powers_a, mixed_a, mixed_c, page_ref, query_ref):
    columns = weight_columns(weight)
    page_ref[...] = page_terms(query_t, weight[0:1, :], powers_a).T
    query_ref[...] = mixed_a[...] * columns[:, 0:1] + mixed_c[...] * columns[:, 2:3]


def sum_body(own, *refs):
    total = own[...]
    for arrived in refs[:-1]:
        total = total + from_short(arrived, own.shape[0])
    refs[-1][...] = total


def last_sums_body(query_own, query_in, loss_row, page_own, far_in, last_in, query_ref, loss_ref, page_ref):
    sum_body(query_own, query_in, query_ref)
    loss_ref[...] = loss_row[0, :]
    sum_body(page_own, far_in, last_in, page_ref)


def last_sums(query_own, query_in, loss_row, page_own, far_in, last_in):
    shapes = (query_own.shape, loss_row.shape[1:], page_own.shape)
    return pl.pallas_call(
        last_sums_body,
        out_shape=[jax.ShapeDtypeStruct(shape, jnp.float32) for shape in shapes],
        in_specs=[VMEM] * 6,
        out_specs=[VMEM] * 3,
        compiler_params=pltpu.CompilerParams(vmem_limit_bytes=4 * MIB),
        cost_estimate=pl.CostEstimate(flops=1000, bytes_accessed=1000, transcendentals=0),
        name="last_sums",
    )(query_own, query_in, loss_row, page_own, far_in, last_in)


def in_hbm(value):
    return pltpu.with_memory_space_constraint(value, pltpu.HBM)


def on_device(queries, positives, pages):
    count, tokens, width = queries.shape
    page = pages[0]
    patches = page.shape[0]
    query = queries.reshape(count * tokens, width)
    rows = count * tokens
    f32, bf16, i16 = jnp.float32, jnp.bfloat16, jnp.int16
    unit = 2 * rows * patches * width

    far_page = passed_along(page, "dp", 2)
    last_page = odd_passed_along(page, "dp", 4)
    mate_query = swapped(query, "dp")

    powers_a, mixed_a, total_a, smooth_a, query_t, own_query, positive = on_core(
        functools.partial(own_body, tokens),
        [((rows, patches), bf16), ((rows, width), f32), ((1, rows), f32), ((1, rows), f32), ((width, rows), bf16),
         ((rows, width), bf16), ((1, rows), f32)],
        tuple(in_hbm(value) for value in (page, query, positives[None])), 2 * unit, "own_unit", specs=[ANY] * 3,
        scratch=[pltpu.VMEM((patches, width), bf16), pltpu.VMEM((1, count), jnp.int32), pltpu.SemaphoreType.DMA((3,)),
                 pltpu.VMEM((rows, COLUMNS), f32)])
    powers_c, total_c, smooth_c = on_core(
        far_body, [((rows, patches), bf16), ((1, rows), f32), ((1, rows), f32)], (far_page, own_query), unit, "far_unit",
        scratch=[pltpu.VMEM((rows, COLUMNS), f32)])
    powers_d, total_d, smooth_far = on_core(
        mate_body, [((rows, patches), bf16), ((1, rows), f32), ((2, rows), f32)],
        (far_page, mate_query, smooth_c), unit, "mate_unit",
        scratch=[pltpu.VMEM((rows, COLUMNS), f32)])
    powers_b, total_b, message = on_core(
        functools.partial(last_body, tokens),
        [((rows, patches), bf16), ((1, rows), f32), ((8, rows), f32)],
        (last_page, mate_query, smooth_a, smooth_far, positive), unit, "last_unit",
        scratch=[pltpu.VMEM((rows, COLUMNS), f32)])
    arrived = swapped(message, "dp")
    mixed_c, mixed_d, mate_query_t = on_core(
        mix_body, [((rows, width), f32)] * 2 + [((width, rows), bf16)],
        (far_page, mate_query, powers_c, powers_d), 2 * unit, "mixes")
    last_out, loss_all, weight = on_core(
        send_last_body,
        [((patches + 4 * PAD, width), i16), ((1, rows), f32), ((4, rows), f32)],
        (message, arrived, total_a, total_c, total_d, total_b, mate_query_t, powers_b), unit, "send_last")
    last_in = odd_passed_along(last_out, "dp", -4)
    far_out, = on_core(
        send_far_body, [((patches + 3 * PAD, width), i16)],
        (weight, query_t, mate_query_t, powers_c, powers_d), 2 * unit, "send_far")
    far_in = passed_along(far_out, "dp", -2)
    query_out, loss = on_core(
        functools.partial(send_query_body, tokens),
        [((rows + PAD, width), i16), ((1, count), f32)],
        (weight, last_page, powers_b, mixed_d, loss_all), 1000, "send_query")
    query_in = swapped(query_out, "dp")
    page_own, query_own = on_core(
        keep_body, [((patches, width), f32), ((rows, width), f32)],
        (weight, query_t, powers_a, mixed_a, mixed_c), 1000, "own_terms")
    query_grad, loss, page_grad = last_sums(query_own, query_in, loss, page_own, far_in, last_in)
    return (loss, query_grad.reshape(count, tokens, width), page_grad[None])


def solution(mesh):
    in_specs = (P("dp", None, None), P("dp"), P("dp", None, None))
    out_specs = (P("dp"), P("dp", None, None), P("dp", None, None))
    return jax.shard_map(
        on_device, mesh=mesh, in_specs=in_specs, out_specs=out_specs, check_vma=False
    )
```

time: 50.7 us -> 48.7 us (0.961)
  Pallas kernels: 14.2 us -> 12.8 us
  waiting for transfers between devices: 11.1 us -> 9.83 us
  starting transfers between devices: 23.9 us -> 25 us
  local copies, waits for them, and re-layouts: 0.51 us -> 0 us
    ppermute x2, starting transfers between devices: 8.38 us -> 5.59 us  [odd_passed_along(): return lax.ppermute(value, axis, pairs)]
    ppermute x2, waiting for transfers between devices: 10.1 us -> 7.73 us  [passed_along(): return lax.ppermute(value, axis, pairs)]
    ppermute x3, starting transfers between devices: 9.49 us -> 11.5 us  [swapped(): lax.ppermute(value, axis, [(source, source ^ 1) for source in range(lax.a...]
    ppermute x2, starting transfers between devices: 5.99 us -> 7.91 us  [passed_along(): return lax.ppermute(value, axis, pairs)]
    pallas_call x2 -> x1, Pallas kernels: 1.81 us -> 1.04 us  [last_sums(): pl.pallas_call(last_sums_body, out_shape=[jax.ShapeDtypeStruct(shape, jnp...]
    ppermute x2, waiting for transfers between devices: 0.65 us -> 1.36 us  [odd_passed_along(): return lax.ppermute(value, axis, pairs)]
    pallas_call x8 -> x9, Pallas kernels: 12.4 us -> 11.8 us  [on_core(): pl.pallas_call(body, out_shape=[pltpu.VMEM(shape, dtype) for shape, dtype...]
    unnamed x1 -> x0, local copies, waits for them, and re-layouts: 0.51 us -> none
  transfers between devices with their start and end apart: 7 -> 7, of which waited for: 4 -> 4; matrix products, arithmetic and copies ran while one was open for 1% -> 0% of each run, Pallas kernels for 18% -> 19%
where the time goes in v4:
time: 48.7 us; the launch traced here: 48.4 us
  starting transfers between devices  25 us (51%)
  Pallas kernels  12.8 us (26%)
  waiting for transfers between devices  9.83 us (20%)
  between operations  0.76 us (2%)
    pallas_call x9, Pallas kernels, on_core(): pl.pallas_call(body, out_shape=[pltpu.VMEM(shape, dtype) for shape, dtype...  11.8 us
    ppermute x3, starting transfers between devices, swapped(): lax.ppermute(value, axis, [(source, source ^ 1) for source in range(lax.a...  11.5 us
    ppermute x2, starting transfers between devices, passed_along(): return lax.ppermute(value, axis, pairs)  7.91 us
    ppermute x2, waiting for transfers between devices, passed_along(): return lax.ppermute(value, axis, pairs)  7.73 us
    ppermute x2, starting transfers between devices, odd_passed_along(): return lax.ppermute(value, axis, pairs)  5.59 us
    ppermute x2, waiting for transfers between devices, odd_passed_along(): return lax.ppermute(value, axis, pairs)  1.36 us
    pallas_call x1, Pallas kernels, last_sums(): pl.pallas_call(last_sums_body, out_shape=[jax.ShapeDtypeStruct(shape, jnp...  1.04 us
  transfers between devices with their start and end apart: 7, of which 4 were waited for; matrix products, arithmetic and copies ran while one was open for 0% of the time, Pallas kernels for 19%

profile of v4, /device:TPU:1, one launch (start us, length us, event | category | flops | bytes accessed | tf_op | source)
XLA Modules:
  0.0 48.4 jit_solution(11411619083248293775)
XLA Ops:
  0.6 4.0 %collective-permute-start.2 = (bf16[1024,128]{1,0:T(8,128)(2,1)}, bf16[1024,128]{1,0:T(8,128)(2,1)S(1)}, u32[]{:S(2)}, u32[]{:S(2)}) collective-permute-start(bf16[1024,128]{1,0:T(8,128)(2,1)} %bitcast.9), channel_id=1, source_target_pairs={{0,2},{1,3},{2,4},{3,5},{4,6},{5,7},{6,8},{7,9},{8,10},{9,11},{10,... | collective-permute-start | bytes 786440 | tf_op jit(solution)/shard_map/ppermute | solution.py:26
  4.7 6.7 %collective-permute-start.1 = (bf16[1024,128]{1,0:T(8,128)(2,1)}, bf16[1024,128]{1,0:T(8,128)(2,1)S(1)}, u32[]{:S(2)}, u32[]{:S(2)}) collective-permute-start(bf16[1024,128]{1,0:T(8,128)(2,1)} %bitcast.7), channel_id=1, source_target_pairs={{0,1},{1,0},{2,3},{3,2},{4,5},{5,4},{6,7},{7,6},{8,9},{9,8},{10,11... | collective-permute-start | bytes 786440 | tf_op jit(solution)/shard_map/ppermute | solution.py:36
  11.4 1.9 %collective-permute-start = (bf16[1024,128]{1,0:T(8,128)(2,1)}, bf16[1024,128]{1,0:T(8,128)(2,1)S(1)}, u32[]{:S(2)}, u32[]{:S(2)}) collective-permute-start(bf16[1024,128]{1,0:T(8,128)(2,1)} %bitcast.10), channel_id=1, source_target_pairs={{0,0},{1,5},{2,2},{3,7},{4,4},{5,9},{6,6},{7,11},{8,8},{9,13},{10,... | collective-permute-start | bytes 786440 | tf_op jit(solution)/shard_map/ppermute | solution.py:32
  13.3 2.7 %own_unit.1 = (bf16[1024,1024]{1,0:T(8,128)(2,1)S(1)}, f32[1024,128]{1,0:T(8,128)S(1)}, f32[1,1024]{1,0:T(1,128)S(1)}, f32[1,1024]{1,0:T(1,128)S(1)}, bf16[128,1...) custom-call(bf16[1024,128]{1,0:T(8,128)(2,1)} %bitcast.11, bf16[1024,128]{1,0:T(8,128)(2,1)} %bitcast.8, ...), custom_call_target="tpu_custom_call" | custom-call | flops 536870912 | bytes 2097152 | tf_op jit(solution)/shard_map/own_unit/pallas_call | solution.py:40
  15.9 7.5 %collective-permute-done.2.page.far_page = bf16[1024,128]{1,0:T(8,128)(2,1)S(1)} collective-permute-done((bf16[1024,128]{1,0:T(8,128)(2,1)}, bf16[1024,128]{1,0:T(8,128)(2,1)S(1)}, u32[]{:S(2)}, u32[]{:S(2)}) %collective-permute-start.2) | collective-permute-done | bytes 262176 | tf_op jit(solution)/shard_map/ppermute | solution.py:26
  23.5 1.3 %far_unit.1 = (bf16[1024,1024]{1,0:T(8,128)(2,1)S(1)}, f32[1,1024]{1,0:T(1,128)S(1)}, f32[1,1024]{1,0:T(1,128)S(1)}) custom-call(bf16[1024,128]{1,0:T(8,128)(2,1)S(1)} %collective-permute-done.2.page.far_page, bf16[1024,128]{1,0:T(8,128)(2,1)S(1)} %get-tuple-element.33.query), custom_call_target="tpu_custom_call" | custom-call | flops 268435456 | bytes 2097152 | tf_op jit(solution)/shard_map/far_unit/pallas_call | solution.py:40
  24.7 0.0 collective-permute-done.1.query.mate_query
  24.8 1.3 %mate_unit.1 = (bf16[1024,1024]{1,0:T(8,128)(2,1)S(1)}, f32[1,1024]{1,0:T(1,128)S(1)}, f32[2,1024]{1,0:T(2,128)S(1)}) custom-call(bf16[1024,128]{1,0:T(8,128)(2,1)S(1)} %collective-permute-done.2.page.far_page, bf16[1024,128]{1,0:T(8,128)(2,1)S(1)} %collective-permute-done.1.query.mate_query, f32[1,1024]{1,0:T(1,128)S(1)} %get-tuple-element.34.smooth_c), custom_call_target="tpu_custom_call" | custom-call | flops 268435456 | bytes 2097152 | tf_op jit(solution)/shard_map/mate_unit/pallas_call | solution.py:40
  26.0 1.4 %collective-permute-done.page.last_page = bf16[1024,128]{1,0:T(8,128)(2,1)S(1)} collective-permute-done((bf16[1024,128]{1,0:T(8,128)(2,1)}, bf16[1024,128]{1,0:T(8,128)(2,1)S(1)}, u32[]{:S(2)}, u32[]{:S(2)}) %collective-permute-start) | collective-permute-done | bytes 262176 | tf_op jit(solution)/shard_map/ppermute | solution.py:32
  27.4 1.8 %last_unit.1 = (bf16[1024,1024]{1,0:T(8,128)(2,1)S(1)}, f32[1,1024]{1,0:T(1,128)S(1)}, f32[8,1024]{1,0:T(8,128)S(1)}) custom-call(bf16[1024,128]{1,0:T(8,128)(2,1)S(1)} %collective-permute-done.page.last_page, bf16[1024,128]{1,0:T(8,128)(2,1)S(1)} %collective-permute-done.1.query.mate_query, f32[1,1024]{1,0:T(1,128)S(1)} %get-tuple-element.32.smooth_a, ...), custom_call_target="tpu_custom_call" | custom-call | flops 268435456 | bytes 2097152 | tf_op jit(solution)/shard_map/last_unit/pallas_call | solution.py:40
  29.3 2.9 %collective-permute-start.3 = (f32[8,1024]{1,0:T(8,128)S(1)}, f32[8,1024]{1,0:T(8,128)S(1)}, u32[]{:S(2)}, u32[]{:S(2)}) collective-permute-start(f32[8,1024]{1,0:T(8,128)S(1)} %get-tuple-element.37.message), channel_id=1, source_target_pairs={{0,1},{1,0},{2,3},{3,2},{4,5},{5,4},{6,7},{7,6},{8,9},{9,8},{10,11... | collective-permute-start | bytes 98312 | tf_op jit(solution)/shard_map/ppermute | solution.py:36
  32.1 1.2 %mixes.1 = (f32[1024,128]{1,0:T(8,128)S(1)}, f32[1024,128]{1,0:T(8,128)S(1)}, bf16[128,1024]{1,0:T(8,128)(2,1)S(1)}) custom-call(bf16[1024,128]{1,0:T(8,128)(2,1)S(1)} %collective-permute-done.2.page.far_page, bf16[1024,128]{1,0:T(8,128)(2,1)S(1)} %collective-permute-done.1.query.mate_query, bf16[1024,1024]{1,0:T(8,128)(2,1)S(1)} %get-tuple-element.42.powers_c, ...), custom_call_target="tpu_custom_call" | custom-call | flops 536870912 | bytes 2097152 | tf_op jit(solution)/shard_map/mixes/pallas_call | solution.py:40
  33.4 0.0 collective-permute-done.3.arrived
  33.4 0.9 %send_last.1 = (s16[1088,128]{1,0:T(8,128)(2,1)S(1)}, f32[1,1024]{1,0:T(1,128)S(1)}, f32[4,1024]{1,0:T(4,128)S(1)}) custom-call(f32[8,1024]{1,0:T(8,128)S(1)} %get-tuple-element.37.message, f32[8,1024]{1,0:T(8,128)S(1)} %collective-permute-done.3.arrived, f32[1,1024]{1,0:T(1,128)S(1)} %get-tuple-element.38.total_a, f32[1,1024]{1,0:T(1,128)S(1)} %get-tuple-element.39.total_c, ...), custom_call_target="tpu_custom_call" | custom-call | flops 268435456 | bytes 2097152 | tf_op jit(solution)/shard_map/send_last/pallas_call | solution.py:40
  34.3 3.7 %collective-permute-start.6 = (s16[1088,128]{1,0:T(8,128)(2,1)S(1)}, s16[1088,128]{1,0:T(8,128)(2,1)S(1)}, u32[]{:S(2)}, u32[]{:S(2)}) collective-permute-start(s16[1088,128]{1,0:T(8,128)(2,1)S(1)} %get-tuple-element.57), channel_id=1, source_target_pairs={{0,0},{1,509},{2,2},{3,511},{4,4},{5,1},{6,6},{7,3},{8,8},{9,5},{1... | collective-permute-start | bytes 835592 | tf_op jit(solution)/shard_map/ppermute | solution.py:32
  38.0 0.9 %send_far.1 = s16[1072,128]{1,0:T(8,128)(2,1)S(1)} custom-call(f32[4,1024]{1,0:T(4,128)S(1)} %get-tuple-element.46.weight, bf16[128,1024]{1,0:T(8,128)(2,1)S(1)} %get-tuple-element.47.query_t, bf16[128,1024]{1,0:T(8,128)(2,1)S(1)} %get-tuple-element.44.mate_query_t, bf16[1024,1024]{1,0:T(8,128)(2,1)S(1)} %get-tuple-element.42.powers_c, ...), custom_call_target="tpu_custom_call" | custom-call | flops 536870912 | bytes 2097152 | tf_op jit(solution)/shard_map/send_far/pallas_call | solution.py:40
  38.9 3.9 %collective-permute-start.5 = (s16[1072,128]{1,0:T(8,128)(2,1)S(1)}, s16[1072,128]{1,0:T(8,128)(2,1)S(1)}, u32[]{:S(2)}, u32[]{:S(2)}) collective-permute-start(s16[1072,128]{1,0:T(8,128)(2,1)S(1)} %send_far.1), channel_id=1, source_target_pairs={{0,510},{1,511},{2,0},{3,1},{4,2},{5,3},{6,4},{7,5},{8,6},{9,7},{1... | collective-permute-start | bytes 823304 | tf_op jit(solution)/shard_map/ppermute | solution.py:26
  42.8 0.9 %send_query.1 = (s16[1040,128]{1,0:T(8,128)(2,1)S(1)}, f32[1,32]{1,0:T(1,128)S(1)}) custom-call(f32[4,1024]{1,0:T(4,128)S(1)} %get-tuple-element.46.weight, bf16[1024,128]{1,0:T(8,128)(2,1)S(1)} %collective-permute-done.page.last_page, bf16[1024,1024]{1,0:T(8,128)(2,1)S(1)} %get-tuple-element.45.powers_b, f32[1024,128]{1,0:T(8,128)S(1)} %get-tuple-element.52.mixed_d, ...), custom_call_target="tpu_custom_call" | custom-call | flops 1000 | bytes 2097152 | tf_op jit(solution)/shard_map/send_query/pallas_call | solution.py:40
  43.7 1.9 %collective-permute-start.4 = (s16[1040,128]{1,0:T(8,128)(2,1)S(1)}, s16[1040,128]{1,0:T(8,128)(2,1)S(1)}, u32[]{:S(2)}, u32[]{:S(2)}) collective-permute-start(s16[1040,128]{1,0:T(8,128)(2,1)S(1)} %get-tuple-element.54), channel_id=1, source_target_pairs={{0,1},{1,0},{2,3},{3,2},{4,5},{5,4},{6,7},{7,6},{8,9},{9,8},{10,11... | collective-permute-start | bytes 798728 | tf_op jit(solution)/shard_map/ppermute | solution.py:36
  45.6 0.8 %own_terms.1 = (f32[1024,128]{1,0:T(8,128)S(1)}, f32[1024,128]{1,0:T(8,128)S(1)}) custom-call(f32[4,1024]{1,0:T(4,128)S(1)} %get-tuple-element.46.weight, bf16[128,1024]{1,0:T(8,128)(2,1)S(1)} %get-tuple-element.47.query_t, bf16[1024,1024]{1,0:T(8,128)(2,1)S(1)} %get-tuple-element.48.powers_a, f32[1024,128]{1,0:T(8,128)S(1)} %get-tuple-element.49.mixed_a, ...), custom_call_target="tpu_custom_call" | custom-call | flops 1000 | bytes 2097152 | tf_op jit(solution)/shard_map/own_terms/pallas_call | solution.py:40
  46.4 0.7 %collective-permute-done.4.query_in = s16[1040,128]{1,0:T(8,128)(2,1)S(1)} collective-permute-done((s16[1040,128]{1,0:T(8,128)(2,1)S(1)}, s16[1040,128]{1,0:T(8,128)(2,1)S(1)}, u32[]{:S(2)}, u32[]{:S(2)}) %collective-permute-start.4) | collective-permute-done | bytes 266272 | tf_op jit(solution)/shard_map/ppermute | solution.py:36
  47.1 0.2 collective-permute-done.5.far_in
  47.3 0.0 collective-permute-done.6.last_in
  47.3 1.0 %last_sums.1 = (f32[1024,128]{1,0:T(8,128)}, f32[32]{0:T(128)}, f32[1024,128]{1,0:T(8,128)}) custom-call(f32[1024,128]{1,0:T(8,128)S(1)} %get-tuple-element.51.query_own, s16[1040,128]{1,0:T(8,128)(2,1)S(1)} %collective-permute-done.4.query_in, f32[1,32]{1,0:T(1,128)S(1)} %get-tuple-element.55.loss_row, f32[1024,128]{1,0:T(8,128)S(1)} %get-tuple-element.56.page_own, ...), custom_call_target="tpu_custom_call" | custom-call | flops 1000 | bytes 1000 | tf_op jit(solution)/shard_map/last_sums/pallas_call | solution.py:246
Async XLA Ops:
  0.6 22.8 %collective-permute-start.2 = (bf16[1024,128]{1,0:T(8,128)(2,1)}, bf16[1024,128]{1,0:T(8,128)(2,1)S(1)}, u32[]{:S(2)}, u32[]{:S(2)}) collective-permute-start(bf16[1024,128]{1,0:T(8,128)(2,1)} %bitcast.9), channel_id=1, source_target_pairs={{0,2},{1,3},{2,4},{3,5},{4,6},{5,7},{6,8},{7,9},{8,10},{9,11},{10,... | collective-permute-start | bytes 786440 | tf_op jit(solution)/shard_map/ppermute | solution.py:26
  4.7 20.1 %collective-permute-start.1 = (bf16[1024,128]{1,0:T(8,128)(2,1)}, bf16[1024,128]{1,0:T(8,128)(2,1)S(1)}, u32[]{:S(2)}, u32[]{:S(2)}) collective-permute-start(bf16[1024,128]{1,0:T(8,128)(2,1)} %bitcast.7), channel_id=1, source_target_pairs={{0,1},{1,0},{2,3},{3,2},{4,5},{5,4},{6,7},{7,6},{8,9},{9,8},{10,11... | collective-permute-start | bytes 786440 | tf_op jit(solution)/shard_map/ppermute | solution.py:36
  11.4 16.1 %collective-permute-start = (bf16[1024,128]{1,0:T(8,128)(2,1)}, bf16[1024,128]{1,0:T(8,128)(2,1)S(1)}, u32[]{:S(2)}, u32[]{:S(2)}) collective-permute-start(bf16[1024,128]{1,0:T(8,128)(2,1)} %bitcast.10), channel_id=1, source_target_pairs={{0,0},{1,5},{2,2},{3,7},{4,4},{5,9},{6,6},{7,11},{8,8},{9,13},{10,... | collective-permute-start | bytes 786440 | tf_op jit(solution)/shard_map/ppermute | solution.py:32
  29.3 4.1 %collective-permute-start.3 = (f32[8,1024]{1,0:T(8,128)S(1)}, f32[8,1024]{1,0:T(8,128)S(1)}, u32[]{:S(2)}, u32[]{:S(2)}) collective-permute-start(f32[8,1024]{1,0:T(8,128)S(1)} %get-tuple-element.37.message), channel_id=1, source_target_pairs={{0,1},{1,0},{2,3},{3,2},{4,5},{5,4},{6,7},{7,6},{8,9},{9,8},{10,11... | collective-permute-start | bytes 98312 | tf_op jit(solution)/shard_map/ppermute | solution.py:36
  34.3 13.0 %collective-permute-start.6 = (s16[1088,128]{1,0:T(8,128)(2,1)S(1)}, s16[1088,128]{1,0:T(8,128)(2,1)S(1)}, u32[]{:S(2)}, u32[]{:S(2)}) collective-permute-start(s16[1088,128]{1,0:T(8,128)(2,1)S(1)} %get-tuple-element.57), channel_id=1, source_target_pairs={{0,0},{1,509},{2,2},{3,511},{4,4},{5,1},{6,6},{7,3},{8,8},{9,5},{1... | collective-permute-start | bytes 835592 | tf_op jit(solution)/shard_map/ppermute | solution.py:32
  38.9 8.4 %collective-permute-start.5 = (s16[1072,128]{1,0:T(8,128)(2,1)S(1)}, s16[1072,128]{1,0:T(8,128)(2,1)S(1)}, u32[]{:S(2)}, u32[]{:S(2)}) collective-permute-start(s16[1072,128]{1,0:T(8,128)(2,1)S(1)} %send_far.1), channel_id=1, source_target_pairs={{0,510},{1,511},{2,0},{3,1},{4,2},{5,3},{6,4},{7,5},{8,6},{9,7},{1... | collective-permute-start | bytes 823304 | tf_op jit(solution)/shard_map/ppermute | solution.py:26
  43.7 3.4 %collective-permute-start.4 = (s16[1040,128]{1,0:T(8,128)(2,1)S(1)}, s16[1040,128]{1,0:T(8,128)(2,1)S(1)}, u32[]{:S(2)}, u32[]{:S(2)}) collective-permute-start(s16[1040,128]{1,0:T(8,128)(2,1)S(1)} %get-tuple-element.54), channel_id=1, source_target_pairs={{0,1},{1,0},{2,3},{3,2},{4,5},{5,4},{6,7},{7,6},{8,9},{9,8},{10,11... | collective-permute-start | bytes 798728 | tf_op jit(solution)/shard_map/ppermute | solution.py:36

commit v5 on v4

--- a/solution.py
+++ b/solution.py
@@ -13,6 +13,7 @@
 EXPONENT = math.log2(math.e) / tau_scale
 CHUNK = 128
 COLUMNS = 8
+LANES = 128
 PAD = 16
 MIB = 1024 * 1024
 
@@ -123,15 +124,18 @@
 
 
 def query_sums(value, tokens):
-    lane = lax.broadcasted_iota(jnp.int32, value.shape, 1)
-    width = value.shape[1]
-    step = tokens // 2
-    while step:
-        ahead = pltpu.roll(value, width - step, 1)
-        behind = pltpu.roll(value, step, 1)
-        value = value + jnp.where((lane & step) != 0, behind, ahead)
-        step //= 2
-    return value
+    parts = []
+    for start in range(0, value.shape[1], LANES):
+        part = value[:, start : start + LANES]
+        lane = lax.broadcasted_iota(jnp.int32, part.shape, 1)
+        step = tokens // 2
+        while step:
+            ahead = pltpu.roll(part, LANES - step, 1)
+            behind = pltpu.roll(part, step, 1)
+            part = part + jnp.where((lane & step) != 0, behind, ahead)
+            step //= 2
+        parts.append(part)
+    return jnp.concatenate(parts, axis=1)
 
 
 def mate_body(page, query, smooth_c, powers_ref, total_ref, smooth_ref, stats):
@@ -156,14 +160,19 @@
     mix_pages(far_page, powers_d, mixed_d_ref)
 
 
+def loss_of(scores, positive):
+    flags = [(positive == float(offset)).astype(jnp.float32) for offset in range(4)]
+    positive_score = sum(flag * score for flag, score in zip(flags, scores))
+    return sum((1.0 - flag) * jax.nn.softplus(score - positive_score) for flag, score in zip(flags, scores))
+
+
 def slopes_of(scores, positive):
     flags = [(positive == float(offset)).astype(jnp.float32) for offset in range(4)]
     positive_score = sum(flag * score for flag, score in zip(flags, scores))
     margins = [score - positive_score for score in scores]
-    loss = sum((1.0 - flag) * jax.nn.softplus(margin) for flag, margin in zip(flags, margins))
     terms = [(1.0 - flag) * jax.nn.sigmoid(margin) for flag, margin in zip(flags, margins)]
     total = sum(terms)
-    return loss, [term - flag * total for flag, term in zip(flags, terms)]
+    return [term - flag * total for flag, term in zip(flags, terms)]
 
 
 def to_short(value):
@@ -191,35 +200,44 @@
         ref[start : start + PAD, :] = tail
 
 
-def send_last_body(message, arrived, total_a, total_c, total_d, total_b, mate_query_t, powers_b,
-                   out_ref, loss_ref, weight_ref):
-    even = lax.axis_index("dp") % 2 == 0
+def is_even():
+    return lax.axis_index("dp") % 2 == 0
+
+
+def own_scores(even, own, mate):
+    return [own[0:1], jnp.where(even, mate[2:3], mate[3:4]), own[1:2], jnp.where(even, mate[3:4], mate[2:3])]
+
+
+def send_far_body(message, arrived, total_a, total_c, total_d, total_b, query_t, mate_query_t, powers_c, powers_d,
+                  out_ref, weight_ref):
+    even = is_even()
     own = message[...]
     mate = arrived[...]
-    loss, slopes = slopes_of(
-        [own[0:1], jnp.where(even, mate[2:3], mate[3:4]), own[1:2], jnp.where(even, mate[3:4], mate[2:3])], own[4:5])
-    _, mate_slopes = slopes_of(
+    slopes = slopes_of(own_scores(even, own, mate), own[4:5])
+    mate_slopes = slopes_of(
         [mate[0:1], jnp.where(even, own[3:4], own[2:3]), mate[1:2], jnp.where(even, own[2:3], own[3:4])], mate[4:5])
-    loss_ref[...] = loss
-    weight_b = jnp.where(even, mate_slopes[1], mate_slopes[3]) / total_b[...]
+    weight_c = slopes[2] / total_c[...]
+    weight_d = jnp.where(even, mate_slopes[3], mate_slopes[1]) / total_d[...]
     weight_ref[0:1, :] = slopes[0] / total_a[...]
-    weight_ref[1:2, :] = weight_b
-    weight_ref[2:3, :] = slopes[2] / total_c[...]
-    weight_ref[3:4, :] = jnp.where(even, mate_slopes[3], mate_slopes[1]) / total_d[...]
-    put_short(out_ref, page_terms(mate_query_t, weight_b, powers_b).T)
-
-
-def send_far_body(weight, query_t, mate_query_t, powers_c, powers_d, out_ref):
-    term = page_terms(query_t, weight[2:3, :], powers_c) + page_terms(mate_query_t, weight[3:4, :], powers_d)
+    weight_ref[1:2, :] = jnp.where(even, mate_slopes[1], mate_slopes[3]) / total_b[...]
+    weight_ref[2:3, :] = weight_c
+    weight_ref[3:4, :] = weight_d
+    term = page_terms(query_t, weight_c, powers_c) + page_terms(mate_query_t, weight_d, powers_d)
     put_short(out_ref, term.T)
 
 
-def send_query_body(tokens, weight, last_page, powers_b, mixed_d, loss_all, out_ref, loss_ref):
+def send_last_body(weight, mate_query_t, powers_b, out_ref):
+    put_short(out_ref, page_terms(mate_query_t, weight[1:2, :], powers_b).T)
+
+
+def send_query_body(tokens, weight, last_page, powers_b, mixed_d, message, arrived, out_ref, loss_ref):
+    own = message[...]
+    loss = loss_of(own_scores(is_even(), own, arrived[...]), own[4:5])
     mixed_b = jnp.dot(powers_b[...], last_page[...], preferred_element_type=jnp.float32)
     columns = weight_columns(weight)
     put_short(out_ref, mixed_b * columns[:, 1:2] + mixed_d[...] * columns[:, 3:4])
-    token, query = of_token((loss_ref.shape[1], loss_all.shape[1]), 1, tokens)
-    loss_ref[...] = jnp.sum(jnp.where(token == query * tokens, loss_all[...], 0.0), axis=1, keepdims=True).T
+    token, query = of_token((loss_ref.shape[1], loss.shape[1]), 1, tokens)
+    loss_ref[...] = jnp.sum(jnp.where(token == query * tokens, loss, 0.0), axis=1, keepdims=True).T
 
 
 def keep_body(weight, query_t, powers_a, mixed_a, mixed_c, page_ref, query_ref):
@@ -235,13 +253,13 @@
     refs[-1][...] = total
 
 
-def last_sums_body(query_own, query_in, loss_row, page_own, far_in, last_in, query_ref, loss_ref, page_ref):
+def last_sums_body(query_own, query_in, loss_row, page_own, last_in, far_in, query_ref, loss_ref, page_ref):
     sum_body(query_own, query_in, query_ref)
     loss_ref[...] = loss_row[0, :]
     sum_body(page_own, far_in, last_in, page_ref)
 
 
-def last_sums(query_own, query_in, loss_row, page_own, far_in, last_in):
+def last_sums(query_own, query_in, loss_row, page_own, last_in, far_in):
     shapes = (query_own.shape, loss_row.shape[1:], page_own.shape)
     return pl.pallas_call(
         last_sums_body,
@@ -251,7 +269,7 @@
         compiler_params=pltpu.CompilerParams(vmem_limit_bytes=4 * MIB),
         cost_estimate=pl.CostEstimate(flops=1000, bytes_accessed=1000, transcendentals=0),
         name="last_sums",
-    )(query_own, query_in, loss_row, page_own, far_in, last_in)
+    )(query_own, query_in, loss_row, page_own, last_in, far_in)
 
 
 def in_hbm(value):
@@ -294,24 +312,24 @@
     mixed_c, mixed_d, mate_query_t = on_core(
         mix_body, [((rows, width), f32)] * 2 + [((width, rows), bf16)],
         (far_page, mate_query, powers_c, powers_d), 2 * unit, "mixes")
-    last_out, loss_all, weight = on_core(
-        send_last_body,
-        [((patches + 4 * PAD, width), i16), ((1, rows), f32), ((4, rows), f32)],
-        (message, arrived, total_a, total_c, total_d, total_b, mate_query_t, powers_b), unit, "send_last")
+    far_out, weight = on_core(
+        send_far_body,
+        [((patches + 4 * PAD, width), i16), ((4, rows), f32)],
+        (message, arrived, total_a, total_c, total_d, total_b, query_t, mate_query_t, powers_c, powers_d),
+        2 * unit, "send_far")
+    far_in = passed_along(far_out, "dp", -2)
+    last_out, = on_core(
+        send_last_body, [((patches + 3 * PAD, width), i16)], (weight, mate_query_t, powers_b), unit, "send_last")
     last_in = odd_passed_along(last_out, "dp", -4)
-    far_out, = on_core(
-        send_far_body, [((patches + 3 * PAD, width), i16)],
-        (weight, query_t, mate_query_t, powers_c, powers_d), 2 * unit, "send_far")
-    far_in = passed_along(far_out, "dp", -2)
     query_out, loss = on_core(
         functools.partial(send_query_body, tokens),
         [((rows + PAD, width), i16), ((1, count), f32)],
-        (weight, last_page, powers_b, mixed_d, loss_all), 1000, "send_query")
+        (weight, last_page, powers_b, mixed_d, message, arrived), 1000, "send_query")
     query_in = swapped(query_out, "dp")
     page_own, query_own = on_core(
         keep_body, [((patches, width), f32), ((rows, width), f32)],
         (weight, query_t, powers_a, mixed_a, mixed_c), 1000, "own_terms")
-    query_grad, loss, page_grad = last_sums(query_own, query_in, loss, page_own, far_in, last_in)
+    query_grad, loss, page_grad = last_sums(query_own, query_in, loss, page_own, last_in, far_in)
     return (loss, query_grad.reshape(count, tokens, width), page_grad[None])
 
 

time: 48.7 us -> 47.5 us (0.975)
  starting transfers between devices: 25 us -> 24.4 us
    ppermute x2, starting transfers between devices: 7.91 us -> 6.33 us  [passed_along(): return lax.ppermute(value, axis, pairs)]
    ppermute x2, starting transfers between devices: 5.59 us -> 6.59 us  [odd_passed_along(): return lax.ppermute(value, axis, pairs)]
  transfers between devices with their start and end apart: 7 -> 7, of which waited for: 4 -> 3; matrix products, arithmetic and copies ran while one was open for 0% -> 0% of each run, Pallas kernels for 19% -> 19%
where the time goes in v5:
time: 47.5 us; the launch traced here: 47.2 us
  starting transfers between devices  24.4 us (51%)
  Pallas kernels  12.5 us (26%)
  waiting for transfers between devices  9.64 us (20%)
  between operations  0.75 us (2%)
    pallas_call x9, Pallas kernels, on_core(): pl.pallas_call(body, out_shape=[pltpu.VMEM(shape, dtype) for shape, dtype...  11.4 us
    ppermute x3, starting transfers between devices, swapped(): lax.ppermute(value, axis, [(source, source ^ 1) for source in range(lax.a...  11.4 us
    ppermute x2, waiting for transfers between devices, passed_along(): return lax.ppermute(value, axis, pairs)  7.52 us
    ppermute x2, starting transfers between devices, odd_passed_along(): return lax.ppermute(value, axis, pairs)  6.59 us
    ppermute x2, starting transfers between devices, passed_along(): return lax.ppermute(value, axis, pairs)  6.33 us
    ppermute x2, waiting for transfers between devices, odd_passed_along(): return lax.ppermute(value, axis, pairs)  1.37 us
    pallas_call x1, Pallas kernels, last_sums(): pl.pallas_call(last_sums_body, out_shape=[jax.ShapeDtypeStruct(shape, jnp...  1.05 us
  transfers between devices with their start and end apart: 7, of which 3 were waited for; matrix products, arithmetic and copies ran while one was open for 0% of the time, Pallas kernels for 19%

profile of v5, /device:TPU:1, one launch (start us, length us, event | category | flops | bytes accessed | tf_op | source)
XLA Modules:
  0.0 47.2 jit_solution(4243508083075529860)
XLA Ops:
  0.6 4.0 %collective-permute-start.2 = (bf16[1024,128]{1,0:T(8,128)(2,1)}, bf16[1024,128]{1,0:T(8,128)(2,1)S(1)}, u32[]{:S(2)}, u32[]{:S(2)}) collective-permute-start(bf16[1024,128]{1,0:T(8,128)(2,1)} %bitcast.9), channel_id=1, source_target_pairs={{0,2},{1,3},{2,4},{3,5},{4,6},{5,7},{6,8},{7,9},{8,10},{9,11},{10,... | collective-permute-start | bytes 786440 | tf_op jit(solution)/shard_map/ppermute | solution.py:27
  4.7 6.7 %collective-permute-start.1 = (bf16[1024,128]{1,0:T(8,128)(2,1)}, bf16[1024,128]{1,0:T(8,128)(2,1)S(1)}, u32[]{:S(2)}, u32[]{:S(2)}) collective-permute-start(bf16[1024,128]{1,0:T(8,128)(2,1)} %bitcast.7), channel_id=1, source_target_pairs={{0,1},{1,0},{2,3},{3,2},{4,5},{5,4},{6,7},{7,6},{8,9},{9,8},{10,11... | collective-permute-start | bytes 786440 | tf_op jit(solution)/shard_map/ppermute | solution.py:37
  11.4 1.9 %collective-permute-start = (bf16[1024,128]{1,0:T(8,128)(2,1)}, bf16[1024,128]{1,0:T(8,128)(2,1)S(1)}, u32[]{:S(2)}, u32[]{:S(2)}) collective-permute-start(bf16[1024,128]{1,0:T(8,128)(2,1)} %bitcast.10), channel_id=1, source_target_pairs={{0,0},{1,5},{2,2},{3,7},{4,4},{5,9},{6,6},{7,11},{8,8},{9,13},{10,... | collective-permute-start | bytes 786440 | tf_op jit(solution)/shard_map/ppermute | solution.py:33
  13.3 2.7 %own_unit.1 = (bf16[1024,1024]{1,0:T(8,128)(2,1)S(1)}, f32[1024,128]{1,0:T(8,128)S(1)}, f32[1,1024]{1,0:T(1,128)S(1)}, f32[1,1024]{1,0:T(1,128)S(1)}, bf16[128,1...) custom-call(bf16[1024,128]{1,0:T(8,128)(2,1)} %bitcast.11, bf16[1024,128]{1,0:T(8,128)(2,1)} %bitcast.8, ...), custom_call_target="tpu_custom_call" | custom-call | flops 536870912 | bytes 2097152 | tf_op jit(solution)/shard_map/own_unit/pallas_call | solution.py:41
  15.9 7.5 %collective-permute-done.2.page.far_page = bf16[1024,128]{1,0:T(8,128)(2,1)S(1)} collective-permute-done((bf16[1024,128]{1,0:T(8,128)(2,1)}, bf16[1024,128]{1,0:T(8,128)(2,1)S(1)}, u32[]{:S(2)}, u32[]{:S(2)}) %collective-permute-start.2) | collective-permute-done | bytes 262176 | tf_op jit(solution)/shard_map/ppermute | solution.py:27
  23.5 1.3 %far_unit.1 = (bf16[1024,1024]{1,0:T(8,128)(2,1)S(1)}, f32[1,1024]{1,0:T(1,128)S(1)}, f32[1,1024]{1,0:T(1,128)S(1)}) custom-call(bf16[1024,128]{1,0:T(8,128)(2,1)S(1)} %collective-permute-done.2.page.far_page, bf16[1024,128]{1,0:T(8,128)(2,1)S(1)} %get-tuple-element.32.query), custom_call_target="tpu_custom_call" | custom-call | flops 268435456 | bytes 2097152 | tf_op jit(solution)/shard_map/far_unit/pallas_call | solution.py:41
  24.7 0.0 collective-permute-done.1.query.mate_query
  24.8 1.3 %mate_unit.1 = (bf16[1024,1024]{1,0:T(8,128)(2,1)S(1)}, f32[1,1024]{1,0:T(1,128)S(1)}, f32[2,1024]{1,0:T(2,128)S(1)}) custom-call(bf16[1024,128]{1,0:T(8,128)(2,1)S(1)} %collective-permute-done.2.page.far_page, bf16[1024,128]{1,0:T(8,128)(2,1)S(1)} %collective-permute-done.1.query.mate_query, f32[1,1024]{1,0:T(1,128)S(1)} %get-tuple-element.33.smooth_c), custom_call_target="tpu_custom_call" | custom-call | flops 268435456 | bytes 2097152 | tf_op jit(solution)/shard_map/mate_unit/pallas_call | solution.py:41
  26.0 1.4 %collective-permute-done.page.last_page = bf16[1024,128]{1,0:T(8,128)(2,1)S(1)} collective-permute-done((bf16[1024,128]{1,0:T(8,128)(2,1)}, bf16[1024,128]{1,0:T(8,128)(2,1)S(1)}, u32[]{:S(2)}, u32[]{:S(2)}) %collective-permute-start) | collective-permute-done | bytes 262176 | tf_op jit(solution)/shard_map/ppermute | solution.py:33
  27.4 1.7 %last_unit.1 = (bf16[1024,1024]{1,0:T(8,128)(2,1)S(1)}, f32[1,1024]{1,0:T(1,128)S(1)}, f32[8,1024]{1,0:T(8,128)S(1)}) custom-call(bf16[1024,128]{1,0:T(8,128)(2,1)S(1)} %collective-permute-done.page.last_page, bf16[1024,128]{1,0:T(8,128)(2,1)S(1)} %collective-permute-done.1.query.mate_query, f32[1,1024]{1,0:T(1,128)S(1)} %get-tuple-element.31.smooth_a, ...), custom_call_target="tpu_custom_call" | custom-call | flops 268435456 | bytes 2097152 | tf_op jit(solution)/shard_map/last_unit/pallas_call | solution.py:41
  29.1 2.9 %collective-permute-start.3 = (f32[8,1024]{1,0:T(8,128)S(1)}, f32[8,1024]{1,0:T(8,128)S(1)}, u32[]{:S(2)}, u32[]{:S(2)}) collective-permute-start(f32[8,1024]{1,0:T(8,128)S(1)} %get-tuple-element.36.message), channel_id=1, source_target_pairs={{0,1},{1,0},{2,3},{3,2},{4,5},{5,4},{6,7},{7,6},{8,9},{9,8},{10,11... | collective-permute-start | bytes 98312 | tf_op jit(solution)/shard_map/ppermute | solution.py:37
  32.0 1.2 %mixes.1 = (f32[1024,128]{1,0:T(8,128)S(1)}, f32[1024,128]{1,0:T(8,128)S(1)}, bf16[128,1024]{1,0:T(8,128)(2,1)S(1)}) custom-call(bf16[1024,128]{1,0:T(8,128)(2,1)S(1)} %collective-permute-done.2.page.far_page, bf16[1024,128]{1,0:T(8,128)(2,1)S(1)} %collective-permute-done.1.query.mate_query, bf16[1024,1024]{1,0:T(8,128)(2,1)S(1)} %get-tuple-element.42.powers_c, ...), custom_call_target="tpu_custom_call" | custom-call | flops 536870912 | bytes 2097152 | tf_op jit(solution)/shard_map/mixes/pallas_call | solution.py:41
  33.2 0.0 collective-permute-done.3.arrived
  33.2 1.0 %send_far.1 = (s16[1088,128]{1,0:T(8,128)(2,1)S(1)}, f32[4,1024]{1,0:T(4,128)S(1)}) custom-call(f32[8,1024]{1,0:T(8,128)S(1)} %get-tuple-element.36.message, f32[8,1024]{1,0:T(8,128)S(1)} %collective-permute-done.3.arrived, f32[1,1024]{1,0:T(1,128)S(1)} %get-tuple-element.37.total_a, f32[1,1024]{1,0:T(1,128)S(1)} %get-tuple-element.38.total_c, ...), custom_call_target="tpu_custom_call" | custom-call | flops 536870912 | bytes 2097152 | tf_op jit(solution)/shard_map/send_far/pallas_call | solution.py:41
  34.2 2.3 %collective-permute-start.6 = (s16[1088,128]{1,0:T(8,128)(2,1)S(1)}, s16[1088,128]{1,0:T(8,128)(2,1)S(1)}, u32[]{:S(2)}, u32[]{:S(2)}) collective-permute-start(s16[1088,128]{1,0:T(8,128)(2,1)S(1)} %get-tuple-element.55), channel_id=1, source_target_pairs={{0,510},{1,511},{2,0},{3,1},{4,2},{5,3},{6,4},{7,5},{8,6},{9,7},{1... | collective-permute-start | bytes 835592 | tf_op jit(solution)/shard_map/ppermute | solution.py:27
  36.5 0.7 %send_last.1 = s16[1072,128]{1,0:T(8,128)(2,1)S(1)} custom-call(f32[4,1024]{1,0:T(4,128)S(1)} %get-tuple-element.45.weight, bf16[128,1024]{1,0:T(8,128)(2,1)S(1)} %get-tuple-element.44.mate_query_t, bf16[1024,1024]{1,0:T(8,128)(2,1)S(1)} %get-tuple-element.50.powers_b), custom_call_target="tpu_custom_call" | custom-call | flops 268435456 | bytes 2097152 | tf_op jit(solution)/shard_map/send_last/pallas_call | solution.py:41
  37.2 4.7 %collective-permute-start.5 = (s16[1072,128]{1,0:T(8,128)(2,1)S(1)}, s16[1072,128]{1,0:T(8,128)(2,1)S(1)}, u32[]{:S(2)}, u32[]{:S(2)}) collective-permute-start(s16[1072,128]{1,0:T(8,128)(2,1)S(1)} %send_last.1), channel_id=1, source_target_pairs={{0,0},{1,509},{2,2},{3,511},{4,4},{5,1},{6,6},{7,3},{8,8},{9,5},{1... | collective-permute-start | bytes 823304 | tf_op jit(solution)/shard_map/ppermute | solution.py:33
  41.8 0.9 %send_query.1 = (s16[1040,128]{1,0:T(8,128)(2,1)S(1)}, f32[1,32]{1,0:T(1,128)S(1)}) custom-call(f32[4,1024]{1,0:T(4,128)S(1)} %get-tuple-element.45.weight, bf16[1024,128]{1,0:T(8,128)(2,1)S(1)} %collective-permute-done.page.last_page, bf16[1024,1024]{1,0:T(8,128)(2,1)S(1)} %get-tuple-element.50.powers_b, f32[1024,128]{1,0:T(8,128)S(1)} %get-tuple-element.51.mixed_d, ...), custom_call_target="tpu_custom_call" | custom-call | flops 1000 | bytes 2097152 | tf_op jit(solution)/shard_map/send_query/pallas_call | solution.py:41
  42.8 1.9 %collective-permute-start.4 = (s16[1040,128]{1,0:T(8,128)(2,1)S(1)}, s16[1040,128]{1,0:T(8,128)(2,1)S(1)}, u32[]{:S(2)}, u32[]{:S(2)}) collective-permute-start(s16[1040,128]{1,0:T(8,128)(2,1)S(1)} %get-tuple-element.52), channel_id=1, source_target_pairs={{0,1},{1,0},{2,3},{3,2},{4,5},{5,4},{6,7},{7,6},{8,9},{9,8},{10,11... | collective-permute-start | bytes 798728 | tf_op jit(solution)/shard_map/ppermute | solution.py:37
  44.7 0.8 %own_terms.1 = (f32[1024,128]{1,0:T(8,128)S(1)}, f32[1024,128]{1,0:T(8,128)S(1)}) custom-call(f32[4,1024]{1,0:T(4,128)S(1)} %get-tuple-element.45.weight, bf16[128,1024]{1,0:T(8,128)(2,1)S(1)} %get-tuple-element.41.query_t, bf16[1024,1024]{1,0:T(8,128)(2,1)S(1)} %get-tuple-element.46.powers_a, f32[1024,128]{1,0:T(8,128)S(1)} %get-tuple-element.47.mixed_a, ...), custom_call_target="tpu_custom_call" | custom-call | flops 1000 | bytes 2097152 | tf_op jit(solution)/shard_map/own_terms/pallas_call | solution.py:41
  45.5 0.7 %collective-permute-done.4.query_in = s16[1040,128]{1,0:T(8,128)(2,1)S(1)} collective-permute-done((s16[1040,128]{1,0:T(8,128)(2,1)S(1)}, s16[1040,128]{1,0:T(8,128)(2,1)S(1)}, u32[]{:S(2)}, u32[]{:S(2)}) %collective-permute-start.4) | collective-permute-done | bytes 266272 | tf_op jit(solution)/shard_map/ppermute | solution.py:37
  46.2 0.0 collective-permute-done.5.last_in
  46.2 0.0 collective-permute-done.6.far_in
  46.2 1.0 %last_sums.1 = (f32[1024,128]{1,0:T(8,128)}, f32[32]{0:T(128)}, f32[1024,128]{1,0:T(8,128)}) custom-call(f32[1024,128]{1,0:T(8,128)S(1)} %get-tuple-element.49.query_own, s16[1040,128]{1,0:T(8,128)(2,1)S(1)} %collective-permute-done.4.query_in, f32[1,32]{1,0:T(1,128)S(1)} %get-tuple-element.53.loss_row, f32[1024,128]{1,0:T(8,128)S(1)} %get-tuple-element.54.page_own, ...), custom_call_target="tpu_custom_call" | custom-call | flops 1000 | bytes 1000 | tf_op jit(solution)/shard_map/last_sums/pallas_call | solution.py:264
Async XLA Ops:
  0.6 22.8 %collective-permute-start.2 = (bf16[1024,128]{1,0:T(8,128)(2,1)}, bf16[1024,128]{1,0:T(8,128)(2,1)S(1)}, u32[]{:S(2)}, u32[]{:S(2)}) collective-permute-start(bf16[1024,128]{1,0:T(8,128)(2,1)} %bitcast.9), channel_id=1, source_target_pairs={{0,2},{1,3},{2,4},{3,5},{4,6},{5,7},{6,8},{7,9},{8,10},{9,11},{10,... | collective-permute-start | bytes 786440 | tf_op jit(solution)/shard_map/ppermute | solution.py:27
  4.7 20.1 %collective-permute-start.1 = (bf16[1024,128]{1,0:T(8,128)(2,1)}, bf16[1024,128]{1,0:T(8,128)(2,1)S(1)}, u32[]{:S(2)}, u32[]{:S(2)}) collective-permute-start(bf16[1024,128]{1,0:T(8,128)(2,1)} %bitcast.7), channel_id=1, source_target_pairs={{0,1},{1,0},{2,3},{3,2},{4,5},{5,4},{6,7},{7,6},{8,9},{9,8},{10,11... | collective-permute-start | bytes 786440 | tf_op jit(solution)/shard_map/ppermute | solution.py:37
  11.4 16.1 %collective-permute-start = (bf16[1024,128]{1,0:T(8,128)(2,1)}, bf16[1024,128]{1,0:T(8,128)(2,1)S(1)}, u32[]{:S(2)}, u32[]{:S(2)}) collective-permute-start(bf16[1024,128]{1,0:T(8,128)(2,1)} %bitcast.10), channel_id=1, source_target_pairs={{0,0},{1,5},{2,2},{3,7},{4,4},{5,9},{6,6},{7,11},{8,8},{9,13},{10,... | collective-permute-start | bytes 786440 | tf_op jit(solution)/shard_map/ppermute | solution.py:33
  29.1 4.1 %collective-permute-start.3 = (f32[8,1024]{1,0:T(8,128)S(1)}, f32[8,1024]{1,0:T(8,128)S(1)}, u32[]{:S(2)}, u32[]{:S(2)}) collective-permute-start(f32[8,1024]{1,0:T(8,128)S(1)} %get-tuple-element.36.message), channel_id=1, source_target_pairs={{0,1},{1,0},{2,3},{3,2},{4,5},{5,4},{6,7},{7,6},{8,9},{9,8},{10,11... | collective-permute-start | bytes 98312 | tf_op jit(solution)/shard_map/ppermute | solution.py:37
  34.2 12.0 %collective-permute-start.6 = (s16[1088,128]{1,0:T(8,128)(2,1)S(1)}, s16[1088,128]{1,0:T(8,128)(2,1)S(1)}, u32[]{:S(2)}, u32[]{:S(2)}) collective-permute-start(s16[1088,128]{1,0:T(8,128)(2,1)S(1)} %get-tuple-element.55), channel_id=1, source_target_pairs={{0,510},{1,511},{2,0},{3,1},{4,2},{5,3},{6,4},{7,5},{8,6},{9,7},{1... | collective-permute-start | bytes 835592 | tf_op jit(solution)/shard_map/ppermute | solution.py:27
  37.2 9.0 %collective-permute-start.5 = (s16[1072,128]{1,0:T(8,128)(2,1)S(1)}, s16[1072,128]{1,0:T(8,128)(2,1)S(1)}, u32[]{:S(2)}, u32[]{:S(2)}) collective-permute-start(s16[1072,128]{1,0:T(8,128)(2,1)S(1)} %send_last.1), channel_id=1, source_target_pairs={{0,0},{1,509},{2,2},{3,511},{4,4},{5,1},{6,6},{7,3},{8,8},{9,5},{1... | collective-permute-start | bytes 823304 | tf_op jit(solution)/shard_map/ppermute | solution.py:33
  42.8 3.4 %collective-permute-start.4 = (s16[1040,128]{1,0:T(8,128)(2,1)S(1)}, s16[1040,128]{1,0:T(8,128)(2,1)S(1)}, u32[]{:S(2)}, u32[]{:S(2)}) collective-permute-start(s16[1040,128]{1,0:T(8,128)(2,1)S(1)} %get-tuple-element.52), channel_id=1, source_target_pairs={{0,1},{1,0},{2,3},{3,2},{4,5},{5,4},{6,7},{7,6},{8,9},{9,8},{10,11... | collective-permute-start | bytes 798728 | tf_op jit(solution)/shard_map/ppermute | solution.py:37

commit v6 on v5

--- a/solution.py
+++ b/solution.py
@@ -154,10 +154,10 @@
     message_ref[5:8, :] = sums[0:3, :]
 
 
-def mix_body(far_page, mate_query, powers_c, powers_d, mixed_c_ref, mixed_d_ref, mate_query_t_ref):
+def mix_body(far_page, last_page, mate_query, powers_d, powers_b, mixed_d_ref, mixed_b_ref, mate_query_t_ref):
     mate_query_t_ref[...] = turned(mate_query[...])
-    mix_pages(far_page, powers_c, mixed_c_ref)
     mix_pages(far_page, powers_d, mixed_d_ref)
+    mix_pages(last_page, powers_b, mixed_b_ref)
 
 
 def loss_of(scores, positive):
@@ -230,20 +230,21 @@
     put_short(out_ref, page_terms(mate_query_t, weight[1:2, :], powers_b).T)
 
 
-def send_query_body(tokens, weight, last_page, powers_b, mixed_d, message, arrived, out_ref, loss_ref):
+def send_query_body(weight, mixed_b, mixed_d, out_ref):
+    columns = weight_columns(weight)
+    put_short(out_ref, mixed_b[...] * columns[:, 1:2] + mixed_d[...] * columns[:, 3:4])
+
+
+def keep_body(tokens, weight, query_t, powers_a, mixed_a, far_page, powers_c, message, arrived,
+              page_ref, query_ref, loss_ref):
+    columns = weight_columns(weight)
+    page_ref[...] = page_terms(query_t, weight[0:1, :], powers_a).T
+    mixed_c = jnp.dot(powers_c[...], far_page[...], preferred_element_type=jnp.float32)
+    query_ref[...] = mixed_a[...] * columns[:, 0:1] + mixed_c * columns[:, 2:3]
     own = message[...]
     loss = loss_of(own_scores(is_even(), own, arrived[...]), own[4:5])
-    mixed_b = jnp.dot(powers_b[...], last_page[...], preferred_element_type=jnp.float32)
-    columns = weight_columns(weight)
-    put_short(out_ref, mixed_b * columns[:, 1:2] + mixed_d[...] * columns[:, 3:4])
     token, query = of_token((loss_ref.shape[1], loss.shape[1]), 1, tokens)
     loss_ref[...] = jnp.sum(jnp.where(token == query * tokens, loss, 0.0), axis=1, keepdims=True).T
-
-
-def keep_body(weight, query_t, powers_a, mixed_a, mixed_c, page_ref, query_ref):
-    columns = weight_columns(weight)
-    page_ref[...] = page_terms(query_t, weight[0:1, :], powers_a).T
-    query_ref[...] = mixed_a[...] * columns[:, 0:1] + mixed_c[...] * columns[:, 2:3]
 
 
 def sum_body(own, *refs):
@@ -309,9 +310,9 @@
         (last_page, mate_query, smooth_a, smooth_far, positive), unit, "last_unit",
         scratch=[pltpu.VMEM((rows, COLUMNS), f32)])
     arrived = swapped(message, "dp")
-    mixed_c, mixed_d, mate_query_t = on_core(
+    mixed_d, mixed_b, mate_query_t = on_core(
         mix_body, [((rows, width), f32)] * 2 + [((width, rows), bf16)],
-        (far_page, mate_query, powers_c, powers_d), 2 * unit, "mixes")
+        (far_page, last_page, mate_query, powers_d, powers_b), 2 * unit, "mixes")
     far_out, weight = on_core(
         send_far_body,
         [((patches + 4 * PAD, width), i16), ((4, rows), f32)],
@@ -321,14 +322,13 @@
     last_out, = on_core(
         send_last_body, [((patches + 3 * PAD, width), i16)], (weight, mate_query_t, powers_b), unit, "send_last")
     last_in = odd_passed_along(last_out, "dp", -4)
-    query_out, loss = on_core(
-        functools.partial(send_query_body, tokens),
-        [((rows + PAD, width), i16), ((1, count), f32)],
-        (weight, last_page, powers_b, mixed_d, message, arrived), 1000, "send_query")
+    query_out, = on_core(
+        send_query_body, [((rows + PAD, width), i16)], (weight, mixed_b, mixed_d), 1000, "send_query")
     query_in = swapped(query_out, "dp")
-    page_own, query_own = on_core(
-        keep_body, [((patches, width), f32), ((rows, width), f32)],
-        (weight, query_t, powers_a, mixed_a, mixed_c), 1000, "own_terms")
+    page_own, query_own, loss = on_core(
+        functools.partial(keep_body, tokens),
+        [((patches, width), f32), ((rows, width), f32), ((1, count), f32)],
+        (weight, query_t, powers_a, mixed_a, far_page, powers_c, message, arrived), 1000, "own_terms")
     query_grad, loss, page_grad = last_sums(query_own, query_in, loss, page_own, last_in, far_in)
     return (loss, query_grad.reshape(count, tokens, width), page_grad[None])
 

time: 47.5 us -> 47.4 us (level)
  transfers between devices with their start and end apart: 7 -> 7, of which waited for: 3 -> 4; matrix products, arithmetic and copies ran while one was open for 0% -> 0% of each run, Pallas kernels for 19% -> 19%
where the time goes in v6:
time: 47.4 us; the launch traced here: 47.1 us
  starting transfers between devices  24.4 us (51%)
  Pallas kernels  12.7 us (27%)
  waiting for transfers between devices  9.29 us (20%)
  between operations  0.75 us (2%)
    pallas_call x9, Pallas kernels, on_core(): pl.pallas_call(body, out_shape=[pltpu.VMEM(shape, dtype) for shape, dtype...  11.6 us
    ppermute x3, starting transfers between devices, swapped(): lax.ppermute(value, axis, [(source, source ^ 1) for source in range(lax.a...  11.5 us
    ppermute x2, waiting for transfers between devices, passed_along(): return lax.ppermute(value, axis, pairs)  7.52 us
    ppermute x2, starting transfers between devices, odd_passed_along(): return lax.ppermute(value, axis, pairs)  6.51 us
    ppermute x2, starting transfers between devices, passed_along(): return lax.ppermute(value, axis, pairs)  6.33 us
    ppermute x2, waiting for transfers between devices, odd_passed_along(): return lax.ppermute(value, axis, pairs)  1.39 us
    pallas_call x1, Pallas kernels, last_sums(): pl.pallas_call(last_sums_body, out_shape=[jax.ShapeDtypeStruct(shape, jnp...  1.04 us
  transfers between devices with their start and end apart: 7, of which 4 were waited for; matrix products, arithmetic and copies ran while one was open for 0% of the time, Pallas kernels for 19%

profile of v6, /device:TPU:1, one launch (start us, length us, event | category | flops | bytes accessed | tf_op | source)
XLA Modules:
  0.0 47.1 jit_solution(16535715998862352597)
XLA Ops:
  0.6 4.0 %collective-permute-start.2 = (bf16[1024,128]{1,0:T(8,128)(2,1)}, bf16[1024,128]{1,0:T(8,128)(2,1)S(1)}, u32[]{:S(2)}, u32[]{:S(2)}) collective-permute-start(bf16[1024,128]{1,0:T(8,128)(2,1)} %bitcast.9), channel_id=1, source_target_pairs={{0,2},{1,3},{2,4},{3,5},{4,6},{5,7},{6,8},{7,9},{8,10},{9,11},{10,... | collective-permute-start | bytes 786440 | tf_op jit(solution)/shard_map/ppermute | solution.py:27
  4.7 6.7 %collective-permute-start.1 = (bf16[1024,128]{1,0:T(8,128)(2,1)}, bf16[1024,128]{1,0:T(8,128)(2,1)S(1)}, u32[]{:S(2)}, u32[]{:S(2)}) collective-permute-start(bf16[1024,128]{1,0:T(8,128)(2,1)} %bitcast.7), channel_id=1, source_target_pairs={{0,1},{1,0},{2,3},{3,2},{4,5},{5,4},{6,7},{7,6},{8,9},{9,8},{10,11... | collective-permute-start | bytes 786440 | tf_op jit(solution)/shard_map/ppermute | solution.py:37
  11.4 1.9 %collective-permute-start = (bf16[1024,128]{1,0:T(8,128)(2,1)}, bf16[1024,128]{1,0:T(8,128)(2,1)S(1)}, u32[]{:S(2)}, u32[]{:S(2)}) collective-permute-start(bf16[1024,128]{1,0:T(8,128)(2,1)} %bitcast.10), channel_id=1, source_target_pairs={{0,0},{1,5},{2,2},{3,7},{4,4},{5,9},{6,6},{7,11},{8,8},{9,13},{10,... | collective-permute-start | bytes 786440 | tf_op jit(solution)/shard_map/ppermute | solution.py:33
  13.3 2.7 %own_unit.1 = (bf16[1024,1024]{1,0:T(8,128)(2,1)S(1)}, f32[1024,128]{1,0:T(8,128)S(1)}, f32[1,1024]{1,0:T(1,128)S(1)}, f32[1,1024]{1,0:T(1,128)S(1)}, bf16[128,1...) custom-call(bf16[1024,128]{1,0:T(8,128)(2,1)} %bitcast.11, bf16[1024,128]{1,0:T(8,128)(2,1)} %bitcast.8, ...), custom_call_target="tpu_custom_call" | custom-call | flops 536870912 | bytes 2097152 | tf_op jit(solution)/shard_map/own_unit/pallas_call | solution.py:41
  15.9 7.5 %collective-permute-done.2.page.far_page = bf16[1024,128]{1,0:T(8,128)(2,1)S(1)} collective-permute-done((bf16[1024,128]{1,0:T(8,128)(2,1)}, bf16[1024,128]{1,0:T(8,128)(2,1)S(1)}, u32[]{:S(2)}, u32[]{:S(2)}) %collective-permute-start.2) | collective-permute-done | bytes 262176 | tf_op jit(solution)/shard_map/ppermute | solution.py:27
  23.5 1.3 %far_unit.1 = (bf16[1024,1024]{1,0:T(8,128)(2,1)S(1)}, f32[1,1024]{1,0:T(1,128)S(1)}, f32[1,1024]{1,0:T(1,128)S(1)}) custom-call(bf16[1024,128]{1,0:T(8,128)(2,1)S(1)} %collective-permute-done.2.page.far_page, bf16[1024,128]{1,0:T(8,128)(2,1)S(1)} %get-tuple-element.31.query), custom_call_target="tpu_custom_call" | custom-call | flops 268435456 | bytes 2097152 | tf_op jit(solution)/shard_map/far_unit/pallas_call | solution.py:41
  24.8 0.0 collective-permute-done.1.query.mate_query
  24.8 1.3 %mate_unit.1 = (bf16[1024,1024]{1,0:T(8,128)(2,1)S(1)}, f32[1,1024]{1,0:T(1,128)S(1)}, f32[2,1024]{1,0:T(2,128)S(1)}) custom-call(bf16[1024,128]{1,0:T(8,128)(2,1)S(1)} %collective-permute-done.2.page.far_page, bf16[1024,128]{1,0:T(8,128)(2,1)S(1)} %collective-permute-done.1.query.mate_query, f32[1,1024]{1,0:T(1,128)S(1)} %get-tuple-element.32.smooth_c), custom_call_target="tpu_custom_call" | custom-call | flops 268435456 | bytes 2097152 | tf_op jit(solution)/shard_map/mate_unit/pallas_call | solution.py:41
  26.1 1.3 %collective-permute-done.page.last_page = bf16[1024,128]{1,0:T(8,128)(2,1)S(1)} collective-permute-done((bf16[1024,128]{1,0:T(8,128)(2,1)}, bf16[1024,128]{1,0:T(8,128)(2,1)S(1)}, u32[]{:S(2)}, u32[]{:S(2)}) %collective-permute-start) | collective-permute-done | bytes 262176 | tf_op jit(solution)/shard_map/ppermute | solution.py:33
  27.4 1.7 %last_unit.1 = (bf16[1024,1024]{1,0:T(8,128)(2,1)S(1)}, f32[1,1024]{1,0:T(1,128)S(1)}, f32[8,1024]{1,0:T(8,128)S(1)}) custom-call(bf16[1024,128]{1,0:T(8,128)(2,1)S(1)} %collective-permute-done.page.last_page, bf16[1024,128]{1,0:T(8,128)(2,1)S(1)} %collective-permute-done.1.query.mate_query, f32[1,1024]{1,0:T(1,128)S(1)} %get-tuple-element.30.smooth_a, ...), custom_call_target="tpu_custom_call" | custom-call | flops 268435456 | bytes 2097152 | tf_op jit(solution)/shard_map/last_unit/pallas_call | solution.py:41
  29.1 2.9 %collective-permute-start.3 = (f32[8,1024]{1,0:T(8,128)S(1)}, f32[8,1024]{1,0:T(8,128)S(1)}, u32[]{:S(2)}, u32[]{:S(2)}) collective-permute-start(f32[8,1024]{1,0:T(8,128)S(1)} %get-tuple-element.35.message), channel_id=1, source_target_pairs={{0,1},{1,0},{2,3},{3,2},{4,5},{5,4},{6,7},{7,6},{8,9},{9,8},{10,11... | collective-permute-start | bytes 98312 | tf_op jit(solution)/shard_map/ppermute | solution.py:37
  32.1 1.2 %mixes.1 = (f32[1024,128]{1,0:T(8,128)S(1)}, f32[1024,128]{1,0:T(8,128)S(1)}, bf16[128,1024]{1,0:T(8,128)(2,1)S(1)}) custom-call(bf16[1024,128]{1,0:T(8,128)(2,1)S(1)} %collective-permute-done.2.page.far_page, bf16[1024,128]{1,0:T(8,128)(2,1)S(1)} %collective-permute-done.page.last_page, bf16[1024,128]{1,0:T(8,128)(2,1)S(1)} %collective-permute-done.1.query.mate_query, ...), custom_call_target="tpu_custom_call" | custom-call | flops 536870912 | bytes 2097152 | tf_op jit(solution)/shard_map/mixes/pallas_call | solution.py:41
  33.3 0.0 collective-permute-done.3.arrived
  33.3 1.0 %send_far.1 = (s16[1088,128]{1,0:T(8,128)(2,1)S(1)}, f32[4,1024]{1,0:T(4,128)S(1)}) custom-call(f32[8,1024]{1,0:T(8,128)S(1)} %get-tuple-element.35.message, f32[8,1024]{1,0:T(8,128)S(1)} %collective-permute-done.3.arrived, f32[1,1024]{1,0:T(1,128)S(1)} %get-tuple-element.36.total_a, f32[1,1024]{1,0:T(1,128)S(1)} %get-tuple-element.37.total_c, ...), custom_call_target="tpu_custom_call" | custom-call | flops 536870912 | bytes 2097152 | tf_op jit(solution)/shard_map/send_far/pallas_call | solution.py:41
  34.3 2.3 %collective-permute-start.6 = (s16[1088,128]{1,0:T(8,128)(2,1)S(1)}, s16[1088,128]{1,0:T(8,128)(2,1)S(1)}, u32[]{:S(2)}, u32[]{:S(2)}) collective-permute-start(s16[1088,128]{1,0:T(8,128)(2,1)S(1)} %get-tuple-element.53), channel_id=1, source_target_pairs={{0,510},{1,511},{2,0},{3,1},{4,2},{5,3},{6,4},{7,5},{8,6},{9,7},{1... | collective-permute-start | bytes 835592 | tf_op jit(solution)/shard_map/ppermute | solution.py:27
  36.6 0.7 %send_last.1 = s16[1072,128]{1,0:T(8,128)(2,1)S(1)} custom-call(f32[4,1024]{1,0:T(4,128)S(1)} %get-tuple-element.45.weight, bf16[128,1024]{1,0:T(8,128)(2,1)S(1)} %get-tuple-element.43.mate_query_t, bf16[1024,1024]{1,0:T(8,128)(2,1)S(1)} %get-tuple-element.42.powers_b), custom_call_target="tpu_custom_call" | custom-call | flops 268435456 | bytes 2097152 | tf_op jit(solution)/shard_map/send_last/pallas_call | solution.py:41
  37.3 4.6 %collective-permute-start.5 = (s16[1072,128]{1,0:T(8,128)(2,1)S(1)}, s16[1072,128]{1,0:T(8,128)(2,1)S(1)}, u32[]{:S(2)}, u32[]{:S(2)}) collective-permute-start(s16[1072,128]{1,0:T(8,128)(2,1)S(1)} %send_last.1), channel_id=1, source_target_pairs={{0,0},{1,509},{2,2},{3,511},{4,4},{5,1},{6,6},{7,3},{8,8},{9,5},{1... | collective-permute-start | bytes 823304 | tf_op jit(solution)/shard_map/ppermute | solution.py:33
  41.9 0.6 %send_query.1 = s16[1040,128]{1,0:T(8,128)(2,1)S(1)} custom-call(f32[4,1024]{1,0:T(4,128)S(1)} %get-tuple-element.45.weight, f32[1024,128]{1,0:T(8,128)S(1)} %get-tuple-element.49.mixed_b, f32[1024,128]{1,0:T(8,128)S(1)} %get-tuple-element.50.mixed_d), custom_call_target="tpu_custom_call" | custom-call | flops 1000 | bytes 2097152 | tf_op jit(solution)/shard_map/send_query/pallas_call | solution.py:41
  42.5 1.9 %collective-permute-start.4 = (s16[1040,128]{1,0:T(8,128)(2,1)S(1)}, s16[1040,128]{1,0:T(8,128)(2,1)S(1)}, u32[]{:S(2)}, u32[]{:S(2)}) collective-permute-start(s16[1040,128]{1,0:T(8,128)(2,1)S(1)} %send_query.1), channel_id=1, source_target_pairs={{0,1},{1,0},{2,3},{3,2},{4,5},{5,4},{6,7},{7,6},{8,9},{9,8},{10,11... | collective-permute-start | bytes 798728 | tf_op jit(solution)/shard_map/ppermute | solution.py:37
  44.4 1.1 %own_terms.1 = (f32[1024,128]{1,0:T(8,128)S(1)}, f32[1024,128]{1,0:T(8,128)S(1)}, f32[1,32]{1,0:T(1,128)S(1)}) custom-call(f32[4,1024]{1,0:T(4,128)S(1)} %get-tuple-element.45.weight, bf16[128,1024]{1,0:T(8,128)(2,1)S(1)} %get-tuple-element.40.query_t, bf16[1024,1024]{1,0:T(8,128)(2,1)S(1)} %get-tuple-element.46.powers_a, ...), custom_call_target="tpu_custom_call" | custom-call | flops 1000 | bytes 2097152 | tf_op jit(solution)/shard_map/own_terms/pallas_call | solution.py:41
  45.6 0.4 collective-permute-done.4.query_in
  45.9 0.1 collective-permute-done.5.last_in
  46.0 0.0 collective-permute-done.6.far_in
  46.0 1.0 %last_sums.1 = (f32[1024,128]{1,0:T(8,128)}, f32[32]{0:T(128)}, f32[1024,128]{1,0:T(8,128)}) custom-call(f32[1024,128]{1,0:T(8,128)S(1)} %get-tuple-element.48.query_own, s16[1040,128]{1,0:T(8,128)(2,1)S(1)} %collective-permute-done.4.query_in, f32[1,32]{1,0:T(1,128)S(1)} %get-tuple-element.51.loss_row, f32[1024,128]{1,0:T(8,128)S(1)} %get-tuple-element.52.page_own, ...), custom_call_target="tpu_custom_call" | custom-call | flops 1000 | bytes 1000 | tf_op jit(solution)/shard_map/last_sums/pallas_call | solution.py:265
Async XLA Ops:
  0.6 22.8 %collective-permute-start.2 = (bf16[1024,128]{1,0:T(8,128)(2,1)}, bf16[1024,128]{1,0:T(8,128)(2,1)S(1)}, u32[]{:S(2)}, u32[]{:S(2)}) collective-permute-start(bf16[1024,128]{1,0:T(8,128)(2,1)} %bitcast.9), channel_id=1, source_target_pairs={{0,2},{1,3},{2,4},{3,5},{4,6},{5,7},{6,8},{7,9},{8,10},{9,11},{10,... | collective-permute-start | bytes 786440 | tf_op jit(solution)/shard_map/ppermute | solution.py:27
  4.7 20.1 %collective-permute-start.1 = (bf16[1024,128]{1,0:T(8,128)(2,1)}, bf16[1024,128]{1,0:T(8,128)(2,1)S(1)}, u32[]{:S(2)}, u32[]{:S(2)}) collective-permute-start(bf16[1024,128]{1,0:T(8,128)(2,1)} %bitcast.7), channel_id=1, source_target_pairs={{0,1},{1,0},{2,3},{3,2},{4,5},{5,4},{6,7},{7,6},{8,9},{9,8},{10,11... | collective-permute-start | bytes 786440 | tf_op jit(solution)/shard_map/ppermute | solution.py:37
  11.4 16.1 %collective-permute-start = (bf16[1024,128]{1,0:T(8,128)(2,1)}, bf16[1024,128]{1,0:T(8,128)(2,1)S(1)}, u32[]{:S(2)}, u32[]{:S(2)}) collective-permute-start(bf16[1024,128]{1,0:T(8,128)(2,1)} %bitcast.10), channel_id=1, source_target_pairs={{0,0},{1,5},{2,2},{3,7},{4,4},{5,9},{6,6},{7,11},{8,8},{9,13},{10,... | collective-permute-start | bytes 786440 | tf_op jit(solution)/shard_map/ppermute | solution.py:33
  29.1 4.2 %collective-permute-start.3 = (f32[8,1024]{1,0:T(8,128)S(1)}, f32[8,1024]{1,0:T(8,128)S(1)}, u32[]{:S(2)}, u32[]{:S(2)}) collective-permute-start(f32[8,1024]{1,0:T(8,128)S(1)} %get-tuple-element.35.message), channel_id=1, source_target_pairs={{0,1},{1,0},{2,3},{3,2},{4,5},{5,4},{6,7},{7,6},{8,9},{9,8},{10,11... | collective-permute-start | bytes 98312 | tf_op jit(solution)/shard_map/ppermute | solution.py:37
  34.3 11.7 %collective-permute-start.6 = (s16[1088,128]{1,0:T(8,128)(2,1)S(1)}, s16[1088,128]{1,0:T(8,128)(2,1)S(1)}, u32[]{:S(2)}, u32[]{:S(2)}) collective-permute-start(s16[1088,128]{1,0:T(8,128)(2,1)S(1)} %get-tuple-element.53), channel_id=1, source_target_pairs={{0,510},{1,511},{2,0},{3,1},{4,2},{5,3},{6,4},{7,5},{8,6},{9,7},{1... | collective-permute-start | bytes 835592 | tf_op jit(solution)/shard_map/ppermute | solution.py:27
  37.3 8.8 %collective-permute-start.5 = (s16[1072,128]{1,0:T(8,128)(2,1)S(1)}, s16[1072,128]{1,0:T(8,128)(2,1)S(1)}, u32[]{:S(2)}, u32[]{:S(2)}) collective-permute-start(s16[1072,128]{1,0:T(8,128)(2,1)S(1)} %send_last.1), channel_id=1, source_target_pairs={{0,0},{1,509},{2,2},{3,511},{4,4},{5,1},{6,6},{7,3},{8,8},{9,5},{1... | collective-permute-start | bytes 823304 | tf_op jit(solution)/shard_map/ppermute | solution.py:33
  42.5 3.4 %collective-permute-start.4 = (s16[1040,128]{1,0:T(8,128)(2,1)S(1)}, s16[1040,128]{1,0:T(8,128)(2,1)S(1)}, u32[]{:S(2)}, u32[]{:S(2)}) collective-permute-start(s16[1040,128]{1,0:T(8,128)(2,1)S(1)} %send_query.1), channel_id=1, source_target_pairs={{0,1},{1,0},{2,3},{3,2},{4,5},{5,4},{6,7},{7,6},{8,9},{9,8},{10,11... | collective-permute-start | bytes 798728 | tf_op jit(solution)/shard_map/ppermute | solution.py:37

commit v7 on v6

--- a/solution.py
+++ b/solution.py
@@ -138,8 +138,10 @@
     return jnp.concatenate(parts, axis=1)
 
 
-def mate_body(page, query, smooth_c, powers_ref, total_ref, smooth_ref, stats):
+def mate_body(page, query, smooth_c, powers_ref, total_ref, smooth_ref, mixed_ref, query_t_ref, stats):
     token_powers(page, query, powers_ref, stats, 0)
+    query_t_ref[...] = turned(query[...])
+    mix_pages(page, powers_ref, mixed_ref)
     smooth_ref[0:1, :] = smooth_c[...]
     smooth_ref[1:2, :] = token_rows(stats, 1, total_ref)[0]
 
@@ -154,10 +156,9 @@
     message_ref[5:8, :] = sums[0:3, :]
 
 
-def mix_body(far_page, last_page, mate_query, powers_d, powers_b, mixed_d_ref, mixed_b_ref, mate_query_t_ref):
-    mate_query_t_ref[...] = turned(mate_query[...])
-    mix_pages(far_page, powers_d, mixed_d_ref)
-    mix_pages(last_page, powers_b, mixed_b_ref)
+def last_mix_body(page, powers, total, mixed_ref, total_ref):
+    mix_pages(page, powers, mixed_ref)
+    total_ref[...] = total[...]
 
 
 def loss_of(scores, positive):
@@ -300,8 +301,9 @@
     powers_c, total_c, smooth_c = on_core(
         far_body, [((rows, patches), bf16), ((1, rows), f32), ((1, rows), f32)], (far_page, own_query), unit, "far_unit",
         scratch=[pltpu.VMEM((rows, COLUMNS), f32)])
-    powers_d, total_d, smooth_far = on_core(
-        mate_body, [((rows, patches), bf16), ((1, rows), f32), ((2, rows), f32)],
+    powers_d, total_d, smooth_far, mixed_d, mate_query_t = on_core(
+        mate_body,
+        [((rows, patches), bf16), ((1, rows), f32), ((2, rows), f32), ((rows, width), f32), ((width, rows), bf16)],
         (far_page, mate_query, smooth_c), unit, "mate_unit",
         scratch=[pltpu.VMEM((rows, COLUMNS), f32)])
     powers_b, total_b, message = on_core(
@@ -310,17 +312,16 @@
         (last_page, mate_query, smooth_a, smooth_far, positive), unit, "last_unit",
         scratch=[pltpu.VMEM((rows, COLUMNS), f32)])
     arrived = swapped(message, "dp")
-    mixed_d, mixed_b, mate_query_t = on_core(
-        mix_body, [((rows, width), f32)] * 2 + [((width, rows), bf16)],
-        (far_page, last_page, mate_query, powers_d, powers_b), 2 * unit, "mixes")
+    mixed_b, total_b = on_core(
+        last_mix_body, [((rows, width), f32), ((1, rows), f32)], (last_page, powers_b, total_b), 2 * unit, "last_mix")
     far_out, weight = on_core(
         send_far_body,
-        [((patches + 4 * PAD, width), i16), ((4, rows), f32)],
+        [((patches + 3 * PAD, width), i16), ((4, rows), f32)],
         (message, arrived, total_a, total_c, total_d, total_b, query_t, mate_query_t, powers_c, powers_d),
         2 * unit, "send_far")
     far_in = passed_along(far_out, "dp", -2)
     last_out, = on_core(
-        send_last_body, [((patches + 3 * PAD, width), i16)], (weight, mate_query_t, powers_b), unit, "send_last")
+        send_last_body, [((patches + 2 * PAD, width), i16)], (weight, mate_query_t, powers_b), unit, "send_last")
     last_in = odd_passed_along(last_out, "dp", -4)
     query_out, = on_core(
         send_query_body, [((rows + PAD, width), i16)], (weight, mixed_b, mixed_d), 1000, "send_query")

time: 47.4 us -> 47.3 us (level)
  no operation moved by 1% of the time
where the time goes in v7:
time: 47.3 us; the launch traced here: 47 us
  starting transfers between devices  24.7 us (52%)
  Pallas kernels  12.6 us (27%)
  waiting for transfers between devices  8.94 us (19%)
  between operations  0.74 us (2%)
    ppermute x3, starting transfers between devices, swapped(): lax.ppermute(value, axis, [(source, source ^ 1) for source in range(lax.a...  11.9 us
    pallas_call x9, Pallas kernels, on_core(): pl.pallas_call(body, out_shape=[pltpu.VMEM(shape, dtype) for shape, dtype...  11.6 us
    ppermute x2, waiting for transfers between devices, passed_along(): return lax.ppermute(value, axis, pairs)  7.47 us
    ppermute x2, starting transfers between devices, odd_passed_along(): return lax.ppermute(value, axis, pairs)  6.5 us
    ppermute x2, starting transfers between devices, passed_along(): return lax.ppermute(value, axis, pairs)  6.34 us
    pallas_call x1, Pallas kernels, last_sums(): pl.pallas_call(last_sums_body, out_shape=[jax.ShapeDtypeStruct(shape, jnp...  1.05 us
    ppermute x2, waiting for transfers between devices, odd_passed_along(): return lax.ppermute(value, axis, pairs)  0.98 us
  transfers between devices with their start and end apart: 7, of which 4 were waited for; matrix products, arithmetic and copies ran while one was open for 0% of the time, Pallas kernels for 19%

profile of v7, /device:TPU:1, one launch (start us, length us, event | category | flops | bytes accessed | tf_op | source)
XLA Modules:
  0.0 47.0 jit_solution(9212197671884060935)
XLA Ops:
  0.6 4.0 %collective-permute-start.2 = (bf16[1024,128]{1,0:T(8,128)(2,1)}, bf16[1024,128]{1,0:T(8,128)(2,1)S(1)}, u32[]{:S(2)}, u32[]{:S(2)}) collective-permute-start(bf16[1024,128]{1,0:T(8,128)(2,1)} %bitcast.9), channel_id=1, source_target_pairs={{0,2},{1,3},{2,4},{3,5},{4,6},{5,7},{6,8},{7,9},{8,10},{9,11},{10,... | collective-permute-start | bytes 786440 | tf_op jit(solution)/shard_map/ppermute | solution.py:27
  4.7 6.7 %collective-permute-start.1 = (bf16[1024,128]{1,0:T(8,128)(2,1)}, bf16[1024,128]{1,0:T(8,128)(2,1)S(1)}, u32[]{:S(2)}, u32[]{:S(2)}) collective-permute-start(bf16[1024,128]{1,0:T(8,128)(2,1)} %bitcast.7), channel_id=1, source_target_pairs={{0,1},{1,0},{2,3},{3,2},{4,5},{5,4},{6,7},{7,6},{8,9},{9,8},{10,11... | collective-permute-start | bytes 786440 | tf_op jit(solution)/shard_map/ppermute | solution.py:37
  11.4 1.9 %collective-permute-start = (bf16[1024,128]{1,0:T(8,128)(2,1)}, bf16[1024,128]{1,0:T(8,128)(2,1)S(1)}, u32[]{:S(2)}, u32[]{:S(2)}) collective-permute-start(bf16[1024,128]{1,0:T(8,128)(2,1)} %bitcast.10), channel_id=1, source_target_pairs={{0,0},{1,5},{2,2},{3,7},{4,4},{5,9},{6,6},{7,11},{8,8},{9,13},{10,... | collective-permute-start | bytes 786440 | tf_op jit(solution)/shard_map/ppermute | solution.py:33
  13.3 2.7 %own_unit.1 = (bf16[1024,1024]{1,0:T(8,128)(2,1)S(1)}, f32[1024,128]{1,0:T(8,128)S(1)}, f32[1,1024]{1,0:T(1,128)S(1)}, f32[1,1024]{1,0:T(1,128)S(1)}, bf16[128,1...) custom-call(bf16[1024,128]{1,0:T(8,128)(2,1)} %bitcast.11, bf16[1024,128]{1,0:T(8,128)(2,1)} %bitcast.8, ...), custom_call_target="tpu_custom_call" | custom-call | flops 536870912 | bytes 2097152 | tf_op jit(solution)/shard_map/own_unit/pallas_call | solution.py:41
  16.0 7.5 %collective-permute-done.2.page.far_page = bf16[1024,128]{1,0:T(8,128)(2,1)S(1)} collective-permute-done((bf16[1024,128]{1,0:T(8,128)(2,1)}, bf16[1024,128]{1,0:T(8,128)(2,1)S(1)}, u32[]{:S(2)}, u32[]{:S(2)}) %collective-permute-start.2) | collective-permute-done | bytes 262176 | tf_op jit(solution)/shard_map/ppermute | solution.py:27
  23.5 1.3 %far_unit.1 = (bf16[1024,1024]{1,0:T(8,128)(2,1)S(1)}, f32[1,1024]{1,0:T(1,128)S(1)}, f32[1,1024]{1,0:T(1,128)S(1)}) custom-call(bf16[1024,128]{1,0:T(8,128)(2,1)S(1)} %collective-permute-done.2.page.far_page, bf16[1024,128]{1,0:T(8,128)(2,1)S(1)} %get-tuple-element.32.query), custom_call_target="tpu_custom_call" | custom-call | flops 268435456 | bytes 2097152 | tf_op jit(solution)/shard_map/far_unit/pallas_call | solution.py:41
  24.8 0.0 collective-permute-done.1.query.mate_query
  24.8 1.7 %mate_unit.1 = (bf16[1024,1024]{1,0:T(8,128)(2,1)S(1)}, f32[1,1024]{1,0:T(1,128)S(1)}, f32[2,1024]{1,0:T(2,128)S(1)}, f32[1024,128]{1,0:T(8,128)S(1)}, bf16[128,1024]{1,0:T(8,128)(2,1)S(1)}) custom-call(bf16[1024,128]{1,0:T(8,128)(2,1)S(1)} %collective-permute-done.2.page.far_page, bf16[1024,128]{1,0:T(8,128)(2,1)S(1)} %collective-permute-done.1.query.mate_query, ...), custom_call_target="tpu_custom_call" | custom-call | flops 268435456 | bytes 2097152 | tf_op jit(solution)/shard_map/mate_unit/pallas_call | solution.py:41
  26.4 1.0 %collective-permute-done.page = bf16[1024,128]{1,0:T(8,128)(2,1)S(1)} collective-permute-done((bf16[1024,128]{1,0:T(8,128)(2,1)}, bf16[1024,128]{1,0:T(8,128)(2,1)S(1)}, u32[]{:S(2)}, u32[]{:S(2)}) %collective-permute-start) | collective-permute-done | bytes 262176 | tf_op jit(solution)/shard_map/ppermute | solution.py:33
  27.4 1.8 %last_unit.1 = (bf16[1024,1024]{1,0:T(8,128)(2,1)S(1)}, f32[1,1024]{1,0:T(1,128)S(1)}, f32[8,1024]{1,0:T(8,128)S(1)}) custom-call(bf16[1024,128]{1,0:T(8,128)(2,1)S(1)} %collective-permute-done.page, bf16[1024,128]{1,0:T(8,128)(2,1)S(1)} %collective-permute-done.1.query.mate_query, f32[1,1024]{1,0:T(1,128)S(1)} %get-tuple-element.31.smooth_a, ...), custom_call_target="tpu_custom_call" | custom-call | flops 268435456 | bytes 2097152 | tf_op jit(solution)/shard_map/last_unit/pallas_call | solution.py:41
  29.2 3.3 %collective-permute-start.3 = (f32[8,1024]{1,0:T(8,128)S(1)}, f32[8,1024]{1,0:T(8,128)S(1)}, u32[]{:S(2)}, u32[]{:S(2)}) collective-permute-start(f32[8,1024]{1,0:T(8,128)S(1)} %get-tuple-element.36.message), channel_id=1, source_target_pairs={{0,1},{1,0},{2,3},{3,2},{4,5},{5,4},{6,7},{7,6},{8,9},{9,8},{10,11... | collective-permute-start | bytes 98312 | tf_op jit(solution)/shard_map/ppermute | solution.py:37
  32.4 0.7 %last_mix.1 = (f32[1024,128]{1,0:T(8,128)S(1)}, f32[1,1024]{1,0:T(1,128)S(1)}) custom-call(bf16[1024,128]{1,0:T(8,128)(2,1)S(1)} %collective-permute-done.page, bf16[1024,1024]{1,0:T(8,128)(2,1)S(1)} %get-tuple-element.40.powers.powers_b, f32[1,1024]{1,0:T(1,128)S(1)} %get-tuple-element.41.total), custom_call_target="tpu_custom_call" | custom-call | flops 536870912 | bytes 2097152 | tf_op jit(solution)/shard_map/last_mix/pallas_call | solution.py:41
  33.1 0.1 collective-permute-done.3.arrived
  33.3 1.0 %send_far.1 = (s16[1072,128]{1,0:T(8,128)(2,1)S(1)}, f32[4,1024]{1,0:T(4,128)S(1)}) custom-call(f32[8,1024]{1,0:T(8,128)S(1)} %get-tuple-element.36.message, f32[8,1024]{1,0:T(8,128)S(1)} %collective-permute-done.3.arrived, f32[1,1024]{1,0:T(1,128)S(1)} %get-tuple-element.37.total_a, f32[1,1024]{1,0:T(1,128)S(1)} %get-tuple-element.38.total_c, ...), custom_call_target="tpu_custom_call" | custom-call | flops 536870912 | bytes 2097152 | tf_op jit(solution)/shard_map/send_far/pallas_call | solution.py:41
  34.3 2.3 %collective-permute-start.6 = (s16[1072,128]{1,0:T(8,128)(2,1)S(1)}, s16[1072,128]{1,0:T(8,128)(2,1)S(1)}, u32[]{:S(2)}, u32[]{:S(2)}) collective-permute-start(s16[1072,128]{1,0:T(8,128)(2,1)S(1)} %get-tuple-element.55), channel_id=1, source_target_pairs={{0,510},{1,511},{2,0},{3,1},{4,2},{5,3},{6,4},{7,5},{8,6},{9,7},{1... | collective-permute-start | bytes 823304 | tf_op jit(solution)/shard_map/ppermute | solution.py:27
  36.6 0.7 %send_last.1 = s16[1056,128]{1,0:T(8,128)(2,1)S(1)} custom-call(f32[4,1024]{1,0:T(4,128)S(1)} %get-tuple-element.47.weight, bf16[128,1024]{1,0:T(8,128)(2,1)S(1)} %get-tuple-element.44.mate_query_t, bf16[1024,1024]{1,0:T(8,128)(2,1)S(1)} %get-tuple-element.40.powers.powers_b), custom_call_target="tpu_custom_call" | custom-call | flops 268435456 | bytes 2097152 | tf_op jit(solution)/shard_map/send_last/pallas_call | solution.py:41
  37.2 4.6 %collective-permute-start.5 = (s16[1056,128]{1,0:T(8,128)(2,1)S(1)}, s16[1056,128]{1,0:T(8,128)(2,1)S(1)}, u32[]{:S(2)}, u32[]{:S(2)}) collective-permute-start(s16[1056,128]{1,0:T(8,128)(2,1)S(1)} %send_last.1), channel_id=1, source_target_pairs={{0,0},{1,509},{2,2},{3,511},{4,4},{5,1},{6,6},{7,3},{8,8},{9,5},{1... | collective-permute-start | bytes 811016 | tf_op jit(solution)/shard_map/ppermute | solution.py:33
  41.8 0.7 %send_query.1 = s16[1040,128]{1,0:T(8,128)(2,1)S(1)} custom-call(f32[4,1024]{1,0:T(4,128)S(1)} %get-tuple-element.47.weight, f32[1024,128]{1,0:T(8,128)S(1)} %get-tuple-element.51.mixed_b, f32[1024,128]{1,0:T(8,128)S(1)} %get-tuple-element.52.mixed_d), custom_call_target="tpu_custom_call" | custom-call | flops 1000 | bytes 2097152 | tf_op jit(solution)/shard_map/send_query/pallas_call | solution.py:41
  42.5 1.9 %collective-permute-start.4 = (s16[1040,128]{1,0:T(8,128)(2,1)S(1)}, s16[1040,128]{1,0:T(8,128)(2,1)S(1)}, u32[]{:S(2)}, u32[]{:S(2)}) collective-permute-start(s16[1040,128]{1,0:T(8,128)(2,1)S(1)} %send_query.1), channel_id=1, source_target_pairs={{0,1},{1,0},{2,3},{3,2},{4,5},{5,4},{6,7},{7,6},{8,9},{9,8},{10,11... | collective-permute-start | bytes 798728 | tf_op jit(solution)/shard_map/ppermute | solution.py:37
  44.4 1.1 %own_terms.1 = (f32[1024,128]{1,0:T(8,128)S(1)}, f32[1024,128]{1,0:T(8,128)S(1)}, f32[1,32]{1,0:T(1,128)S(1)}) custom-call(f32[4,1024]{1,0:T(4,128)S(1)} %get-tuple-element.47.weight, bf16[128,1024]{1,0:T(8,128)(2,1)S(1)} %get-tuple-element.43.query_t, bf16[1024,1024]{1,0:T(8,128)(2,1)S(1)} %get-tuple-element.48.powers_a, ...), custom_call_target="tpu_custom_call" | custom-call | flops 1000 | bytes 2097152 | tf_op jit(solution)/shard_map/own_terms/pallas_call | solution.py:41
  45.6 0.4 collective-permute-done.4.query_in
  45.9 0.0 collective-permute-done.5.last_in
  45.9 0.0 collective-permute-done.6.far_in
  45.9 1.0 %last_sums.1 = (f32[1024,128]{1,0:T(8,128)}, f32[32]{0:T(128)}, f32[1024,128]{1,0:T(8,128)}) custom-call(f32[1024,128]{1,0:T(8,128)S(1)} %get-tuple-element.50.query_own, s16[1040,128]{1,0:T(8,128)(2,1)S(1)} %collective-permute-done.4.query_in, f32[1,32]{1,0:T(1,128)S(1)} %get-tuple-element.53.loss_row, f32[1024,128]{1,0:T(8,128)S(1)} %get-tuple-element.54.page_own, ...), custom_call_target="tpu_custom_call" | custom-call | flops 1000 | bytes 1000 | tf_op jit(solution)/shard_map/last_sums/pallas_call | solution.py:266
Async XLA Ops:
  0.6 22.8 %collective-permute-start.2 = (bf16[1024,128]{1,0:T(8,128)(2,1)}, bf16[1024,128]{1,0:T(8,128)(2,1)S(1)}, u32[]{:S(2)}, u32[]{:S(2)}) collective-permute-start(bf16[1024,128]{1,0:T(8,128)(2,1)} %bitcast.9), channel_id=1, source_target_pairs={{0,2},{1,3},{2,4},{3,5},{4,6},{5,7},{6,8},{7,9},{8,10},{9,11},{10,... | collective-permute-start | bytes 786440 | tf_op jit(solution)/shard_map/ppermute | solution.py:27
  4.7 20.1 %collective-permute-start.1 = (bf16[1024,128]{1,0:T(8,128)(2,1)}, bf16[1024,128]{1,0:T(8,128)(2,1)S(1)}, u32[]{:S(2)}, u32[]{:S(2)}) collective-permute-start(bf16[1024,128]{1,0:T(8,128)(2,1)} %bitcast.7), channel_id=1, source_target_pairs={{0,1},{1,0},{2,3},{3,2},{4,5},{5,4},{6,7},{7,6},{8,9},{9,8},{10,11... | collective-permute-start | bytes 786440 | tf_op jit(solution)/shard_map/ppermute | solution.py:37
  11.4 16.1 %collective-permute-start = (bf16[1024,128]{1,0:T(8,128)(2,1)}, bf16[1024,128]{1,0:T(8,128)(2,1)S(1)}, u32[]{:S(2)}, u32[]{:S(2)}) collective-permute-start(bf16[1024,128]{1,0:T(8,128)(2,1)} %bitcast.10), channel_id=1, source_target_pairs={{0,0},{1,5},{2,2},{3,7},{4,4},{5,9},{6,6},{7,11},{8,8},{9,13},{10,... | collective-permute-start | bytes 786440 | tf_op jit(solution)/shard_map/ppermute | solution.py:33
  29.2 4.1 %collective-permute-start.3 = (f32[8,1024]{1,0:T(8,128)S(1)}, f32[8,1024]{1,0:T(8,128)S(1)}, u32[]{:S(2)}, u32[]{:S(2)}) collective-permute-start(f32[8,1024]{1,0:T(8,128)S(1)} %get-tuple-element.36.message), channel_id=1, source_target_pairs={{0,1},{1,0},{2,3},{3,2},{4,5},{5,4},{6,7},{7,6},{8,9},{9,8},{10,11... | collective-permute-start | bytes 98312 | tf_op jit(solution)/shard_map/ppermute | solution.py:37
  34.3 11.7 %collective-permute-start.6 = (s16[1072,128]{1,0:T(8,128)(2,1)S(1)}, s16[1072,128]{1,0:T(8,128)(2,1)S(1)}, u32[]{:S(2)}, u32[]{:S(2)}) collective-permute-start(s16[1072,128]{1,0:T(8,128)(2,1)S(1)} %get-tuple-element.55), channel_id=1, source_target_pairs={{0,510},{1,511},{2,0},{3,1},{4,2},{5,3},{6,4},{7,5},{8,6},{9,7},{1... | collective-permute-start | bytes 823304 | tf_op jit(solution)/shard_map/ppermute | solution.py:27
  37.2 8.7 %collective-permute-start.5 = (s16[1056,128]{1,0:T(8,128)(2,1)S(1)}, s16[1056,128]{1,0:T(8,128)(2,1)S(1)}, u32[]{:S(2)}, u32[]{:S(2)}) collective-permute-start(s16[1056,128]{1,0:T(8,128)(2,1)S(1)} %send_last.1), channel_id=1, source_target_pairs={{0,0},{1,509},{2,2},{3,511},{4,4},{5,1},{6,6},{7,3},{8,8},{9,5},{1... | collective-permute-start | bytes 811016 | tf_op jit(solution)/shard_map/ppermute | solution.py:33
  42.5 3.4 %collective-permute-start.4 = (s16[1040,128]{1,0:T(8,128)(2,1)S(1)}, s16[1040,128]{1,0:T(8,128)(2,1)S(1)}, u32[]{:S(2)}, u32[]{:S(2)}) collective-permute-start(s16[1040,128]{1,0:T(8,128)(2,1)S(1)} %send_query.1), channel_id=1, source_target_pairs={{0,1},{1,0},{2,3},{3,2},{4,5},{5,4},{6,7},{7,6},{8,9},{9,8},{10,11... | collective-permute-start | bytes 798728 | tf_op jit(solution)/shard_map/ppermute | solution.py:37
